TPU v7x, 256 devices: a whole 4x4x8 slice. The times are simulated.
256 devices in a mesh: blk: 16 (over z, y_lo), rep: 16 (over y_hi, x, core).
Axes of the slice: x: 4, y: 4 (y_hi: 2, y_lo: 2; y = y_hi * 2 + y_lo), z: 8, core: 2. Of those that a mesh axis runs over, the one named last changes fastest.
Arguments:
- image_feats: bfloat16 [16, 2048, 1152], P('rep', 'blk'), may hold values from -7 to 7
- text_feats: bfloat16 [16, 2048, 1152], P('rep', 'blk'), may hold values from -7 to 7
- image_head: bfloat16 [1152, 1152], replicated, may hold values from -0.1875 to 0.1875
- text_head: bfloat16 [1152, 1152], replicated, may hold values from -0.1875 to 0.1875
- log_scale: float32 [1], replicated, may hold values from 1.4 to 2.8
- bias: float32 [1], replicated, may hold values from -4 to -2
Outputs:
- grad_image_feats: bfloat16 [16, 2048, 1152], P('rep', 'blk')
- grad_text_feats: bfloat16 [16, 2048, 1152], P('rep', 'blk')
- head_grads: float32 [1152, 2, 1152], P('blk')
All inputs are finite; a program needn't handle non-finite values.
Results may differ from a plain program's by a relative error of at most 0.02.
Values may be sent and summed in bfloat16 or wider, within the bound.
No kernel may reach another device: no remote copies, remote signals or barrier semaphores. Data moves between devices by JAX's collectives and lax.ppermute only.
A program may use at most 128 MiB of HBM per device.

v0:
```python
import jax
import jax.numpy as jnp
from jax import lax
from jax.sharding import PartitionSpec as P

STEPS = 4


EPSILON = 1e-06


def from_behind(array, axis, by):
    devices = lax.axis_size(axis)
    return lax.ppermute(array, axis, [(i, (i + by) % devices) for i in range(devices)])


def project_rows(features, head):
    projected = jnp.dot(features, head, preferred_element_type=jnp.float32)
    row_norm = jnp.sqrt(jnp.sum(projected * projected, axis=1, keepdims=True) + EPSILON)
    return (projected / row_norm, row_norm)


def unit_backward(unit_grad, unit_rows, row_norm):
    radial = jnp.sum(unit_rows * unit_grad, axis=1, keepdims=True)
    return ((unit_grad - unit_rows * radial) / row_norm).astype(jnp.bfloat16)


def contract_rows(left, right):
    return lax.dot_general(
        left, right, (((0,), (0,)), ((), ())), preferred_element_type=jnp.float32
    )


def contract_cols(left, right):
    return lax.dot_general(
        left, right, (((1,), (1,)), ((), ())), preferred_element_type=jnp.float32
    )


def pair_weights(image_emb, visiting, logit_scale, offset, positives):
    logits = logit_scale * contract_cols(image_emb, visiting) + offset
    probs = jax.nn.sigmoid(logits) - positives
    return (logit_scale * probs).astype(jnp.bfloat16)


def advance(visiting):
    return from_behind(visiting, "blk", 1)


def body(image_feats, text_feats, image_head, text_head, log_scale, bias):
    logit_scale = jnp.exp(log_scale[0])
    offset = bias[0]
    image_rows = image_feats[0]
    text_rows = text_feats[0]
    image_unit, image_norm = project_rows(image_rows, image_head)
    text_unit, text_norm = project_rows(text_rows, text_head)
    image_emb = image_unit.astype(jnp.bfloat16)
    text_emb = text_unit.astype(jnp.bfloat16)
    row_total = image_emb.shape[0]
    positives = jnp.eye(row_total, dtype=jnp.float32)
    visiting = text_emb
    image_grad = jnp.zeros(image_unit.shape, jnp.float32)
    carried = jnp.zeros(text_unit.shape, jnp.float32)
    for turn_index in range(STEPS):
        weights = pair_weights(
            image_emb, visiting, logit_scale, offset, positives if turn_index == 0 else 0.0
        )
        image_grad = image_grad + jnp.dot(weights, visiting, preferred_element_type=jnp.float32)
        carried = carried + contract_rows(weights, image_emb)
        if turn_index + 1 < STEPS:
            visiting = advance(visiting)
            carried = from_behind(carried, "blk", 1)
    text_grad = from_behind(carried.astype(jnp.bfloat16), "blk", 1 - STEPS).astype(carried.dtype)
    image_dpre = unit_backward(image_grad, image_unit, image_norm)
    text_dpre = unit_backward(text_grad, text_unit, text_norm)
    image_out = contract_cols(image_dpre, image_head).astype(jnp.bfloat16)
    text_out = contract_cols(text_dpre, text_head).astype(jnp.bfloat16)
    partial_heads = lax.psum_scatter(
        jnp.stack(
            [contract_rows(image_rows, image_dpre), contract_rows(text_rows, text_dpre)], axis=1
        ).astype(jnp.bfloat16),
        "blk",
        scatter_dimension=0,
        tiled=True,
    )
    head_grads = lax.psum(partial_heads, "rep").astype(jnp.float32)
    return (image_out[None], text_out[None], head_grads)


def solution(mesh):
    placed = (P("rep", "blk", None), P("rep", "blk", None), P(), P(), P(), P())
    return jax.shard_map(
        body,
        mesh=mesh,
        in_specs=placed,
        out_specs=(P("rep", "blk", None), P("rep", "blk", None), P("blk", None, None)),
        check_vma=False,
    )
```

profile of v0, /device:TPU:1, one launch (start us, length us, event | category | flops | bytes accessed | tf_op | source)
XLA Modules:
  0.0 513.4 jit_solution(4145799648984553721)
XLA Ops:
  7.2 1.7 copy-done
  8.9 1.8 multiply_reduce_fusion.2
  10.8 0.7 multiply_reduce_fusion.1
  13.0 0.3 fusion.29
  13.3 0.3 fusion.47
  13.6 2.2 collective-permute-start.3
  15.8 1.5 collective-permute-start
  17.5 22.9 %collective-permute-done = bf16[128,1152]{1,0:T(8,128)(2,1)S(1)} collective-permute-done((bf16[128,1152]{1,0:T(8,128)(2,1)S(1)}, bf16[128,1152]{1,0:T(8,128)(2,1)S(1)}, u32[]{:S(2)}, u32[]{:S(2)}) %collective-permute-start) | collective-permute-done | bytes 294944 | tf_op jit(solution)/shard_map/ppermute | solution.py:14
  40.5 0.3 fusion.30
  40.8 0.3 convolution_add_fusion
  41.4 8.5 %collective-permute-done.1 = bf16[128,1152]{1,0:T(8,128)(2,1)S(1)} collective-permute-done((bf16[128,1152]{1,0:T(8,128)(2,1)S(1)}, bf16[128,1152]{1,0:T(8,128)(2,1)S(1)}, u32[]{:S(2)}, u32[]{:S(2)}) %collective-permute-start.1) | collective-permute-done | bytes 294944 | tf_op jit(solution)/shard_map/ppermute | solution.py:14
  49.9 0.3 fusion.31
  50.1 0.3 fusion.48
  50.4 12.1 %collective-permute-done.4 = f32[128,1152]{1,0:T(8,128)S(1)} collective-permute-done((f32[128,1152]{1,0:T(8,128)S(1)}, f32[128,1152]{1,0:T(8,128)S(1)}, u32[]{:S(2)}, u32[]{:S(2)}) %collective-permute-start.4) | collective-permute-done | bytes 589856 | tf_op jit(solution)/shard_map/ppermute | solution.py:14
  62.9 5.9 %collective-permute-done.2 = bf16[128,1152]{1,0:T(8,128)(2,1)S(1)} collective-permute-done((bf16[128,1152]{1,0:T(8,128)(2,1)S(1)}, bf16[128,1152]{1,0:T(8,128)(2,1)S(1)}, u32[]{:S(2)}, u32[]{:S(2)}) %collective-permute-start.2) | collective-permute-done | bytes 294944 | tf_op jit(solution)/shard_map/ppermute | solution.py:14
  68.8 0.3 fusion.32
  69.4 12.1 %collective-permute-done.5 = f32[128,1152]{1,0:T(8,128)S(1)} collective-permute-done((f32[128,1152]{1,0:T(8,128)S(1)}, f32[128,1152]{1,0:T(8,128)S(1)}, u32[]{:S(2)}, u32[]{:S(2)}) %collective-permute-start.5) | collective-permute-done | bytes 589856 | tf_op jit(solution)/shard_map/ppermute | solution.py:14
  81.6 0.3 multiply_reduce_fusion
  82.0 1.0 fusion
  83.0 9.4 %collective-permute-done.6 = bf16[128,1152]{1,0:T(8,128)(2,1)S(1)} collective-permute-done((bf16[128,1152]{1,0:T(8,128)(2,1)S(1)}, bf16[128,1152]{1,0:T(8,128)(2,1)S(1)}, u32[]{:S(2)}, u32[]{:S(2)}) %collective-permute-start.6) | collective-permute-done | bytes 294944 | tf_op jit(solution)/shard_map/ppermute | solution.py:14
  92.7 0.5 copy-done.6
  93.2 1.0 fusion.1
  94.2 2.9 pad_maximum_fusion
  97.0 16.6 %copy.10 = bf16[1152,2,1152]{2,1,0:T(2,128)(2,1)} copy(bf16[1152,2,1152]{0,2,1:T(8,128)(2,1)} %pad_maximum_fusion) | data formatting | bytes 10616832 | tf_op jit(solution)/shard_map/stack | solution.py:79
  113.7 0.6 copy-done.8
  114.3 0.6 dynamic-slice
  115.6 2.9 fusion.2
  118.5 243.1 %all-reduce.6.cloned.1.call-done = bf16[1152,2,1152]{2,1,0:T(2,128)(2,1)} async-done(((bf16[1152,2,1152]{2,1,0:T(2,128)(2,1)}), bf16[1152,2,1152]{2,1,0:T(2,128)(2,1)}) %all-reduce.6.cloned.1.call-update) | async-done | bytes 5308432
  361.6 1.9 constant_dynamic-slice_fusion
  363.6 3.4 fusion.3
  367.0 137.6 %all-reduce.4.cloned.1.call-done = bf16[72,2,1152]{2,1,0:T(2,128)(2,1)} async-done(((bf16[72,2,1152]{2,1,0:T(2,128)(2,1)}), bf16[72,2,1152]{2,1,0:T(2,128)(2,1)}) %all-reduce.4.cloned.1.call-update) | async-done | bytes 331792 | tf_op jit(solution)/shard_map/psum | solution.py:86
  504.6 2.0 convert_element_type.56
  (38 shorter events, 1.9 us)
Async XLA Ops:
  7.2 1.8 copy-start
  7.2 3.6 copy-start.4
  7.2 354.4 %all-reduce.6.cloned.1.call-start = ((), (), s32[]{:S(2)}) async-start(), calls=%async_computation.1 | async-start | bytes 10616832
  8.9 1.8 copy-start.1
  10.7 71.3 %copy-start.2 = (f32[128,1152]{1,0:T(8,128)}, f32[128,1152]{1,0:T(8,128)S(1)}, u32[]{:S(2)}) copy-start(f32[128,1152]{1,0:T(8,128)S(1)} %get-tuple-element.7) | copy-start | bytes 1769476
  13.6 27.2 %collective-permute-start.3 = (f32[128,1152]{1,0:T(8,128)S(1)}, f32[128,1152]{1,0:T(8,128)S(1)}, u32[]{:S(2)}, u32[]{:S(2)}) collective-permute-start(f32[128,1152]{1,0:T(8,128)S(1)} %fusion.47), channel_id=1, source_target_pairs={{0,16},{16,32},{32,48},{48,64},{64,80},{80,96},{96,112},{112,128},... | collective-permute-start | bytes 1769480 | tf_op jit(solution)/shard_map/ppermute | solution.py:14
  15.8 24.7 %collective-permute-start = (bf16[128,1152]{1,0:T(8,128)(2,1)S(1)}, bf16[128,1152]{1,0:T(8,128)(2,1)S(1)}, u32[]{:S(2)}, u32[]{:S(2)}) collective-permute-start(bf16[128,1152]{1,0:T(8,128)(2,1)S(1)} %fusion.43), channel_id=1, source_target_pairs={{0,16},{16,32},{32,48},{48,64},{64,80},{80,96},{96,112},{112,128},... | collective-permute-start | bytes 884744 | tf_op jit(solution)/shard_map/ppermute | solution.py:14
  40.5 9.4 %collective-permute-start.1 = (bf16[128,1152]{1,0:T(8,128)(2,1)S(1)}, bf16[128,1152]{1,0:T(8,128)(2,1)S(1)}, u32[]{:S(2)}, u32[]{:S(2)}) collective-permute-start(bf16[128,1152]{1,0:T(8,128)(2,1)S(1)} %collective-permute-done), channel_id=1, source_target_pairs={{0,16},{16,32},{32,48},{48,64},{64,80},{80,96},{96,112},{112,128},... | collective-permute-start | bytes 884744 | tf_op jit(solution)/shard_map/ppermute | solution.py:14
  41.0 21.5 %collective-permute-start.4 = (f32[128,1152]{1,0:T(8,128)S(1)}, f32[128,1152]{1,0:T(8,128)S(1)}, u32[]{:S(2)}, u32[]{:S(2)}) collective-permute-start(f32[128,1152]{1,0:T(8,128)S(1)} %convolution_add_fusion), channel_id=1, source_target_pairs={{0,16},{16,32},{32,48},{48,64},{64,80},{80,96},{96,112},{112,128},... | collective-permute-start | bytes 1769480 | tf_op jit(solution)/shard_map/ppermute | solution.py:14
  49.9 19.0 %collective-permute-start.2 = (bf16[128,1152]{1,0:T(8,128)(2,1)S(1)}, bf16[128,1152]{1,0:T(8,128)(2,1)S(1)}, u32[]{:S(2)}, u32[]{:S(2)}) collective-permute-start(bf16[128,1152]{1,0:T(8,128)(2,1)S(1)} %collective-permute-done.1), channel_id=1, source_target_pairs={{0,16},{16,32},{32,48},{48,64},{64,80},{80,96},{96,112},{112,128},... | collective-permute-start | bytes 884744 | tf_op jit(solution)/shard_map/ppermute | solution.py:14
  62.6 18.9 %collective-permute-start.5 = (f32[128,1152]{1,0:T(8,128)S(1)}, f32[128,1152]{1,0:T(8,128)S(1)}, u32[]{:S(2)}, u32[]{:S(2)}) collective-permute-start(f32[128,1152]{1,0:T(8,128)S(1)} %add.83), channel_id=1, source_target_pairs={{0,16},{16,32},{32,48},{48,64},{64,80},{80,96},{96,112},{112,128},... | collective-permute-start | bytes 1769480 | tf_op jit(solution)/shard_map/ppermute | solution.py:14
  69.1 12.9 %copy-start.3 = (bf16[1,128,1152]{2,1,0:T(8,128)(2,1)S(1)}, bf16[1,128,1152]{2,1,0:T(8,128)(2,1)}, u32[]{:S(2)}) copy-start(bf16[1,128,1152]{2,1,0:T(8,128)(2,1)} %param.6) | copy-start | bytes 884740
  81.5 10.9 %collective-permute-start.6 = (bf16[128,1152]{1,0:T(8,128)(2,1)S(1)}, bf16[128,1152]{1,0:T(8,128)(2,1)S(1)}, u32[]{:S(2)}, u32[]{:S(2)}) collective-permute-start(bf16[128,1152]{1,0:T(8,128)(2,1)S(1)} %add_convert_fusion), channel_id=1, source_target_pairs={{0,208},{16,224},{32,240},{48,0},{64,16},{80,32},{96,48},{112,64},... | collective-permute-start | bytes 884744 | tf_op jit(solution)/shard_map/ppermute | solution.py:14
  82.0 10.5 %copy-start.9 = (f32[128,1152]{1,0:T(8,128)}, f32[128,1152]{1,0:T(8,128)S(1)}, u32[]{:S(2)}) copy-start(f32[128,1152]{1,0:T(8,128)S(1)} %get-tuple-element.11) | copy-start | bytes 1769476
  82.0 11.2 %copy-start.5 = (bf16[1,128,1152]{2,1,0:T(8,128)(2,1)S(1)}, bf16[1,128,1152]{2,1,0:T(8,128)(2,1)}, u32[]{:S(2)}) copy-start(bf16[1,128,1152]{2,1,0:T(8,128)(2,1)} %param.7) | copy-start | bytes 884740
  92.4 0.7 copy-start.6
  113.6 0.7 copy-start.8
  113.7 390.9 %all-reduce.4.cloned.1.call-start = ((), (), s32[]{:S(2)}) async-start(), calls=%async_computation | async-start | bytes 663552 | tf_op jit(solution)/shard_map/psum | solution.py:86
  115.6 248.0 %copy-start.7 = (bf16[128,1152]{1,0:T(8,128)(2,1)S(1)}, bf16[128,1152]{1,0:T(8,128)(2,1)}, u32[]{:S(2)}) copy-start(bf16[128,1152]{1,0:T(8,128)(2,1)} %copy-done.6) | copy-start | bytes 884740
Sparse Core Ops, SparseCore 0:
  113.8 247.7 all-reduce.5
  364.8 139.6 all-reduce.3
where the time goes:
time: 514 us; the launch traced here: 513 us
  waiting for transfers between devices  452 us (88%)
  local copies, waits for them, and re-layouts  21.9 us (4%)
  between operations  16.3 us (3%)
  matrix products  13.9 us (3%)
  other arithmetic  5.51 us (1%)
    unnamed x3, waiting for transfers between devices  243 us
    psum x1, waiting for transfers between devices, body(): head_grads = lax.psum(partial_heads, 'rep').astype(jnp.float32)  138 us
    ppermute x7, waiting for transfers between devices, from_behind(): lax.ppermute(array, axis, [(i, (i + by) % devices) for i in range(devices)])  71 us
    another operation x1, local copies, waits for them, and re-layouts, body(): jnp.stack([contract_rows(image_rows, image_dpre), contract_rows(text_rows...  16.6 us
  transfers between devices with their start and end apart: 9, of which 8 were waited for; matrix products, arithmetic and copies ran while one was open for 2% of the time, Pallas kernels for 0%

commit v1 on v0

v1 whole, which is shorter than its diff:
```python
import functools

import jax
import jax.numpy as jnp
from jax import lax
from jax.experimental import pallas as pl
from jax.experimental.pallas import tpu as pltpu
from jax.sharding import Mesh
from jax.sharding import PartitionSpec as P

EPSILON = 1e-06
F32 = jnp.float32
BF16 = jnp.bfloat16

BLK = ("z", "ylo")
REP = ("yhi", "x", "core")
NZ, NYLO, NYHI, NX, NCORE = 8, 2, 2, 4, 2
D = 1152
ROWS = 128
LANES = 128
MAIN = 2 * LANES
TAIL_AT = NX * MAIN
SENT = MAIN + LANES
PER_BLK = D // (NZ * NYLO)
TAIL_ROWS = PER_BLK // (NX * NYHI)
PIECE = 88
PIECES = NZ * NYLO * NYHI
MIB = 1024 * 1024


def call(kernel, name, out_shape, args, in_specs=None, scratch=(), mib=24, flops=0, moved=0):
    return pl.pallas_call(
        kernel,
        out_shape=out_shape,
        in_specs=in_specs or [pl.BlockSpec(memory_space=pltpu.VMEM)] * len(args),
        scratch_shapes=list(scratch),
        compiler_params=pltpu.CompilerParams(vmem_limit_bytes=mib * MIB),
        cost_estimate=pl.CostEstimate(flops=flops, bytes_accessed=moved, transcendentals=0),
        name=name,
    )(*args)


def shape(dims, dtype=BF16):
    return jax.ShapeDtypeStruct(dims, dtype)


VMEM_SPEC = pl.BlockSpec(memory_space=pltpu.VMEM)
SMEM_SPEC = pl.BlockSpec(memory_space=pltpu.SMEM)


def nt(left, right):
    return lax.dot_general(left, right, (((1,), (1,)), ((), ())), preferred_element_type=F32)


def nn(left, right):
    return lax.dot_general(left, right, (((1,), (0,)), ((), ())), preferred_element_type=F32)


def pick(flag, if_zero, if_one):
    return jnp.where(flag == 0, if_zero, if_one)


def project_kernel(image, text, image_head, text_head, emb_u, emb_v, unit_u, unit_v, norm_u, norm_v):
    col = lax.axis_index("ylo")

    def project(rows, head):
        pre = nn(rows[...], head[...])
        norm = jnp.sqrt(jnp.sum(pre * pre, axis=1, keepdims=True) + EPSILON)
        return pre / norm, norm

    image_unit, image_norm = project(image, image_head)
    text_unit, text_norm = project(text, text_head)
    u = pick(col, text_unit, image_unit)
    v = pick(col, image_unit, text_unit)
    emb_u[...] = u.astype(BF16)
    emb_v[...] = v.astype(BF16)
    unit_u[...] = u
    unit_v[...] = v
    norm_u[...] = pick(col, text_norm, image_norm)
    norm_v[...] = pick(col, image_norm, text_norm)


def turn_kernel(image, text, turned):
    core = lax.axis_index("core")
    image_t = image[...].astype(F32).T
    text_t = text[...].astype(F32).T
    turned[0] = pick(core, image_t, text_t).astype(BF16)
    turned[1] = pick(core, text_t, image_t).astype(BF16)


def pair_weights(own, other, scalars, same):
    scale = jnp.exp(scalars[0])
    logits = scale * nt(own, other) + scalars[1]
    probs = jax.nn.sigmoid(logits)
    if same:
        row = lax.broadcasted_iota(jnp.int32, probs.shape, 0)
        column = lax.broadcasted_iota(jnp.int32, probs.shape, 1)
        probs = probs - jnp.where(row == column, 1.0, 0.0)
    return (scale * probs).astype(BF16)


def pull(own, other, scalars, same=False):
    return nn(pair_weights(own, other, scalars, same), other)


def early_kernel(scalars, u, v, u1, v1, v0, u2, grad_u, grad_v):
    own_u, own_v = u[...], v[...]
    grad_u[...] = (
        pull(own_u, own_v, scalars, True)
        + pull(own_u, v0[...], scalars)
        + pull(own_u, v1[...], scalars)
    )
    grad_v[...] = (
        pull(own_v, own_u, scalars, True)
        + pull(own_v, u1[...], scalars)
        + pull(own_v, u2[...], scalars)
    )


def late_kernel(
    scalars, u, v, u3, v3, grad_u, grad_v, unit_u, unit_v, norm_u, norm_v,
    image_dpre, text_dpre, sent0, sent1, sent2, sent3, mine_t, other_t,
):
    col = lax.axis_index("ylo")
    core = lax.axis_index("core")
    at = lax.axis_index("x")

    def backward(grad, unit, norm):
        radial = jnp.sum(unit * grad, axis=1, keepdims=True)
        return (grad - unit * radial) / norm

    dpre_u = backward(grad_u[...] + pull(u[...], v3[...], scalars), unit_u[...], norm_u[...])
    dpre_v = backward(grad_v[...] + pull(v[...], u3[...], scalars), unit_v[...], norm_v[...])
    image = pick(col, dpre_v, dpre_u)
    text = pick(col, dpre_u, dpre_v)
    image_dpre[...] = image.astype(BF16)
    text_dpre[...] = text.astype(BF16)
    mine_t[...] = pick(core, image, text).T.astype(BF16)
    other_t[...] = pick(core, text, image).T.astype(BF16)
    for step, sent in enumerate((sent0, sent1, sent2, sent3)):
        to = lax.rem(at + step, NX)
        rows = pl.ds(pl.multiple_of(to * MAIN, MAIN), MAIN)
        for place, turned in enumerate((mine_t, other_t)):
            sent[place, :MAIN, :] = turned[rows, :]
            sent[place, MAIN:, :] = turned[TAIL_AT:, :]


def feats_grad_kernel(image_dpre, text_dpre, image_head, text_head, image_out, text_out):
    image_out[...] = nt(image_dpre[...], image_head[...]).astype(BF16)
    text_out[...] = nt(text_dpre[...], text_head[...]).astype(BF16)


def side_by_side_kernel(*refs):
    parts, out = refs[:-1], refs[-1]
    for place, part in enumerate(parts):
        out[:, place * ROWS:(place + 1) * ROWS] = part[place % 2]


def head_kernel(feats_t, *refs):
    parts, pieces, right, total, tail = refs[:8], refs[8], refs[9], refs[10], refs[11]
    at = lax.axis_index("x")
    for place, part in enumerate(parts):
        right[:, place * ROWS:(place + 1) * ROWS] = part[place % 2]
    total[...] = nt(feats_t[...], right[...])
    tail[...] = total[:, MAIN:]
    pad = jnp.zeros((PIECE - PER_BLK - TAIL_ROWS, LANES), F32)
    for blk in range(NZ * NYLO):
        rows = slice(blk * PER_BLK, (blk + 1) * PER_BLK)
        for half in range(NYHI):
            start = blk * PER_BLK + (NYHI * at + half) * TAIL_ROWS
            piece = jnp.concatenate(
                [
                    total[rows, half * LANES:(half + 1) * LANES],
                    tail[pl.ds(start, TAIL_ROWS), :],
                    pad,
                ],
                axis=0,
            )
            pieces[blk * NYHI + half] = piece.astype(BF16)


def add_kernel(pieces, out):
    total = pieces[0].astype(F32)
    for place in range(1, PIECES):
        total = total + pieces[place].astype(F32)
    out[...] = total.astype(BF16)


def place_kernel(*refs):
    parts, out = refs[:-1], refs[-1]
    core = lax.axis_index("core")
    at = lax.axis_index("x")
    half_at = lax.axis_index("yhi")
    for place, part in enumerate(parts):
        flip, step = divmod(place, NX)
        came_x = lax.rem(at + NX - step, NX)
        came_half = lax.rem(half_at + flip, NYHI)
        index = NYHI * came_x + came_half
        mine = part[0].astype(F32)
        other = part[1].astype(F32)
        both = jnp.stack([pick(core, mine, other), pick(core, other, mine)], axis=1)
        out[:, :, pl.ds(pl.multiple_of(index * LANES, LANES), LANES)] = both[:PER_BLK]
        out[pl.ds(index * TAIL_ROWS, TAIL_ROWS), :, TAIL_AT:] = both[PER_BLK:PER_BLK + TAIL_ROWS]


def z_shift(array, sign):
    pairs = []
    for z in range(NZ):
        for y in range(NYLO):
            step = sign if y == 0 else -sign
            pairs.append((z * NYLO + y, ((z + step) % NZ) * NYLO + y))
    return lax.ppermute(array, BLK, pairs)


def y_swap(array):
    return lax.ppermute(array, "ylo", [(0, 1), (1, 0)])


def core_swap(array):
    return lax.ppermute(array, "core", [(0, 1), (1, 0)])


def x_turn(array, by):
    return lax.ppermute(array, "x", [(i, (i + by) % NX) for i in range(NX)])


def rep_turn(array, flip, by):
    pairs = []
    for half in range(NYHI):
        for at in range(NX):
            pairs.append((half * NX + at, ((half + flip) % NYHI) * NX + (at + by) % NX))
    return lax.ppermute(array, ("yhi", "x"), pairs)


def body(image_feats, text_feats, image_head, text_head, log_scale, bias):
    image = image_feats[0]
    text = text_feats[0]
    scalars = jnp.concatenate([log_scale, bias])
    block = shape((ROWS, D))
    block32 = shape((ROWS, D), F32)
    column = shape((ROWS, 1), F32)

    u, v, unit_u, unit_v, norm_u, norm_v = call(
        project_kernel, "project", [block, block, block32, block32, column, column],
        (image, text, image_head, text_head), flops=4 * ROWS * D * D, moved=7 * MIB,
    )
    v1 = z_shift(v, -1)
    u1 = z_shift(u, 1)
    v0 = y_swap(u)
    turned = call(turn_kernel, "turn", shape((2, D, ROWS)), (image, text), moved=MIB)
    feats = [turned] + [x_turn(turned, by) for by in (1, 3, 2)]
    feats_across = [core_swap(part) for part in feats]
    u2 = y_swap(v1)
    u3 = z_shift(u2, 1)
    v3 = y_swap(u1)

    grad_u, grad_v = call(
        early_kernel, "early", [block32, block32], (scalars, u, v, u1, v1, v0, u2),
        in_specs=[SMEM_SPEC] + [VMEM_SPEC] * 6, flops=24 * ROWS * ROWS * D, moved=3 * MIB,
    )
    both = [part for pair in zip(feats, feats_across) for part in pair]
    feats_t = call(
        side_by_side_kernel, "side_by_side", shape((D, 8 * ROWS)), both,
        moved=5 * MIB,
    )
    sent = shape((2, SENT, ROWS))
    image_dpre, text_dpre, *parts = call(
        late_kernel, "late", [block, block, sent, sent, sent, sent],
        (scalars, u, v, u3, v3, grad_u, grad_v, unit_u, unit_v, norm_u, norm_v),
        in_specs=[SMEM_SPEC] + [VMEM_SPEC] * 10,
        scratch=[pltpu.VMEM((D, ROWS), BF16)] * 2, flops=8 * ROWS * ROWS * D, moved=4 * MIB,
    )
    parts = [parts[0], x_turn(parts[1], 1), x_turn(parts[3], 3), x_turn(parts[2], 2)]
    parts_across = [core_swap(part) for part in parts]
    image_out, text_out = call(
        feats_grad_kernel, "feats_grad", [block, block],
        (image_dpre, text_dpre, image_head, text_head), flops=4 * ROWS * D * D, moved=7 * MIB,
    )
    both = [part for pair in zip(parts, parts_across) for part in pair]
    pieces = call(
        head_kernel, "head", shape((PIECES, PIECE, LANES)), [feats_t] + both,
        scratch=[
            pltpu.VMEM((SENT, 8 * ROWS), BF16),
            pltpu.VMEM((D, SENT), F32),
            pltpu.VMEM((D, LANES), F32),
        ],
        flops=16 * ROWS * D * SENT, moved=6 * MIB,
    )
    pieces = lax.all_to_all(pieces, ("z", "ylo", "yhi"), 0, 0, tiled=True)
    mine = call(add_kernel, "add", shape((PIECE, LANES)), (pieces,), moved=MIB)
    two = jnp.stack([mine, core_swap(mine)])
    places = [rep_turn(two, flip, by) if flip or by else two for flip in range(NYHI) for by in range(NX)]
    head_grads = call(place_kernel, "place", shape((PER_BLK, 2, D), F32), places, moved=MIB)
    return (image_out[None], text_out[None], head_grads)


def solution(mesh):
    split = Mesh(mesh.devices.reshape(NZ, NYLO, NYHI, NX, NCORE), BLK + REP)
    rows = P(REP, BLK, None)
    return jax.shard_map(
        body,
        mesh=split,
        in_specs=(rows, rows, P(), P(), P(), P()),
        out_specs=(rows, rows, P(BLK, None, None)),
        check_vma=False,
    )
```

time: 514 us -> 113 us (0.22)
  waiting for transfers between devices: 452 us -> 24.7 us
  starting transfers between devices: 4.07 us -> 39.7 us
  blocking collectives: 0 us -> 27.7 us
  local copies, waits for them, and re-layouts: 21.9 us -> 5.43 us
  between operations: 16.3 us -> 2.07 us
  matrix products: 13.9 us -> 0 us
  Pallas kernels: 0 us -> 12 us
  other arithmetic: 5.51 us -> 0.08 us
    unnamed x3 -> x0, waiting for transfers between devices: 243 us -> none
    psum x1 -> x0, waiting for transfers between devices: 138 us -> none  [body(): head_grads = lax.psum(partial_heads, 'rep').astype(jnp.float32)]
    ppermute x7 -> x28, waiting for transfers between devices: 71 us -> 24.7 us  [the longest x6 12.9 us: x_turn(): return lax.ppermute(array, 'x', [(i, (i + by) % NX) for i in range(NX)])]
    ppermute x7 -> x28, starting transfers between devices: 3.99 us -> 39.7 us  [the longest x9 13.1 us: core_swap(): return lax.ppermute(array, 'core', [(0, 1), (1, 0)])]
    all_to_all x0 -> x1, blocking collectives: none -> 27.7 us  [body(): pieces = lax.all_to_all(pieces, ('z', 'ylo', 'yhi'), 0, 0, tiled=True)]
    another operation x1 -> x0, local copies, waits for them, and re-layouts: 16.6 us -> none  [body(): jnp.stack([contract_rows(image_rows, image_dpre), contract_rows(text_rows...]
    dot_general x18 -> x0, matrix products: 13.9 us -> none  [the longest x6 7.41 us: contract_cols(): lax.dot_general(left, right, (((1,), (1,)), ((), ())), preferred_element_...]
    pallas_call x0 -> x9, Pallas kernels: none -> 12 us  [call(): pl.pallas_call(kernel, out_shape=out_shape, in_specs=in_specs or [pl.Bloc...]
  transfers between devices with their start and end apart: 9 -> 28, of which waited for: 8 -> 11; matrix products, arithmetic and copies ran while one was open for 2% -> 0% of each run, Pallas kernels for 0% -> 8%
where the time goes in v1:
time: 113 us; the launch traced here: 112 us
  starting transfers between devices  39.7 us (35%)
  blocking collectives  27.7 us (25%)
  waiting for transfers between devices  24.7 us (22%)
  Pallas kernels  12 us (11%)
  local copies, waits for them, and re-layouts  5.43 us (5%)
  between operations  2.07 us (2%)
    all_to_all x1, blocking collectives, body(): pieces = lax.all_to_all(pieces, ('z', 'ylo', 'yhi'), 0, 0, tiled=True)  27.7 us
    ppermute x9, starting transfers between devices, core_swap(): return lax.ppermute(array, 'core', [(0, 1), (1, 0)])  13.1 us
    ppermute x6, waiting for transfers between devices, x_turn(): return lax.ppermute(array, 'x', [(i, (i + by) % NX) for i in range(NX)])  12.9 us
    pallas_call x9, Pallas kernels, call(): pl.pallas_call(kernel, out_shape=out_shape, in_specs=in_specs or [pl.Bloc...  12 us
    ppermute x7, starting transfers between devices, rep_turn(): return lax.ppermute(array, ('yhi', 'x'), pairs)  11 us
    ppermute x6, starting transfers between devices, x_turn(): return lax.ppermute(array, 'x', [(i, (i + by) % NX) for i in range(NX)])  7.58 us
    ppermute x3, starting transfers between devices, z_shift(): return lax.ppermute(array, BLK, pairs)  5.65 us
    ppermute x3, waiting for transfers between devices, z_shift(): return lax.ppermute(array, BLK, pairs)  5.52 us
  transfers between devices with their start and end apart: 28, of which 11 were waited for; matrix products, arithmetic and copies ran while one was open for 0% of the time, Pallas kernels for 8%

profile of v1, /device:TPU:1, one launch (start us, length us, event | category | flops | bytes accessed | tf_op | source)
XLA Modules:
  0.0 111.6 jit_solution(4704339934424325309)
XLA Ops:
  0.6 1.0 copy-done.4
  1.6 1.0 copy-done.5
  2.8 3.7 %collective-permute-start.11 = (bf16[2,1152,128]{2,1,0:T(8,128)(2,1)S(1)}, bf16[2,1152,128]{2,1,0:T(8,128)(2,1)S(1)}, u32[]{:S(2)}, u32[]{:S(2)}) collective-permute-start(bf16[2,1152,128]{2,1,0:T(8,128)(2,1)S(1)} %turn.1.refs_0_), channel_id=1, source_target_pairs={{0,4},{2,6},{4,0},{6,2},{1,5},{3,7},{5,1},{7,3},{8,12},{10,14},{12... | collective-permute-start | bytes 1769480 | tf_op jit(solution)/shard_map/ppermute | solution.py:224
  6.5 1.7 %copy-done = bf16[1152,1152]{1,0:T(8,128)(2,1)S(1)} copy-done((bf16[1152,1152]{1,0:T(8,128)(2,1)S(1)}, bf16[1152,1152]{1,0:T(8,128)(2,1)}, u32[]{:S(2)}) %copy-start) | copy-done | bytes 2654232
  8.2 1.7 %copy-done.2 = bf16[1152,1152]{1,0:T(8,128)(2,1)S(1)} copy-done((bf16[1152,1152]{1,0:T(8,128)(2,1)S(1)}, bf16[1152,1152]{1,0:T(8,128)(2,1)}, u32[]{:S(2)}) %copy-start.2) | copy-done | bytes 2654232
  10.0 1.2 %project.1 = (bf16[128,1152]{1,0:T(8,128)(2,1)S(1)}, bf16[128,1152]{1,0:T(8,128)(2,1)S(1)}, f32[128,1152]{1,0:T(8,128)S(1)}, f32[128,1152]{1,0:T(8,128)S(1)}, f3...) custom-call(bf16[128,1152]{1,0:T(8,128)(2,1)S(1)} %bitcast.7, bf16[128,1152]{1,0:T(8,128)(2,1)S(1)} %bitcast.9, ...), custom_call_target="tpu_custom_call" | custom-call | flops 679477248 | bytes 7340032 | tf_op jit(solution)/shard_map/project/pallas_call | solution.py:32
  11.2 5.6 %collective-permute-start = (bf16[128,1152]{1,0:T(8,128)(2,1)S(1)}, bf16[128,1152]{1,0:T(8,128)(2,1)S(1)}, u32[]{:S(2)}, u32[]{:S(2)}) collective-permute-start(bf16[128,1152]{1,0:T(8,128)(2,1)S(1)} %get-tuple-element.20.v), channel_id=1, source_target_pairs={{0,224},{16,48},{32,0},{48,80},{64,32},{80,112},{96,64},{112,144},... | collective-permute-start | bytes 884744 | tf_op jit(solution)/shard_map/ppermute | solution.py:212
  17.8 4.5 %collective-permute-done.v1 = bf16[128,1152]{1,0:T(8,128)(2,1)S(1)} collective-permute-done((bf16[128,1152]{1,0:T(8,128)(2,1)S(1)}, bf16[128,1152]{1,0:T(8,128)(2,1)S(1)}, u32[]{:S(2)}, u32[]{:S(2)}) %collective-permute-start) | collective-permute-done | bytes 294944 | tf_op jit(solution)/shard_map/ppermute | solution.py:212
  22.2 2.4 %collective-permute-start.1 = (bf16[128,1152]{1,0:T(8,128)(2,1)S(1)}, bf16[128,1152]{1,0:T(8,128)(2,1)S(1)}, u32[]{:S(2)}, u32[]{:S(2)}) collective-permute-start(bf16[128,1152]{1,0:T(8,128)(2,1)S(1)} %collective-permute-done.v1), channel_id=1, source_target_pairs={{0,16},{16,0},{1,17},{17,1},{2,18},{18,2},{3,19},{19,3},{4,20},{20... | collective-permute-start | bytes 884744 | tf_op jit(solution)/shard_map/ppermute | solution.py:216
  24.9 1.0 collective-permute-done.3.u1
  26.0 3.0 %collective-permute-start.6 = (bf16[2,1152,128]{2,1,0:T(8,128)(2,1)S(1)}, bf16[2,1152,128]{2,1,0:T(8,128)(2,1)S(1)}, u32[]{:S(2)}, u32[]{:S(2)}) collective-permute-start(bf16[2,1152,128]{2,1,0:T(8,128)(2,1)S(1)} %turn.1.refs_0_), channel_id=1, source_target_pairs={{0,1},{1,0},{2,3},{3,2},{4,5},{5,4},{6,7},{7,6},{8,9},{9,8},{10,11... | collective-permute-start | bytes 1769480 | tf_op jit(solution)/shard_map/ppermute | solution.py:220
  28.9 1.6 %collective-permute-done.1.u2 = bf16[128,1152]{1,0:T(8,128)(2,1)S(1)} collective-permute-done((bf16[128,1152]{1,0:T(8,128)(2,1)S(1)}, bf16[128,1152]{1,0:T(8,128)(2,1)S(1)}, u32[]{:S(2)}, u32[]{:S(2)}) %collective-permute-start.1) | collective-permute-done | bytes 294944 | tf_op jit(solution)/shard_map/ppermute | solution.py:216
  30.5 1.8 %collective-permute-done.9.refs_4_ = bf16[2,1152,128]{2,1,0:T(8,128)(2,1)S(1)} collective-permute-done((bf16[2,1152,128]{2,1,0:T(8,128)(2,1)S(1)}, bf16[2,1152,128]{2,1,0:T(8,128)(2,1)S(1)}, u32[]{:S(2)}, u32[]{:S(2)}) %collective-permute-start.9) | collective-permute-done | bytes 589856 | tf_op jit(solution)/shard_map/ppermute | solution.py:224
  32.3 2.1 %collective-permute-start.12 = (bf16[2,1152,128]{2,1,0:T(8,128)(2,1)S(1)}, bf16[2,1152,128]{2,1,0:T(8,128)(2,1)S(1)}, u32[]{:S(2)}, u32[]{:S(2)}) collective-permute-start(bf16[2,1152,128]{2,1,0:T(8,128)(2,1)S(1)} %collective-permute-done.11.refs_6_), channel_id=1, source_target_pairs={{0,1},{1,0},{2,3},{3,2},{4,5},{5,4},{6,7},{7,6},{8,9},{9,8},{10,11... | collective-permute-start | bytes 1769480 | tf_op jit(solution)/shard_map/ppermute | solution.py:220
  34.4 2.5 %collective-permute-done.4.v3 = bf16[128,1152]{1,0:T(8,128)(2,1)S(1)} collective-permute-done((bf16[128,1152]{1,0:T(8,128)(2,1)S(1)}, bf16[128,1152]{1,0:T(8,128)(2,1)S(1)}, u32[]{:S(2)}, u32[]{:S(2)}) %collective-permute-start.4) | collective-permute-done | bytes 294944 | tf_op jit(solution)/shard_map/ppermute | solution.py:216
  36.8 2.1 %collective-permute-start.10 = (bf16[2,1152,128]{2,1,0:T(8,128)(2,1)S(1)}, bf16[2,1152,128]{2,1,0:T(8,128)(2,1)S(1)}, u32[]{:S(2)}, u32[]{:S(2)}) collective-permute-start(bf16[2,1152,128]{2,1,0:T(8,128)(2,1)S(1)} %collective-permute-done.9.refs_4_), channel_id=1, source_target_pairs={{0,1},{1,0},{2,3},{3,2},{4,5},{5,4},{6,7},{7,6},{8,9},{9,8},{10,11... | collective-permute-start | bytes 1769480 | tf_op jit(solution)/shard_map/ppermute | solution.py:220
  40.3 2.3 %early.1 = (f32[128,1152]{1,0:T(8,128)S(1)}, f32[128,1152]{1,0:T(8,128)S(1)}) custom-call(f32[2]{0:T(128)S(1)} %pad_maximum_fusion.1.scalars, bf16[128,1152]{1,0:T(8,128)(2,1)S(1)} %get-tuple-element.19.u, bf16[128,1152]{1,0:T(8,128)(2,1)S(1)} %get-tuple-element.20.v, bf16[128,1152]{1,0:T(8,128)(2,1)S(1)} %collective-permute-done.3.u1, ...), custom_call_target="tpu_custom_call" | custom-call | flops 452984832 | bytes 3145728 | tf_op jit(solution)/shard_map/early/pallas_call | solution.py:32
  42.7 2.0 %late.1 = (bf16[128,1152]{1,0:T(8,128)(2,1)S(1)}, bf16[128,1152]{1,0:T(8,128)(2,1)S(1)}, bf16[2,384,128]{2,1,0:T(8,128)(2,1)S(1)}, bf16[2,384,128]{2,1,0:T(8,128...) custom-call(f32[2]{0:T(128)S(1)} %pad_maximum_fusion.1.scalars, ...), custom_call_target="tpu_custom_call" | custom-call | flops 150994944 | bytes 4194304 | tf_op jit(solution)/shard_map/late/pallas_call | solution.py:32
  45.4 2.4 %collective-permute-start.16 = (bf16[2,384,128]{2,1,0:T(8,128)(2,1)S(1)}, bf16[2,384,128]{2,1,0:T(8,128)(2,1)S(1)}, u32[]{:S(2)}, u32[]{:S(2)}) collective-permute-start(bf16[2,384,128]{2,1,0:T(8,128)(2,1)S(1)} %get-tuple-element.33), channel_id=1, source_target_pairs={{0,6},{2,0},{4,2},{6,4},{1,7},{3,1},{5,3},{7,5},{8,14},{10,8},{12,... | collective-permute-start | bytes 589832 | tf_op jit(solution)/shard_map/ppermute | solution.py:224
  47.8 4.8 %collective-permute-done.14.refs_2_ = bf16[2,384,128]{2,1,0:T(8,128)(2,1)S(1)} collective-permute-done((bf16[2,384,128]{2,1,0:T(8,128)(2,1)S(1)}, bf16[2,384,128]{2,1,0:T(8,128)(2,1)S(1)}, u32[]{:S(2)}, u32[]{:S(2)}) %collective-permute-start.14) | collective-permute-done | bytes 196640 | tf_op jit(solution)/shard_map/ppermute | solution.py:224
  53.3 6.4 %collective-permute-done.18.refs_6_ = bf16[2,384,128]{2,1,0:T(8,128)(2,1)S(1)} collective-permute-done((bf16[2,384,128]{2,1,0:T(8,128)(2,1)S(1)}, bf16[2,384,128]{2,1,0:T(8,128)(2,1)S(1)}, u32[]{:S(2)}, u32[]{:S(2)}) %collective-permute-start.18) | collective-permute-done | bytes 196640 | tf_op jit(solution)/shard_map/ppermute | solution.py:224
  59.7 1.7 %collective-permute-start.15 = (bf16[2,384,128]{2,1,0:T(8,128)(2,1)S(1)}, bf16[2,384,128]{2,1,0:T(8,128)(2,1)S(1)}, u32[]{:S(2)}, u32[]{:S(2)}) collective-permute-start(bf16[2,384,128]{2,1,0:T(8,128)(2,1)S(1)} %collective-permute-done.14.refs_2_), channel_id=1, source_target_pairs={{0,1},{1,0},{2,3},{3,2},{4,5},{5,4},{6,7},{7,6},{8,9},{9,8},{10,11... | collective-permute-start | bytes 589832 | tf_op jit(solution)/shard_map/ppermute | solution.py:220
  63.1 1.5 %head.1 = bf16[32,88,128]{2,1,0:T(8,128)(2,1)S(1)} custom-call(bf16[1152,1024]{1,0:T(8,128)(2,1)S(1)} %side_by_side.1.feats_t, bf16[2,384,128]{2,1,0:T(8,128)(2,1)S(1)} %get-tuple-element.31.refs_0_, bf16[2,384,128]{2,1,0:T(8,128)(2,1)S(1)} %collective-permute-done.13.refs_1_, bf16[2,384,128]{2,1,0:T(8,128)(2,1)S(1)} %collective-permute-done.14.refs_2_, ...), custom_call_target="tpu_custom_call" | custom-call | flops 905969664 | bytes 6291456 | tf_op jit(solution)/shard_map/head/pallas_call | solution.py:32
  64.6 27.7 %all_to_all.5.pieces = bf16[32,88,128]{2,1,0:T(8,128)(2,1)S(1)} all-to-all(bf16[32,88,128]{2,1,0:T(8,128)(2,1)S(1)} %head.1), channel_id=1, replica_groups=mesh['z'=8,'ylo'=2,'yhi'=2,'x'=4,'core'=2] {'z','ylo','yhi'}, dimensions={0} | all-to-all | bytes 1441792 | tf_op jit(solution)/shard_map/all_to_all | solution.py:289
  92.5 2.7 %collective-permute-start.20 = (bf16[88,128]{1,0:T(8,128)(2,1)S(1)}, bf16[88,128]{1,0:T(8,128)(2,1)S(1)}, u32[]{:S(2)}, u32[]{:S(2)}) collective-permute-start(bf16[88,128]{1,0:T(8,128)(2,1)S(1)} %add.1), channel_id=1, source_target_pairs={{0,1},{1,0},{2,3},{3,2},{4,5},{5,4},{6,7},{7,6},{8,9},{9,8},{10,11... | collective-permute-start | bytes 67592 | tf_op jit(solution)/shard_map/ppermute | solution.py:220
  96.0 1.7 %collective-permute-start.27 = (bf16[2,88,128]{2,1,0:T(8,128)(2,1)S(1)}, bf16[2,88,128]{2,1,0:T(8,128)(2,1)S(1)}, u32[]{:S(2)}, u32[]{:S(2)}) collective-permute-start(bf16[2,88,128]{2,1,0:T(8,128)(2,1)S(1)} %pad_maximum_fusion.refs_0_), channel_id=1, source_target_pairs={{0,14},{2,8},{4,10},{6,12},{8,6},{10,0},{12,2},{14,4},{1,15},{3,9}... | collective-permute-start | bytes 135176 | tf_op jit(solution)/shard_map/ppermute | solution.py:232
  97.8 1.6 %collective-permute-start.26 = (bf16[2,88,128]{2,1,0:T(8,128)(2,1)S(1)}, bf16[2,88,128]{2,1,0:T(8,128)(2,1)S(1)}, u32[]{:S(2)}, u32[]{:S(2)}) collective-permute-start(bf16[2,88,128]{2,1,0:T(8,128)(2,1)S(1)} %pad_maximum_fusion.refs_0_), channel_id=1, source_target_pairs={{0,12},{2,14},{4,8},{6,10},{8,4},{10,6},{12,0},{14,2},{1,13},{3,15... | collective-permute-start | bytes 135176 | tf_op jit(solution)/shard_map/ppermute | solution.py:232
  99.3 2.1 %collective-permute-start.25 = (bf16[2,88,128]{2,1,0:T(8,128)(2,1)S(1)}, bf16[2,88,128]{2,1,0:T(8,128)(2,1)S(1)}, u32[]{:S(2)}, u32[]{:S(2)}) collective-permute-start(bf16[2,88,128]{2,1,0:T(8,128)(2,1)S(1)} %pad_maximum_fusion.refs_0_), channel_id=1, source_target_pairs={{0,10},{2,12},{4,14},{6,8},{8,2},{10,4},{12,6},{14,0},{1,11},{3,13... | collective-permute-start | bytes 135176 | tf_op jit(solution)/shard_map/ppermute | solution.py:232
  102.3 2.4 %collective-permute-start.23 = (bf16[2,88,128]{2,1,0:T(8,128)(2,1)S(1)}, bf16[2,88,128]{2,1,0:T(8,128)(2,1)S(1)}, u32[]{:S(2)}, u32[]{:S(2)}) collective-permute-start(bf16[2,88,128]{2,1,0:T(8,128)(2,1)S(1)} %pad_maximum_fusion.refs_0_), channel_id=1, source_target_pairs={{0,6},{2,0},{4,2},{6,4},{8,14},{10,8},{12,10},{14,12},{1,7},{3,1},... | collective-permute-start | bytes 135176 | tf_op jit(solution)/shard_map/ppermute | solution.py:232
  104.7 1.5 %collective-permute-start.22 = (bf16[2,88,128]{2,1,0:T(8,128)(2,1)S(1)}, bf16[2,88,128]{2,1,0:T(8,128)(2,1)S(1)}, u32[]{:S(2)}, u32[]{:S(2)}) collective-permute-start(bf16[2,88,128]{2,1,0:T(8,128)(2,1)S(1)} %pad_maximum_fusion.refs_0_), channel_id=1, source_target_pairs={{0,4},{2,6},{4,0},{6,2},{8,12},{10,14},{12,8},{14,10},{1,5},{3,7},... | collective-permute-start | bytes 135176 | tf_op jit(solution)/shard_map/ppermute | solution.py:232
  107.0 2.4 %feats_grad.1 = (bf16[128,1152]{1,0:T(8,128)(2,1)}, bf16[128,1152]{1,0:T(8,128)(2,1)}) custom-call(bf16[128,1152]{1,0:T(8,128)(2,1)S(1)} %get-tuple-element.27.image_dpre, bf16[128,1152]{1,0:T(8,128)(2,1)S(1)} %get-tuple-element.28.text_dpre, bf16[1152,1152]{1,0:T(8,128)(2,1)S(1)} %copy-done.1, bf16[1152,1152]{1,0:T(8,128)(2,1)S(1)} %copy-done.3), custom_call_target="tpu_custom_call" | custom-call | flops 679477248 | bytes 7340032 | tf_op jit(solution)/shard_map/feats_grad/pallas_call | solution.py:32
  110.3 1.3 %place.1 = f32[72,2,1152]{2,1,0:T(2,128)} custom-call(bf16[2,88,128]{2,1,0:T(8,128)(2,1)S(1)} %pad_maximum_fusion.refs_0_, bf16[2,88,128]{2,1,0:T(8,128)(2,1)S(1)} %collective-permute-done.21.refs_1_, bf16[2,88,128]{2,1,0:T(8,128)(2,1)S(1)} %collective-permute-done.22.refs_2_, bf16[2,88,128]{2,1,0:T(8,128)(2,1)S(1)} %collective-permute-done.23.refs_3_, ...), custom_call_target="tpu_custom_call" | custom-call | bytes 1048576 | tf_op jit(solution)/shard_map/place/pallas_call | solution.py:32
  (48 shorter events, 8.2 us)
Async XLA Ops:
  2.8 23.1 %collective-permute-start.11 = (bf16[2,1152,128]{2,1,0:T(8,128)(2,1)S(1)}, bf16[2,1152,128]{2,1,0:T(8,128)(2,1)S(1)}, u32[]{:S(2)}, u32[]{:S(2)}) collective-permute-start(bf16[2,1152,128]{2,1,0:T(8,128)(2,1)S(1)} %turn.1.refs_0_), channel_id=1, source_target_pairs={{0,4},{2,6},{4,0},{6,2},{1,5},{3,7},{5,1},{7,3},{8,12},{10,14},{12... | collective-permute-start | bytes 1769480 | tf_op jit(solution)/shard_map/ppermute | solution.py:224
  6.5 1.7 %copy-start = (bf16[1152,1152]{1,0:T(8,128)(2,1)S(1)}, bf16[1152,1152]{1,0:T(8,128)(2,1)}, u32[]{:S(2)}) copy-start(bf16[1152,1152]{1,0:T(8,128)(2,1)} %image_head.3) | copy-start | bytes 7962628
  8.2 1.7 %copy-start.2 = (bf16[1152,1152]{1,0:T(8,128)(2,1)S(1)}, bf16[1152,1152]{1,0:T(8,128)(2,1)}, u32[]{:S(2)}) copy-start(bf16[1152,1152]{1,0:T(8,128)(2,1)} %text_head.3) | copy-start | bytes 7962628
  11.2 11.0 %collective-permute-start = (bf16[128,1152]{1,0:T(8,128)(2,1)S(1)}, bf16[128,1152]{1,0:T(8,128)(2,1)S(1)}, u32[]{:S(2)}, u32[]{:S(2)}) collective-permute-start(bf16[128,1152]{1,0:T(8,128)(2,1)S(1)} %get-tuple-element.20.v), channel_id=1, source_target_pairs={{0,224},{16,48},{32,0},{48,80},{64,32},{80,112},{96,64},{112,144},... | collective-permute-start | bytes 884744 | tf_op jit(solution)/shard_map/ppermute | solution.py:212
  16.9 7.7 %collective-permute-start.5 = (bf16[128,1152]{1,0:T(8,128)(2,1)S(1)}, bf16[128,1152]{1,0:T(8,128)(2,1)S(1)}, u32[]{:S(2)}, u32[]{:S(2)}) collective-permute-start(bf16[128,1152]{1,0:T(8,128)(2,1)S(1)} %get-tuple-element.19.u), channel_id=1, source_target_pairs={{0,16},{16,0},{1,17},{17,1},{2,18},{18,2},{3,19},{19,3},{4,20},{20... | collective-permute-start | bytes 884744 | tf_op jit(solution)/shard_map/ppermute | solution.py:216
  16.9 15.4 %collective-permute-start.9 = (bf16[2,1152,128]{2,1,0:T(8,128)(2,1)S(1)}, bf16[2,1152,128]{2,1,0:T(8,128)(2,1)S(1)}, u32[]{:S(2)}, u32[]{:S(2)}) collective-permute-start(bf16[2,1152,128]{2,1,0:T(8,128)(2,1)S(1)} %turn.1.refs_0_), channel_id=1, source_target_pairs={{0,6},{2,0},{4,2},{6,4},{1,7},{3,1},{5,3},{7,5},{8,14},{10,8},{12,... | collective-permute-start | bytes 1769480 | tf_op jit(solution)/shard_map/ppermute | solution.py:224
  17.8 8.2 %collective-permute-start.3 = (bf16[128,1152]{1,0:T(8,128)(2,1)S(1)}, bf16[128,1152]{1,0:T(8,128)(2,1)S(1)}, u32[]{:S(2)}, u32[]{:S(2)}) collective-permute-start(bf16[128,1152]{1,0:T(8,128)(2,1)S(1)} %get-tuple-element.19.u), channel_id=1, source_target_pairs={{0,32},{16,240},{32,64},{48,16},{64,96},{80,48},{96,128},{112,80},... | collective-permute-start | bytes 884744 | tf_op jit(solution)/shard_map/ppermute | solution.py:212
  22.2 8.3 %collective-permute-start.1 = (bf16[128,1152]{1,0:T(8,128)(2,1)S(1)}, bf16[128,1152]{1,0:T(8,128)(2,1)S(1)}, u32[]{:S(2)}, u32[]{:S(2)}) collective-permute-start(bf16[128,1152]{1,0:T(8,128)(2,1)S(1)} %collective-permute-done.v1), channel_id=1, source_target_pairs={{0,16},{16,0},{1,17},{17,1},{2,18},{18,2},{3,19},{19,3},{4,20},{20... | collective-permute-start | bytes 884744 | tf_op jit(solution)/shard_map/ppermute | solution.py:216
  24.6 20.5 %collective-permute-start.7 = (bf16[2,1152,128]{2,1,0:T(8,128)(2,1)S(1)}, bf16[2,1152,128]{2,1,0:T(8,128)(2,1)S(1)}, u32[]{:S(2)}, u32[]{:S(2)}) collective-permute-start(bf16[2,1152,128]{2,1,0:T(8,128)(2,1)S(1)} %turn.1.refs_0_), channel_id=1, source_target_pairs={{0,2},{2,4},{4,6},{6,0},{1,3},{3,5},{5,7},{7,1},{8,10},{10,12},{12... | collective-permute-start | bytes 1769480 | tf_op jit(solution)/shard_map/ppermute | solution.py:224
  25.9 10.9 %collective-permute-start.4 = (bf16[128,1152]{1,0:T(8,128)(2,1)S(1)}, bf16[128,1152]{1,0:T(8,128)(2,1)S(1)}, u32[]{:S(2)}, u32[]{:S(2)}) collective-permute-start(bf16[128,1152]{1,0:T(8,128)(2,1)S(1)} %collective-permute-done.3.u1), channel_id=1, source_target_pairs={{0,16},{16,0},{1,17},{17,1},{2,18},{18,2},{3,19},{19,3},{4,20},{20... | collective-permute-start | bytes 884744 | tf_op jit(solution)/shard_map/ppermute | solution.py:216
  26.0 19.4 %collective-permute-start.6 = (bf16[2,1152,128]{2,1,0:T(8,128)(2,1)S(1)}, bf16[2,1152,128]{2,1,0:T(8,128)(2,1)S(1)}, u32[]{:S(2)}, u32[]{:S(2)}) collective-permute-start(bf16[2,1152,128]{2,1,0:T(8,128)(2,1)S(1)} %turn.1.refs_0_), channel_id=1, source_target_pairs={{0,1},{1,0},{2,3},{3,2},{4,5},{5,4},{6,7},{7,6},{8,9},{9,8},{10,11... | collective-permute-start | bytes 1769480 | tf_op jit(solution)/shard_map/ppermute | solution.py:220
  30.5 12.2 %collective-permute-start.2 = (bf16[128,1152]{1,0:T(8,128)(2,1)S(1)}, bf16[128,1152]{1,0:T(8,128)(2,1)S(1)}, u32[]{:S(2)}, u32[]{:S(2)}) collective-permute-start(bf16[128,1152]{1,0:T(8,128)(2,1)S(1)} %collective-permute-done.1.u2), channel_id=1, source_target_pairs={{0,32},{16,240},{32,64},{48,16},{64,96},{80,48},{96,128},{112,80},... | collective-permute-start | bytes 884744 | tf_op jit(solution)/shard_map/ppermute | solution.py:212
  32.3 29.1 %collective-permute-start.12 = (bf16[2,1152,128]{2,1,0:T(8,128)(2,1)S(1)}, bf16[2,1152,128]{2,1,0:T(8,128)(2,1)S(1)}, u32[]{:S(2)}, u32[]{:S(2)}) collective-permute-start(bf16[2,1152,128]{2,1,0:T(8,128)(2,1)S(1)} %collective-permute-done.11.refs_6_), channel_id=1, source_target_pairs={{0,1},{1,0},{2,3},{3,2},{4,5},{5,4},{6,7},{7,6},{8,9},{9,8},{10,11... | collective-permute-start | bytes 1769480 | tf_op jit(solution)/shard_map/ppermute | solution.py:220
  36.8 24.5 %collective-permute-start.10 = (bf16[2,1152,128]{2,1,0:T(8,128)(2,1)S(1)}, bf16[2,1152,128]{2,1,0:T(8,128)(2,1)S(1)}, u32[]{:S(2)}, u32[]{:S(2)}) collective-permute-start(bf16[2,1152,128]{2,1,0:T(8,128)(2,1)S(1)} %collective-permute-done.9.refs_4_), channel_id=1, source_target_pairs={{0,1},{1,0},{2,3},{3,2},{4,5},{5,4},{6,7},{7,6},{8,9},{9,8},{10,11... | collective-permute-start | bytes 1769480 | tf_op jit(solution)/shard_map/ppermute | solution.py:220
  44.7 7.8 %collective-permute-start.14 = (bf16[2,384,128]{2,1,0:T(8,128)(2,1)S(1)}, bf16[2,384,128]{2,1,0:T(8,128)(2,1)S(1)}, u32[]{:S(2)}, u32[]{:S(2)}) collective-permute-start(bf16[2,384,128]{2,1,0:T(8,128)(2,1)S(1)} %get-tuple-element.32), channel_id=1, source_target_pairs={{0,2},{2,4},{4,6},{6,0},{1,3},{3,5},{5,7},{7,1},{8,10},{10,12},{12... | collective-permute-start | bytes 589832 | tf_op jit(solution)/shard_map/ppermute | solution.py:224
  45.1 16.8 %collective-permute-start.8 = (bf16[2,1152,128]{2,1,0:T(8,128)(2,1)S(1)}, bf16[2,1152,128]{2,1,0:T(8,128)(2,1)S(1)}, u32[]{:S(2)}, u32[]{:S(2)}) collective-permute-start(bf16[2,1152,128]{2,1,0:T(8,128)(2,1)S(1)} %collective-permute-done.7.refs_2_), channel_id=1, source_target_pairs={{0,1},{1,0},{2,3},{3,2},{4,5},{5,4},{6,7},{7,6},{8,9},{9,8},{10,11... | collective-permute-start | bytes 1769480 | tf_op jit(solution)/shard_map/ppermute | solution.py:220
  45.4 7.1 %collective-permute-start.16 = (bf16[2,384,128]{2,1,0:T(8,128)(2,1)S(1)}, bf16[2,384,128]{2,1,0:T(8,128)(2,1)S(1)}, u32[]{:S(2)}, u32[]{:S(2)}) collective-permute-start(bf16[2,384,128]{2,1,0:T(8,128)(2,1)S(1)} %get-tuple-element.33), channel_id=1, source_target_pairs={{0,6},{2,0},{4,2},{6,4},{1,7},{3,1},{5,3},{7,5},{8,14},{10,8},{12,... | collective-permute-start | bytes 589832 | tf_op jit(solution)/shard_map/ppermute | solution.py:224
  52.5 7.1 %collective-permute-start.18 = (bf16[2,384,128]{2,1,0:T(8,128)(2,1)S(1)}, bf16[2,384,128]{2,1,0:T(8,128)(2,1)S(1)}, u32[]{:S(2)}, u32[]{:S(2)}) collective-permute-start(bf16[2,384,128]{2,1,0:T(8,128)(2,1)S(1)} %get-tuple-element.34), channel_id=1, source_target_pairs={{0,4},{2,6},{4,0},{6,2},{1,5},{3,7},{5,1},{7,3},{8,12},{10,14},{12... | collective-permute-start | bytes 589832 | tf_op jit(solution)/shard_map/ppermute | solution.py:224
  52.5 10.0 %collective-permute-start.13 = (bf16[2,384,128]{2,1,0:T(8,128)(2,1)S(1)}, bf16[2,384,128]{2,1,0:T(8,128)(2,1)S(1)}, u32[]{:S(2)}, u32[]{:S(2)}) collective-permute-start(bf16[2,384,128]{2,1,0:T(8,128)(2,1)S(1)} %get-tuple-element.31.refs_0_), channel_id=1, source_target_pairs={{0,1},{1,0},{2,3},{3,2},{4,5},{5,4},{6,7},{7,6},{8,9},{9,8},{10,11... | collective-permute-start | bytes 589832 | tf_op jit(solution)/shard_map/ppermute | solution.py:220
  59.7 2.9 %collective-permute-start.15 = (bf16[2,384,128]{2,1,0:T(8,128)(2,1)S(1)}, bf16[2,384,128]{2,1,0:T(8,128)(2,1)S(1)}, u32[]{:S(2)}, u32[]{:S(2)}) collective-permute-start(bf16[2,384,128]{2,1,0:T(8,128)(2,1)S(1)} %collective-permute-done.14.refs_2_), channel_id=1, source_target_pairs={{0,1},{1,0},{2,3},{3,2},{4,5},{5,4},{6,7},{7,6},{8,9},{9,8},{10,11... | collective-permute-start | bytes 589832 | tf_op jit(solution)/shard_map/ppermute | solution.py:220
  61.4 1.4 %collective-permute-start.17 = (bf16[2,384,128]{2,1,0:T(8,128)(2,1)S(1)}, bf16[2,384,128]{2,1,0:T(8,128)(2,1)S(1)}, u32[]{:S(2)}, u32[]{:S(2)}) collective-permute-start(bf16[2,384,128]{2,1,0:T(8,128)(2,1)S(1)} %collective-permute-done.16.refs_4_), channel_id=1, source_target_pairs={{0,1},{1,0},{2,3},{3,2},{4,5},{5,4},{6,7},{7,6},{8,9},{9,8},{10,11... | collective-permute-start | bytes 589832 | tf_op jit(solution)/shard_map/ppermute | solution.py:220
  61.4 1.7 %collective-permute-start.19 = (bf16[2,384,128]{2,1,0:T(8,128)(2,1)S(1)}, bf16[2,384,128]{2,1,0:T(8,128)(2,1)S(1)}, u32[]{:S(2)}, u32[]{:S(2)}) collective-permute-start(bf16[2,384,128]{2,1,0:T(8,128)(2,1)S(1)} %collective-permute-done.18.refs_6_), channel_id=1, source_target_pairs={{0,1},{1,0},{2,3},{3,2},{4,5},{5,4},{6,7},{7,6},{8,9},{9,8},{10,11... | collective-permute-start | bytes 589832 | tf_op jit(solution)/shard_map/ppermute | solution.py:220
  62.6 44.5 %copy-start.1 = (bf16[1152,1152]{1,0:T(8,128)(2,1)S(1)}, bf16[1152,1152]{1,0:T(8,128)(2,1)}, u32[]{:S(2)}) copy-start(bf16[1152,1152]{1,0:T(8,128)(2,1)} %image_head.3) | copy-start | bytes 7962628
  62.6 44.5 %copy-start.3 = (bf16[1152,1152]{1,0:T(8,128)(2,1)S(1)}, bf16[1152,1152]{1,0:T(8,128)(2,1)}, u32[]{:S(2)}) copy-start(bf16[1152,1152]{1,0:T(8,128)(2,1)} %text_head.3) | copy-start | bytes 7962628
  92.5 3.5 %collective-permute-start.20 = (bf16[88,128]{1,0:T(8,128)(2,1)S(1)}, bf16[88,128]{1,0:T(8,128)(2,1)S(1)}, u32[]{:S(2)}, u32[]{:S(2)}) collective-permute-start(bf16[88,128]{1,0:T(8,128)(2,1)S(1)} %add.1), channel_id=1, source_target_pairs={{0,1},{1,0},{2,3},{3,2},{4,5},{5,4},{6,7},{7,6},{8,9},{9,8},{10,11... | collective-permute-start | bytes 67592 | tf_op jit(solution)/shard_map/ppermute | solution.py:220
  96.0 8.7 %collective-permute-start.27 = (bf16[2,88,128]{2,1,0:T(8,128)(2,1)S(1)}, bf16[2,88,128]{2,1,0:T(8,128)(2,1)S(1)}, u32[]{:S(2)}, u32[]{:S(2)}) collective-permute-start(bf16[2,88,128]{2,1,0:T(8,128)(2,1)S(1)} %pad_maximum_fusion.refs_0_), channel_id=1, source_target_pairs={{0,14},{2,8},{4,10},{6,12},{8,6},{10,0},{12,2},{14,4},{1,15},{3,9}... | collective-permute-start | bytes 135176 | tf_op jit(solution)/shard_map/ppermute | solution.py:232
  97.8 8.4 %collective-permute-start.26 = (bf16[2,88,128]{2,1,0:T(8,128)(2,1)S(1)}, bf16[2,88,128]{2,1,0:T(8,128)(2,1)S(1)}, u32[]{:S(2)}, u32[]{:S(2)}) collective-permute-start(bf16[2,88,128]{2,1,0:T(8,128)(2,1)S(1)} %pad_maximum_fusion.refs_0_), channel_id=1, source_target_pairs={{0,12},{2,14},{4,8},{6,10},{8,4},{10,6},{12,0},{14,2},{1,13},{3,15... | collective-permute-start | bytes 135176 | tf_op jit(solution)/shard_map/ppermute | solution.py:232
  99.3 10.1 %collective-permute-start.25 = (bf16[2,88,128]{2,1,0:T(8,128)(2,1)S(1)}, bf16[2,88,128]{2,1,0:T(8,128)(2,1)S(1)}, u32[]{:S(2)}, u32[]{:S(2)}) collective-permute-start(bf16[2,88,128]{2,1,0:T(8,128)(2,1)S(1)} %pad_maximum_fusion.refs_0_), channel_id=1, source_target_pairs={{0,10},{2,12},{4,14},{6,8},{8,2},{10,4},{12,6},{14,0},{1,11},{3,13... | collective-permute-start | bytes 135176 | tf_op jit(solution)/shard_map/ppermute | solution.py:232
  101.4 8.1 %collective-permute-start.24 = (bf16[2,88,128]{2,1,0:T(8,128)(2,1)S(1)}, bf16[2,88,128]{2,1,0:T(8,128)(2,1)S(1)}, u32[]{:S(2)}, u32[]{:S(2)}) collective-permute-start(bf16[2,88,128]{2,1,0:T(8,128)(2,1)S(1)} %pad_maximum_fusion.refs_0_), channel_id=1, source_target_pairs={{0,8},{2,10},{4,12},{6,14},{8,0},{10,2},{12,4},{14,6},{1,9},{3,11}... | collective-permute-start | bytes 135176 | tf_op jit(solution)/shard_map/ppermute | solution.py:232
  102.3 7.2 %collective-permute-start.23 = (bf16[2,88,128]{2,1,0:T(8,128)(2,1)S(1)}, bf16[2,88,128]{2,1,0:T(8,128)(2,1)S(1)}, u32[]{:S(2)}, u32[]{:S(2)}) collective-permute-start(bf16[2,88,128]{2,1,0:T(8,128)(2,1)S(1)} %pad_maximum_fusion.refs_0_), channel_id=1, source_target_pairs={{0,6},{2,0},{4,2},{6,4},{8,14},{10,8},{12,10},{14,12},{1,7},{3,1},... | collective-permute-start | bytes 135176 | tf_op jit(solution)/shard_map/ppermute | solution.py:232
  104.7 4.8 %collective-permute-start.22 = (bf16[2,88,128]{2,1,0:T(8,128)(2,1)S(1)}, bf16[2,88,128]{2,1,0:T(8,128)(2,1)S(1)}, u32[]{:S(2)}, u32[]{:S(2)}) collective-permute-start(bf16[2,88,128]{2,1,0:T(8,128)(2,1)S(1)} %pad_maximum_fusion.refs_0_), channel_id=1, source_target_pairs={{0,4},{2,6},{4,0},{6,2},{8,12},{10,14},{12,8},{14,10},{1,5},{3,7},... | collective-permute-start | bytes 135176 | tf_op jit(solution)/shard_map/ppermute | solution.py:232
  106.2 4.1 %collective-permute-start.21 = (bf16[2,88,128]{2,1,0:T(8,128)(2,1)S(1)}, bf16[2,88,128]{2,1,0:T(8,128)(2,1)S(1)}, u32[]{:S(2)}, u32[]{:S(2)}) collective-permute-start(bf16[2,88,128]{2,1,0:T(8,128)(2,1)S(1)} %pad_maximum_fusion.refs_0_), channel_id=1, source_target_pairs={{0,2},{2,4},{4,6},{6,0},{8,10},{10,12},{12,14},{14,8},{1,3},{3,5},... | collective-permute-start | bytes 135176 | tf_op jit(solution)/shard_map/ppermute | solution.py:232
  (2 other events, 1.9 us)

commit v2 on v1

v2 whole, which is shorter than its diff:
```python
import functools

import jax
import jax.numpy as jnp
from jax import lax
from jax.experimental import pallas as pl
from jax.experimental.pallas import tpu as pltpu
from jax.sharding import Mesh
from jax.sharding import PartitionSpec as P

EPSILON = 1e-06
F32 = jnp.float32
BF16 = jnp.bfloat16

BLK = ("z", "ylo")
REP = ("yhi", "x", "core")
NZ, NYLO, NYHI, NX, NCORE = 8, 2, 2, 4, 2
D = 1152
ROWS = 128
LANES = 128
MAIN = 2 * LANES
TAIL_AT = NX * MAIN
SENT = MAIN + LANES
PER_BLK = D // (NZ * NYLO)
TAIL_ROWS = PER_BLK // (NX * NYHI)
PIECE = PER_BLK + TAIL_ROWS
NY = NYLO * NYHI
MIB = 1024 * 1024


def call(kernel, name, out_shape, args, in_specs=None, scratch=(), mib=24):
    return pl.pallas_call(
        kernel,
        out_shape=out_shape,
        in_specs=in_specs or [pl.BlockSpec(memory_space=pltpu.VMEM)] * len(args),
        scratch_shapes=list(scratch),
        compiler_params=pltpu.CompilerParams(vmem_limit_bytes=mib * MIB),
        cost_estimate=pl.CostEstimate(flops=1, bytes_accessed=1, transcendentals=0),
        name=name,
    )(*args)


def shape(dims, dtype=BF16):
    return jax.ShapeDtypeStruct(dims, dtype)


VMEM_SPEC = pl.BlockSpec(memory_space=pltpu.VMEM)
HBM_SPEC = pl.BlockSpec(memory_space=pltpu.HBM)
SMEM_SPEC = pl.BlockSpec(memory_space=pltpu.SMEM)


def nt(left, right):
    return lax.dot_general(left, right, (((1,), (1,)), ((), ())), preferred_element_type=F32)


def nn(left, right):
    return lax.dot_general(left, right, (((1,), (0,)), ((), ())), preferred_element_type=F32)


def pick(flag, if_zero, if_one):
    return jnp.where(flag == 0, if_zero, if_one)


def project(rows, head):
    pre = nn(rows, head[...])
    norm = jnp.sqrt(jnp.sum(pre * pre, axis=1, keepdims=True) + EPSILON)
    return pre / norm, norm


def choose_kernel(image, text, both, raw_u):
    core = lax.axis_index("core")
    both[0] = pick(core, image[...], text[...])
    both[1] = pick(core, text[...], image[...])
    raw_u[...] = pick(lax.axis_index("ylo"), text[...], image[...])


def pack_feats_kernel(both, across, packed):
    packed[0] = both[0]
    packed[1] = across[1]


def project_kernel(
    image, text, image_head_hbm, text_head_hbm,
    emb_u, emb_v, unit_u, unit_v, norm_u, norm_v, image_head, text_head, sems,
):
    col = lax.axis_index("ylo")
    image_copy = pltpu.make_async_copy(image_head_hbm, image_head, sems.at[0])
    text_copy = pltpu.make_async_copy(text_head_hbm, text_head, sems.at[1])
    image_copy.start()
    text_copy.start()
    image_copy.wait()
    image_unit, image_norm = project(image[...], image_head)
    text_copy.wait()
    text_unit, text_norm = project(text[...], text_head)
    u = pick(col, text_unit, image_unit)
    v = pick(col, image_unit, text_unit)
    emb_u[...] = u.astype(BF16)
    emb_v[...] = v.astype(BF16)
    unit_u[...] = u
    unit_v[...] = v
    norm_u[...] = pick(col, text_norm, image_norm)
    norm_v[...] = pick(col, image_norm, text_norm)


def project_came_kernel(image, text, image_head, text_head, emb_u, emb_v):
    col = lax.axis_index("ylo")
    images = project(image[...], image_head)[0].astype(BF16)
    texts = project(text[...], text_head)[0].astype(BF16)
    emb_u[...] = pick(col, texts, images)
    emb_v[...] = pick(col, images, texts)


def turn_kernel(*refs):
    parts, turned = refs[:-1], refs[-1]
    blocks = [part[side] for part in parts[:-2] for side in range(NCORE)]
    blocks += [part[...] for part in parts[-2:]]
    for place, rows in enumerate(blocks):
        turned[:, place * ROWS:(place + 1) * ROWS] = rows.astype(F32).T.astype(BF16)


def pair_weights(own, other, scalars, same):
    scale = jnp.exp(scalars[0])
    logits = scale * nt(own, other) + scalars[1]
    probs = jax.nn.sigmoid(logits)
    if same:
        row = lax.broadcasted_iota(jnp.int32, probs.shape, 0)
        column = lax.broadcasted_iota(jnp.int32, probs.shape, 1)
        probs = probs - jnp.where(row == column, 1.0, 0.0)
    return (scale * probs).astype(BF16)


def pull(own, other, scalars, same=False):
    return nn(pair_weights(own, other, scalars, same), other)


def early_kernel(scalars, u, v, u1, v1, raw_v0, image_head, text_head, grad_u, grad_v, emb_v0):
    col = lax.axis_index("ylo")

    @pl.when(col == 0)
    def _():
        emb_v0[...] = project(raw_v0[...], image_head)[0].astype(BF16)

    @pl.when(col == 1)
    def _():
        emb_v0[...] = project(raw_v0[...], text_head)[0].astype(BF16)

    own_u, own_v = u[...], v[...]
    grad_u[...] = (
        pull(own_u, own_v, scalars, True)
        + pull(own_u, v1[...], scalars)
        + pull(own_u, emb_v0[...], scalars)
    )
    grad_v[...] = pull(own_v, own_u, scalars, True) + pull(own_v, u1[...], scalars)


def middle_kernel(scalars, v, u2, grad_v, out):
    out[...] = grad_v[...] + pull(v[...], u2[...], scalars)


def late_kernel(
    scalars, u, v, u3, v3, grad_u, grad_v, unit_u, unit_v, norm_u, norm_v,
    image_dpre, text_dpre, mine_parts, other_parts, mine_t, other_t,
):
    col = lax.axis_index("ylo")
    core = lax.axis_index("core")
    at = lax.axis_index("x")

    def backward(grad, unit, norm):
        radial = jnp.sum(unit * grad, axis=1, keepdims=True)
        return (grad - unit * radial) / norm

    dpre_u = backward(grad_u[...] + pull(u[...], v3[...], scalars), unit_u[...], norm_u[...])
    dpre_v = backward(grad_v[...] + pull(v[...], u3[...], scalars), unit_v[...], norm_v[...])
    image = pick(col, dpre_v, dpre_u)
    text = pick(col, dpre_u, dpre_v)
    image_dpre[...] = image.astype(BF16)
    text_dpre[...] = text.astype(BF16)
    mine_t[...] = pick(core, image, text).T.astype(BF16)
    other_t[...] = pick(core, text, image).T.astype(BF16)
    for step in range(NX):
        to = lax.rem(at + step, NX)
        rows = pl.ds(pl.multiple_of(to * MAIN, MAIN), MAIN)
        for turned, parts in ((mine_t, mine_parts), (other_t, other_parts)):
            parts[step, :MAIN, :] = turned[rows, :]
            parts[step, MAIN:, :] = turned[TAIL_AT:, :]


def pack_parts_kernel(mine, across, *packed):
    for step, part in enumerate(packed):
        part[0] = mine[step]
        part[1] = across[step]


def feats_grad_kernel(image_dpre, text_dpre, image_head, text_head, image_out, text_out):
    image_out[...] = nt(image_dpre[...], image_head[...]).astype(BF16)
    text_out[...] = nt(text_dpre[...], text_head[...]).astype(BF16)


def head_kernel(feats_t, *refs):
    parts, pieces, right, total, tails = refs[:NX], refs[NX:NX + NY], *refs[NX + NY:]
    at = lax.axis_index("x")
    y = NYLO * lax.axis_index("yhi") + lax.axis_index("ylo")
    for place, part in enumerate(parts):
        for side in range(NCORE):
            start = (place * NCORE + side) * ROWS
            right[:, start:start + ROWS] = part[side]
    total[...] = nt(feats_t[...], right[...])
    tails[...] = total[:, MAIN:]
    for step, piece in enumerate(pieces):
        to = lax.rem(y + step, NY)
        half, low = to // NYLO, lax.rem(to, NYLO)
        lanes = pl.ds(pl.multiple_of(half * LANES, LANES), LANES)
        for z in range(NZ):
            start = pl.multiple_of((z * NYLO + low) * PER_BLK, 8)
            tail = start + (NYHI * at + half) * TAIL_ROWS
            rows = [
                total[pl.ds(start, PER_BLK), lanes],
                tails[pl.ds(tail, TAIL_ROWS), :],
            ]
            piece[z] = jnp.concatenate(rows, axis=0).astype(BF16)


def add_kernel(*refs):
    parts, out = refs[:-1], refs[-1]
    total = parts[0][...].astype(F32)
    for part in parts[1:]:
        total = total + part[...].astype(F32)
    out[...] = total.astype(BF16)


def add_z_kernel(pieces, out):
    total = pieces[0].astype(F32)
    for place in range(1, NZ):
        total = total + pieces[place].astype(F32)
    out[...] = total.astype(BF16)


def place_kernel(*refs):
    parts, out = refs[:-1], refs[-1]
    core = lax.axis_index("core")
    at = lax.axis_index("x")
    half_at = lax.axis_index("yhi")
    for step, part in enumerate(parts):
        came_x = lax.rem(at + NX - step, NX)
        for flip in range(NYHI):
            index = NYHI * came_x + lax.rem(half_at + flip, NYHI)
            mine = part[flip, 0].astype(F32)
            other = part[flip, 1].astype(F32)
            both = jnp.stack([pick(core, mine, other), pick(core, other, mine)], axis=1)
            out[:, :, pl.ds(pl.multiple_of(index * LANES, LANES), LANES)] = both[:PER_BLK]
            out[pl.ds(index * TAIL_ROWS, TAIL_ROWS), :, TAIL_AT:] = both[PER_BLK:PER_BLK + TAIL_ROWS]


def z_shift(array, by):
    return lax.ppermute(array, "z", [(z, (z + by) % NZ) for z in range(NZ)])


def u_shift(array):
    pairs = []
    for z in range(NZ):
        pairs.append((z * NYLO, ((z + 1) % NZ) * NYLO))
        pairs.append((z * NYLO + 1, ((z - 1) % NZ) * NYLO + 1))
    return lax.ppermute(array, BLK, pairs)


def y_swap(array):
    return lax.ppermute(array, "ylo", [(0, 1), (1, 0)])


def core_swap(array):
    return lax.ppermute(array, "core", [(0, 1), (1, 0)])


def x_turn(array, by):
    return lax.ppermute(array, "x", [(i, (i + by) % NX) for i in range(NX)])


def y_turn(array, by):
    index = lambda y: (y % NYLO) * NYHI + y // NYLO
    pairs = [(index(y), index((y + by) % NY)) for y in range(NY)]
    return lax.ppermute(array, ("ylo", "yhi"), pairs)


def half_swap(array, flip, swap):
    pairs = []
    for half in range(NYHI):
        for x in range(NX):
            for core in range(NCORE):
                start = (half * NX + x) * NCORE + core
                pairs.append((start, ((half ^ flip) * NX + x) * NCORE + (core ^ swap)))
    return lax.ppermute(array, REP, pairs)


def body(image_feats, text_feats, image_head, text_head, log_scale, bias):
    image = image_feats[0]
    text = text_feats[0]
    scalars = jnp.concatenate([log_scale, bias])
    block = shape((ROWS, D))
    block32 = shape((ROWS, D), F32)
    column = shape((ROWS, 1), F32)

    text_1 = z_shift(text, 1)
    image_1 = z_shift(image, -1)
    both, raw_u = call(choose_kernel, "choose", [shape((2, ROWS, D)), block], (image, text))
    raw_v0 = y_swap(raw_u)
    packed = call(pack_feats_kernel, "pack_feats", shape((2, ROWS, D)), (both, core_swap(both)))
    feats_1, feats_3 = x_turn(packed, 1), x_turn(packed, 3)
    u, v, unit_u, unit_v, norm_u, norm_v, image_head, text_head = call(
        project_kernel, "project",
        [block, block, block32, block32, column, column, shape((D, D)), shape((D, D))],
        (image, text, image_head, text_head),
        in_specs=[VMEM_SPEC] * 2 + [HBM_SPEC] * 2,
        scratch=[pltpu.SemaphoreType.DMA((2,))], mib=46,
    )
    image_1, text_1, raw_v0, packed = lax.optimization_barrier((image_1, text_1, raw_v0, packed))
    u1, v1 = call(
        project_came_kernel, "project_came", [block, block],
        (image_1, text_1, image_head, text_head),
    )
    u2 = y_swap(v1)
    v3 = y_swap(u1)
    raw_v0, u1 = lax.optimization_barrier((raw_v0, u1))
    grad_u, grad_v = call(
        early_kernel, "early", [block32, block32],
        (scalars, u, v, u1, v1, raw_v0, image_head, text_head),
        in_specs=[SMEM_SPEC] + [VMEM_SPEC] * 7,
        scratch=[pltpu.VMEM((ROWS, D), BF16)],
    )
    u2, grad_u, grad_v, feats_1, feats_3 = lax.optimization_barrier(
        (u2, grad_u, grad_v, feats_1, feats_3)
    )
    u3 = u_shift(u2)
    feats_2 = (x_turn(feats_1[0], 1), x_turn(feats_3[1], 3))
    grad_v = call(
        middle_kernel, "middle", block32, (scalars, v, u2, grad_v),
        in_specs=[SMEM_SPEC] + [VMEM_SPEC] * 3,
    )
    u3, v3, feats_2 = lax.optimization_barrier((u3, v3, feats_2))
    parts = shape((NX, SENT, ROWS))
    image_dpre, text_dpre, mine_parts, other_parts = call(
        late_kernel, "late", [block, block, parts, parts],
        (scalars, u, v, u3, v3, grad_u, grad_v, unit_u, unit_v, norm_u, norm_v),
        in_specs=[SMEM_SPEC] + [VMEM_SPEC] * 10,
        scratch=[pltpu.VMEM((D, ROWS), BF16)] * 2,
    )
    across = core_swap(other_parts)
    parts = call(
        pack_parts_kernel, "pack_parts", [shape((2, SENT, ROWS))] * NX, (mine_parts, across)
    )
    feats_1, feats_2, feats_3, image_dpre, text_dpre = lax.optimization_barrier(
        (feats_1, feats_2, feats_3, image_dpre, text_dpre)
    )
    image_out, text_out = call(
        feats_grad_kernel, "feats_grad", [block, block],
        (image_dpre, text_dpre, image_head, text_head),
    )
    feats_t = call(
        turn_kernel, "turn", shape((D, NX * NCORE * ROWS)), (packed, feats_1, feats_3, *feats_2)
    )
    came = [x_turn(parts[1], 1), x_turn(parts[3], 3), x_turn(parts[2], 2)]
    came, image_out, text_out, feats_t = lax.optimization_barrier(
        (came, image_out, text_out, feats_t)
    )
    pieces = call(
        head_kernel, "head", [shape((NZ, PIECE, LANES))] * NY, [feats_t, parts[0]] + came,
        scratch=[
            pltpu.VMEM((SENT, NX * NCORE * ROWS), BF16),
            pltpu.VMEM((D, SENT), F32),
            pltpu.VMEM((D, LANES), F32),
        ],
    )
    pieces = [pieces[0]] + [y_turn(pieces[by], by) for by in (2, 1, 3)]
    pieces = call(add_kernel, "add_y", shape((NZ, PIECE, LANES)), pieces)
    pieces = lax.all_to_all(pieces, "z", 0, 0, tiled=True)
    mine = call(add_z_kernel, "add_z", shape((PIECE, LANES)), (pieces,))
    four = jnp.stack([mine] + [half_swap(mine, flip, swap) for flip, swap in ((0, 1), (1, 0), (1, 1))])
    four = four.reshape(NYHI, NCORE, PIECE, LANES)
    places = [four] + [x_turn(four, by) for by in (1, 2, 3)]
    head_grads = call(place_kernel, "place", shape((PER_BLK, 2, D), F32), places)
    return (image_out[None], text_out[None], head_grads)


def solution(mesh):
    split = Mesh(mesh.devices.reshape(NZ, NYLO, NYHI, NX, NCORE), BLK + REP)
    rows = P(REP, BLK, None)
    return jax.shard_map(
        body,
        mesh=split,
        in_specs=(rows, rows, P(), P(), P(), P()),
        out_specs=(rows, rows, P(BLK, None, None)),
        check_vma=False,
    )
```

time: 113 us -> 103 us (0.912)
  blocking collectives: 27.7 us -> 11.5 us
  waiting for transfers between devices: 24.7 us -> 31.9 us
  Pallas kernels: 12 us -> 19 us
  local copies, waits for them, and re-layouts: 5.43 us -> 0.05 us
  starting transfers between devices: 39.7 us -> 37.7 us
    all_to_all x1, blocking collectives: 27.7 us -> 11.5 us  [body(): pieces = lax.all_to_all(pieces, 'z', 0, 0, tiled=True)]
    pallas_call x9 -> x14, Pallas kernels: 12 us -> 19 us  [call(): pl.pallas_call(kernel, out_shape=out_shape, in_specs=in_specs or [pl.Bloc...]
    unnamed x12 -> x0, local copies, waits for them, and re-layouts: 5.43 us -> none
    ppermute x9 -> x2, starting transfers between devices: 13.1 us -> 8.67 us  [core_swap(): return lax.ppermute(array, 'core', [(0, 1), (1, 0)])]
    ppermute x10 -> x9, waiting for transfers between devices: 6.34 us -> 9.93 us  [the longest x3 5.55 us: y_turn(): return lax.ppermute(array, ('ylo', 'yhi'), pairs)]
    ppermute x6 -> x10, waiting for transfers between devices: 12.9 us -> 16.4 us  [x_turn(): return lax.ppermute(array, 'x', [(i, (i + by) % NX) for i in range(NX)])]
    ppermute x6 -> x10, starting transfers between devices: 7.58 us -> 11 us  [x_turn(): return lax.ppermute(array, 'x', [(i, (i + by) % NX) for i in range(NX)])]
    ppermute x10 -> x9, starting transfers between devices: 16.6 us -> 15.2 us  [the longest x3 5.71 us: half_swap(): return lax.ppermute(array, REP, pairs)]
  transfers between devices with their start and end apart: 28 -> 24, of which waited for: 11 -> 17; matrix products, arithmetic and copies ran while one was open for 0% -> 0% of each run, Pallas kernels for 8% -> 12%
where the time goes in v2:
time: 103 us; the launch traced here: 102 us
  starting transfers between devices  37.7 us (37%)
  waiting for transfers between devices  31.9 us (31%)
  Pallas kernels  19 us (18%)
  blocking collectives  11.5 us (11%)
  between operations  2.04 us (2%)
    pallas_call x14, Pallas kernels, call(): pl.pallas_call(kernel, out_shape=out_shape, in_specs=in_specs or [pl.Bloc...  19 us
    ppermute x10, waiting for transfers between devices, x_turn(): return lax.ppermute(array, 'x', [(i, (i + by) % NX) for i in range(NX)])  16.4 us
    all_to_all x1, blocking collectives, body(): pieces = lax.all_to_all(pieces, 'z', 0, 0, tiled=True)  11.5 us
    ppermute x10, starting transfers between devices, x_turn(): return lax.ppermute(array, 'x', [(i, (i + by) % NX) for i in range(NX)])  11 us
    ppermute x2, starting transfers between devices, core_swap(): return lax.ppermute(array, 'core', [(0, 1), (1, 0)])  8.67 us
    ppermute x3, starting transfers between devices, half_swap(): return lax.ppermute(array, REP, pairs)  5.71 us
    ppermute x3, starting transfers between devices, y_turn(): return lax.ppermute(array, ('ylo', 'yhi'), pairs)  5.68 us
    ppermute x3, waiting for transfers between devices, y_turn(): return lax.ppermute(array, ('ylo', 'yhi'), pairs)  5.55 us
  transfers between devices with their start and end apart: 24, of which 17 were waited for; matrix products, arithmetic and copies ran while one was open for 0% of the time, Pallas kernels for 12%

profile of v2, /device:TPU:1, one launch (start us, length us, event | category | flops | bytes accessed | tf_op | source)
XLA Modules:
  0.0 102.4 jit_solution(4282124426855138595)
XLA Ops:
  1.8 3.3 %collective-permute-start.3 = (bf16[2,128,1152]{2,1,0:T(8,128)(2,1)S(1)}, bf16[2,128,1152]{2,1,0:T(8,128)(2,1)S(1)}, u32[]{:S(2)}, u32[]{:S(2)}) collective-permute-start(bf16[2,128,1152]{2,1,0:T(8,128)(2,1)S(1)} %get-tuple-element.61.both), channel_id=1, source_target_pairs={{0,1},{1,0},{2,3},{3,2},{4,5},{5,4},{6,7},{7,6},{8,9},{9,8},{10,11... | collective-permute-start | bytes 1769480 | tf_op jit(solution)/shard_map/ppermute | solution.py:271
  5.1 3.9 %collective-permute-start = (bf16[128,1152]{1,0:T(8,128)(2,1)}, bf16[128,1152]{1,0:T(8,128)(2,1)S(1)}, u32[]{:S(2)}, u32[]{:S(2)}) collective-permute-start(bf16[128,1152]{1,0:T(8,128)(2,1)} %bitcast.image), channel_id=1, source_target_pairs={{0,224},{32,0},{64,32},{96,64},{128,96},{160,128},{192,160},{224,1... | collective-permute-start | bytes 884744 | tf_op jit(solution)/shard_map/ppermute | solution.py:255
  9.0 1.3 %collective-permute-start.2 = (bf16[128,1152]{1,0:T(8,128)(2,1)S(1)}, bf16[128,1152]{1,0:T(8,128)(2,1)S(1)}, u32[]{:S(2)}, u32[]{:S(2)}) collective-permute-start(bf16[128,1152]{1,0:T(8,128)(2,1)S(1)} %get-tuple-element.60), channel_id=1, source_target_pairs={{0,16},{16,0},{1,17},{17,1},{2,18},{18,2},{3,19},{19,3},{4,20},{20... | collective-permute-start | bytes 884744 | tf_op jit(solution)/shard_map/ppermute | solution.py:267
  10.3 2.6 %collective-permute-start.6 = (bf16[2,128,1152]{2,1,0:T(8,128)(2,1)S(1)}, bf16[2,128,1152]{2,1,0:T(8,128)(2,1)S(1)}, u32[]{:S(2)}, u32[]{:S(2)}) collective-permute-start(bf16[2,128,1152]{2,1,0:T(8,128)(2,1)S(1)} %pack_feats.1.refs_0_), channel_id=1, source_target_pairs={{0,6},{2,0},{4,2},{6,4},{1,7},{3,1},{5,3},{7,5},{8,14},{10,8},{12,... | collective-permute-start | bytes 1769480 | tf_op jit(solution)/shard_map/ppermute | solution.py:275
  12.9 4.4 %project.1 = (bf16[128,1152]{1,0:T(8,128)(2,1)S(1)}, bf16[128,1152]{1,0:T(8,128)(2,1)S(1)}, f32[128,1152]{1,0:T(8,128)S(1)}, f32[128,1152]{1,0:T(8,128)S(1)}, f3...) custom-call(bf16[128,1152]{1,0:T(8,128)(2,1)} %bitcast.image, ...), custom_call_target="tpu_custom_call" | custom-call | flops 1 | bytes 1 | tf_op jit(solution)/shard_map/project/pallas_call | solution.py:32
  17.3 1.3 %collective-permute-done.1.text = bf16[128,1152]{1,0:T(8,128)(2,1)S(1)} collective-permute-done((bf16[128,1152]{1,0:T(8,128)(2,1)}, bf16[128,1152]{1,0:T(8,128)(2,1)S(1)}, u32[]{:S(2)}, u32[]{:S(2)}) %collective-permute-start.1) | collective-permute-done | bytes 294944 | tf_op jit(solution)/shard_map/ppermute | solution.py:255
  18.6 1.2 %project_came.1 = (bf16[128,1152]{1,0:T(8,128)(2,1)S(1)}, bf16[128,1152]{1,0:T(8,128)(2,1)S(1)}) custom-call(bf16[128,1152]{1,0:T(8,128)(2,1)S(1)} %collective-permute-done.image, bf16[128,1152]{1,0:T(8,128)(2,1)S(1)} %collective-permute-done.1.text, bf16[1152,1152]{1,0:T(8,128)(2,1)S(1)} %get-tuple-element.64.image_head, ...), custom_call_target="tpu_custom_call" | custom-call | flops 1 | bytes 1 | tf_op jit(solution)/shard_map/project_came/pallas_call | solution.py:32
  19.8 1.4 %collective-permute-start.4 = (bf16[128,1152]{1,0:T(8,128)(2,1)S(1)}, bf16[128,1152]{1,0:T(8,128)(2,1)S(1)}, u32[]{:S(2)}, u32[]{:S(2)}) collective-permute-start(bf16[128,1152]{1,0:T(8,128)(2,1)S(1)} %get-tuple-element.66.v1), channel_id=1, source_target_pairs={{0,16},{16,0},{1,17},{17,1},{2,18},{18,2},{3,19},{19,3},{4,20},{20... | collective-permute-start | bytes 884744 | tf_op jit(solution)/shard_map/ppermute | solution.py:267
  22.8 2.8 %early.1 = (f32[128,1152]{1,0:T(8,128)S(1)}, f32[128,1152]{1,0:T(8,128)S(1)}) custom-call(f32[2]{0:T(128)S(1)} %pad_maximum_fusion.1.scalars, bf16[128,1152]{1,0:T(8,128)(2,1)S(1)} %get-tuple-element.58.u, bf16[128,1152]{1,0:T(8,128)(2,1)S(1)} %get-tuple-element.59.v, bf16[128,1152]{1,0:T(8,128)(2,1)S(1)} %get-tuple-element.69.u1, ...), custom_call_target="tpu_custom_call" | custom-call | flops 1 | bytes 1 | tf_op jit(solution)/shard_map/early/pallas_call | solution.py:32
  25.6 1.6 %collective-permute-done.4.u2 = bf16[128,1152]{1,0:T(8,128)(2,1)S(1)} collective-permute-done((bf16[128,1152]{1,0:T(8,128)(2,1)S(1)}, bf16[128,1152]{1,0:T(8,128)(2,1)S(1)}, u32[]{:S(2)}, u32[]{:S(2)}) %collective-permute-start.4) | collective-permute-done | bytes 294944 | tf_op jit(solution)/shard_map/ppermute | solution.py:267
  28.1 1.8 %collective-permute-start.10 = (bf16[128,1152]{1,0:T(8,128)(2,1)S(1)}, bf16[128,1152]{1,0:T(8,128)(2,1)S(1)}, u32[]{:S(2)}, u32[]{:S(2)}) collective-permute-start(bf16[128,1152]{1,0:T(8,128)(2,1)S(1)} %slice_bitcast_fusion), channel_id=1, source_target_pairs={{0,6},{2,0},{4,2},{6,4},{1,7},{3,1},{5,3},{7,5},{8,14},{10,8},{12,... | collective-permute-start | bytes 884744 | tf_op jit(solution)/shard_map/ppermute | solution.py:275
  31.0 2.6 %collective-permute-done.8.v3 = bf16[128,1152]{1,0:T(8,128)(2,1)S(1)} collective-permute-done((bf16[128,1152]{1,0:T(8,128)(2,1)S(1)}, bf16[128,1152]{1,0:T(8,128)(2,1)S(1)}, u32[]{:S(2)}, u32[]{:S(2)}) %collective-permute-start.8) | collective-permute-done | bytes 294944 | tf_op jit(solution)/shard_map/ppermute | solution.py:267
  34.0 2.6 %collective-permute-done.9.refs_3_ = bf16[128,1152]{1,0:T(8,128)(2,1)S(1)} collective-permute-done((bf16[128,1152]{1,0:T(8,128)(2,1)S(1)}, bf16[128,1152]{1,0:T(8,128)(2,1)S(1)}, u32[]{:S(2)}, u32[]{:S(2)}) %collective-permute-start.9) | collective-permute-done | bytes 294944 | tf_op jit(solution)/shard_map/ppermute | solution.py:275
  36.6 2.0 %late.1 = (bf16[128,1152]{1,0:T(8,128)(2,1)S(1)}, bf16[128,1152]{1,0:T(8,128)(2,1)S(1)}, bf16[4,384,128]{2,1,0:T(8,128)(2,1)S(1)}, bf16[4,384,128]{2,1,0:T(8,128)(2,1)S(1)}) custom-call(f32[2]{0:T(128)S(1)} %pad_maximum_fusion.1.scalars, bf16[128,1152]{1,0:T(8,128)(2,1)S(1)} %get-tuple-element.58.u, bf16[128,1152]{1,0:T(8,128)(2,1)S(1)} %get-tuple-element.59.v, ...), custom_call_target="tpu_custom_call" | custom-call | flops 1 | bytes 1 | tf_op jit(solution)/shard_map/late/pallas_call | solution.py:32
  38.7 5.3 %collective-permute-start.11 = (bf16[4,384,128]{2,1,0:T(8,128)(2,1)S(1)}, bf16[4,384,128]{2,1,0:T(8,128)(2,1)S(1)}, u32[]{:S(2)}, u32[]{:S(2)}) collective-permute-start(bf16[4,384,128]{2,1,0:T(8,128)(2,1)S(1)} %get-tuple-element.85), channel_id=1, source_target_pairs={{0,1},{1,0},{2,3},{3,2},{4,5},{5,4},{6,7},{7,6},{8,9},{9,8},{10,11... | collective-permute-start | bytes 1179656 | tf_op jit(solution)/shard_map/ppermute | solution.py:271
  44.0 1.3 %collective-permute-done.11.across = bf16[4,384,128]{2,1,0:T(8,128)(2,1)S(1)} collective-permute-done((bf16[4,384,128]{2,1,0:T(8,128)(2,1)S(1)}, bf16[4,384,128]{2,1,0:T(8,128)(2,1)S(1)}, u32[]{:S(2)}, u32[]{:S(2)}) %collective-permute-start.11) | collective-permute-done | bytes 393248 | tf_op jit(solution)/shard_map/ppermute | solution.py:271
  46.0 2.6 %collective-permute-start.13 = (bf16[2,384,128]{2,1,0:T(8,128)(2,1)S(1)}, bf16[2,384,128]{2,1,0:T(8,128)(2,1)S(1)}, u32[]{:S(2)}, u32[]{:S(2)}) collective-permute-start(bf16[2,384,128]{2,1,0:T(8,128)(2,1)S(1)} %get-tuple-element.87), channel_id=1, source_target_pairs={{0,6},{2,0},{4,2},{6,4},{1,7},{3,1},{5,3},{7,5},{8,14},{10,8},{12,... | collective-permute-start | bytes 589832 | tf_op jit(solution)/shard_map/ppermute | solution.py:275
  49.7 2.4 %feats_grad.1 = (bf16[128,1152]{1,0:T(8,128)(2,1)}, bf16[128,1152]{1,0:T(8,128)(2,1)}) custom-call(bf16[128,1152]{1,0:T(8,128)(2,1)S(1)} %get-tuple-element.93.image_dpre, bf16[128,1152]{1,0:T(8,128)(2,1)S(1)} %get-tuple-element.94.text_dpre, bf16[1152,1152]{1,0:T(8,128)(2,1)S(1)} %get-tuple-element.64.image_head, ...), custom_call_target="tpu_custom_call" | custom-call | flops 1 | bytes 1 | tf_op jit(solution)/shard_map/feats_grad/pallas_call | solution.py:32
  53.4 3.1 %collective-permute-done.13.refs_2_ = bf16[2,384,128]{2,1,0:T(8,128)(2,1)S(1)} collective-permute-done((bf16[2,384,128]{2,1,0:T(8,128)(2,1)S(1)}, bf16[2,384,128]{2,1,0:T(8,128)(2,1)S(1)}, u32[]{:S(2)}, u32[]{:S(2)}) %collective-permute-start.13) | collective-permute-done | bytes 196640 | tf_op jit(solution)/shard_map/ppermute | solution.py:275
  56.5 2.0 %collective-permute-done.14.refs_3_ = bf16[2,384,128]{2,1,0:T(8,128)(2,1)S(1)} collective-permute-done((bf16[2,384,128]{2,1,0:T(8,128)(2,1)S(1)}, bf16[2,384,128]{2,1,0:T(8,128)(2,1)S(1)}, u32[]{:S(2)}, u32[]{:S(2)}) %collective-permute-start.14) | collective-permute-done | bytes 196640 | tf_op jit(solution)/shard_map/ppermute | solution.py:275
  58.5 1.6 %head.1 = (bf16[8,81,128]{2,1,0:T(8,128)(2,1)S(1)}, bf16[8,81,128]{2,1,0:T(8,128)(2,1)S(1)}, bf16[8,81,128]{2,1,0:T(8,128)(2,1)S(1)}, bf16[8,81,128]{2,1,0:T(8,128)(2,1)S(1)}) custom-call(bf16[1152,1024]{1,0:T(8,128)(2,1)S(1)} %turn.1.feats_t, bf16[2,384,128]{2,1,0:T(8,128)(2,1)S(1)} %get-tuple-element.105.refs_0_, ...), custom_call_target="tpu_custom_call" | custom-call | flops 1 | bytes 1 | tf_op jit(solution)/shard_map/head/pallas_call | solution.py:32
  60.1 3.0 %collective-permute-start.15 = (bf16[8,81,128]{2,1,0:T(8,128)(2,1)S(1)}, bf16[8,81,128]{2,1,0:T(8,128)(2,1)S(1)}, u32[]{:S(2)}, u32[]{:S(2)}) collective-permute-start(bf16[8,81,128]{2,1,0:T(8,128)(2,1)S(1)} %get-tuple-element.110), channel_id=1, source_target_pairs={{0,8},{16,24},{8,0},{24,16},{1,9},{17,25},{9,1},{25,17},{2,10},{18... | collective-permute-start | bytes 497672 | tf_op jit(solution)/shard_map/ppermute | solution.py:281
  63.1 2.7 %collective-permute-start.17 = (bf16[8,81,128]{2,1,0:T(8,128)(2,1)S(1)}, bf16[8,81,128]{2,1,0:T(8,128)(2,1)S(1)}, u32[]{:S(2)}, u32[]{:S(2)}) collective-permute-start(bf16[8,81,128]{2,1,0:T(8,128)(2,1)S(1)} %get-tuple-element.112), channel_id=1, source_target_pairs={{0,24},{16,0},{8,16},{24,8},{1,25},{17,1},{9,17},{25,9},{2,26},{18... | collective-permute-start | bytes 497672 | tf_op jit(solution)/shard_map/ppermute | solution.py:281
  66.6 4.8 %collective-permute-done.16.refs_2_ = bf16[8,81,128]{2,1,0:T(8,128)(2,1)S(1)} collective-permute-done((bf16[8,81,128]{2,1,0:T(8,128)(2,1)S(1)}, bf16[8,81,128]{2,1,0:T(8,128)(2,1)S(1)}, u32[]{:S(2)}, u32[]{:S(2)}) %collective-permute-start.16) | collective-permute-done | bytes 165920 | tf_op jit(solution)/shard_map/ppermute | solution.py:281
  71.5 11.5 %all_to_all.5.pieces = bf16[8,81,128]{2,1,0:T(8,128)(2,1)S(1)} all-to-all(bf16[8,81,128]{2,1,0:T(8,128)(2,1)S(1)} %add_y.1), channel_id=1, replica_groups=mesh['z'=8,'ylo'=2,'yhi'=2,'x'=4,'core'=2] {'z'}, dimensions={0} | all-to-all | bytes 331776 | tf_op jit(solution)/shard_map/all_to_all | solution.py:374
  83.0 4.6 %collective-permute-start.20 = (bf16[81,128]{1,0:T(8,128)(2,1)S(1)}, bf16[81,128]{1,0:T(8,128)(2,1)S(1)}, u32[]{:S(2)}, u32[]{:S(2)}) collective-permute-start(bf16[81,128]{1,0:T(8,128)(2,1)S(1)} %add_z.1), channel_id=1, source_target_pairs={{0,9},{1,8},{2,11},{3,10},{4,13},{5,12},{6,15},{7,14},{8,1},{9,0},... | collective-permute-start | bytes 62216 | tf_op jit(solution)/shard_map/ppermute | solution.py:291
  89.1 2.7 %collective-permute-done.19 = bf16[81,128]{1,0:T(8,128)(2,1)S(1)} collective-permute-done((bf16[81,128]{1,0:T(8,128)(2,1)S(1)}, bf16[81,128]{1,0:T(8,128)(2,1)S(1)}, u32[]{:S(2)}, u32[]{:S(2)}) %collective-permute-start.19) | collective-permute-done | bytes 20768 | tf_op jit(solution)/shard_map/ppermute | solution.py:291
  91.8 1.3 %collective-permute-start.23 = (bf16[2,2,81,128]{3,2,1,0:T(8,128)(2,1)S(1)}, bf16[2,2,81,128]{3,2,1,0:T(8,128)(2,1)S(1)}, u32[]{:S(2)}, u32[]{:S(2)}) collective-permute-start(bf16[2,2,81,128]{3,2,1,0:T(8,128)(2,1)S(1)} %bitcast.13), channel_id=1, source_target_pairs={{0,6},{2,0},{4,2},{6,4},{1,7},{3,1},{5,3},{7,5},{8,14},{10,8},{12,... | collective-permute-start | bytes 248840 | tf_op jit(solution)/shard_map/ppermute | solution.py:275
  94.1 2.2 %collective-permute-done.23.refs_3_ = bf16[2,2,81,128]{3,2,1,0:T(8,128)(2,1)S(1)} collective-permute-done((bf16[2,2,81,128]{3,2,1,0:T(8,128)(2,1)S(1)}, bf16[2,2,81,128]{3,2,1,0:T(8,128)(2,1)S(1)}, u32[]{:S(2)}, u32[]{:S(2)}) %collective-permute-start.23) | collective-permute-done | bytes 82976 | tf_op jit(solution)/shard_map/ppermute | solution.py:275
  96.4 2.2 %collective-permute-done.22.refs_2_ = bf16[2,2,81,128]{3,2,1,0:T(8,128)(2,1)S(1)} collective-permute-done((bf16[2,2,81,128]{3,2,1,0:T(8,128)(2,1)S(1)}, bf16[2,2,81,128]{3,2,1,0:T(8,128)(2,1)S(1)}, u32[]{:S(2)}, u32[]{:S(2)}) %collective-permute-start.22) | collective-permute-done | bytes 82976 | tf_op jit(solution)/shard_map/ppermute | solution.py:275
  98.6 2.4 %collective-permute-done.21.refs_1_ = bf16[2,2,81,128]{3,2,1,0:T(8,128)(2,1)S(1)} collective-permute-done((bf16[2,2,81,128]{3,2,1,0:T(8,128)(2,1)S(1)}, bf16[2,2,81,128]{3,2,1,0:T(8,128)(2,1)S(1)}, u32[]{:S(2)}, u32[]{:S(2)}) %collective-permute-start.21) | collective-permute-done | bytes 82976 | tf_op jit(solution)/shard_map/ppermute | solution.py:275
  101.0 1.3 %place.1 = f32[72,2,1152]{2,1,0:T(2,128)} custom-call(bf16[2,2,81,128]{3,2,1,0:T(8,128)(2,1)S(1)} %bitcast.16, bf16[2,2,81,128]{3,2,1,0:T(8,128)(2,1)S(1)} %collective-permute-done.21.refs_1_, bf16[2,2,81,128]{3,2,1,0:T(8,128)(2,1)S(1)} %collective-permute-done.22.refs_2_, bf16[2,2,81,128]{3,2,1,0:T(8,128)(2,1)S(1)} %collective-permute-done.23.refs_3_), custom_call_target="tpu_custom_call" | custom-call | flops 1 | bytes 1 | tf_op jit(solution)/shard_map/place/pallas_call | solution.py:32
  (35 shorter events, 10.3 us)
Async XLA Ops:
  1.8 8.5 %collective-permute-start.3 = (bf16[2,128,1152]{2,1,0:T(8,128)(2,1)S(1)}, bf16[2,128,1152]{2,1,0:T(8,128)(2,1)S(1)}, u32[]{:S(2)}, u32[]{:S(2)}) collective-permute-start(bf16[2,128,1152]{2,1,0:T(8,128)(2,1)S(1)} %get-tuple-element.61.both), channel_id=1, source_target_pairs={{0,1},{1,0},{2,3},{3,2},{4,5},{5,4},{6,7},{7,6},{8,9},{9,8},{10,11... | collective-permute-start | bytes 1769480 | tf_op jit(solution)/shard_map/ppermute | solution.py:271
  5.1 12.2 %collective-permute-start = (bf16[128,1152]{1,0:T(8,128)(2,1)}, bf16[128,1152]{1,0:T(8,128)(2,1)S(1)}, u32[]{:S(2)}, u32[]{:S(2)}) collective-permute-start(bf16[128,1152]{1,0:T(8,128)(2,1)} %bitcast.image), channel_id=1, source_target_pairs={{0,224},{32,0},{64,32},{96,64},{128,96},{160,128},{192,160},{224,1... | collective-permute-start | bytes 884744 | tf_op jit(solution)/shard_map/ppermute | solution.py:255
  9.0 9.7 %collective-permute-start.1 = (bf16[128,1152]{1,0:T(8,128)(2,1)}, bf16[128,1152]{1,0:T(8,128)(2,1)S(1)}, u32[]{:S(2)}, u32[]{:S(2)}) collective-permute-start(bf16[128,1152]{1,0:T(8,128)(2,1)} %bitcast.1.text), channel_id=1, source_target_pairs={{0,32},{32,64},{64,96},{96,128},{128,160},{160,192},{192,224},{224... | collective-permute-start | bytes 884744 | tf_op jit(solution)/shard_map/ppermute | solution.py:255
  9.0 9.7 %collective-permute-start.2 = (bf16[128,1152]{1,0:T(8,128)(2,1)S(1)}, bf16[128,1152]{1,0:T(8,128)(2,1)S(1)}, u32[]{:S(2)}, u32[]{:S(2)}) collective-permute-start(bf16[128,1152]{1,0:T(8,128)(2,1)S(1)} %get-tuple-element.60), channel_id=1, source_target_pairs={{0,16},{16,0},{1,17},{17,1},{2,18},{18,2},{3,19},{19,3},{4,20},{20... | collective-permute-start | bytes 884744 | tf_op jit(solution)/shard_map/ppermute | solution.py:267
  10.3 16.9 %collective-permute-start.6 = (bf16[2,128,1152]{2,1,0:T(8,128)(2,1)S(1)}, bf16[2,128,1152]{2,1,0:T(8,128)(2,1)S(1)}, u32[]{:S(2)}, u32[]{:S(2)}) collective-permute-start(bf16[2,128,1152]{2,1,0:T(8,128)(2,1)S(1)} %pack_feats.1.refs_0_), channel_id=1, source_target_pairs={{0,6},{2,0},{4,2},{6,4},{1,7},{3,1},{5,3},{7,5},{8,14},{10,8},{12,... | collective-permute-start | bytes 1769480 | tf_op jit(solution)/shard_map/ppermute | solution.py:275
  12.9 15.1 %collective-permute-start.5 = (bf16[2,128,1152]{2,1,0:T(8,128)(2,1)S(1)}, bf16[2,128,1152]{2,1,0:T(8,128)(2,1)S(1)}, u32[]{:S(2)}, u32[]{:S(2)}) collective-permute-start(bf16[2,128,1152]{2,1,0:T(8,128)(2,1)S(1)} %pack_feats.1.refs_0_), channel_id=1, source_target_pairs={{0,2},{2,4},{4,6},{6,0},{1,3},{3,5},{5,7},{7,1},{8,10},{10,12},{12... | collective-permute-start | bytes 1769480 | tf_op jit(solution)/shard_map/ppermute | solution.py:275
  19.8 7.4 %collective-permute-start.4 = (bf16[128,1152]{1,0:T(8,128)(2,1)S(1)}, bf16[128,1152]{1,0:T(8,128)(2,1)S(1)}, u32[]{:S(2)}, u32[]{:S(2)}) collective-permute-start(bf16[128,1152]{1,0:T(8,128)(2,1)S(1)} %get-tuple-element.66.v1), channel_id=1, source_target_pairs={{0,16},{16,0},{1,17},{17,1},{2,18},{18,2},{3,19},{19,3},{4,20},{20... | collective-permute-start | bytes 884744 | tf_op jit(solution)/shard_map/ppermute | solution.py:267
  22.6 11.0 %collective-permute-start.8 = (bf16[128,1152]{1,0:T(8,128)(2,1)S(1)}, bf16[128,1152]{1,0:T(8,128)(2,1)S(1)}, u32[]{:S(2)}, u32[]{:S(2)}) collective-permute-start(bf16[128,1152]{1,0:T(8,128)(2,1)S(1)} %get-tuple-element.69.u1), channel_id=1, source_target_pairs={{0,16},{16,0},{1,17},{17,1},{2,18},{18,2},{3,19},{19,3},{4,20},{20... | collective-permute-start | bytes 884744 | tf_op jit(solution)/shard_map/ppermute | solution.py:267
  28.1 5.9 %collective-permute-start.10 = (bf16[128,1152]{1,0:T(8,128)(2,1)S(1)}, bf16[128,1152]{1,0:T(8,128)(2,1)S(1)}, u32[]{:S(2)}, u32[]{:S(2)}) collective-permute-start(bf16[128,1152]{1,0:T(8,128)(2,1)S(1)} %slice_bitcast_fusion), channel_id=1, source_target_pairs={{0,6},{2,0},{4,2},{6,4},{1,7},{3,1},{5,3},{7,5},{8,14},{10,8},{12,... | collective-permute-start | bytes 884744 | tf_op jit(solution)/shard_map/ppermute | solution.py:275
  29.9 6.8 %collective-permute-start.9 = (bf16[128,1152]{1,0:T(8,128)(2,1)S(1)}, bf16[128,1152]{1,0:T(8,128)(2,1)S(1)}, u32[]{:S(2)}, u32[]{:S(2)}) collective-permute-start(bf16[128,1152]{1,0:T(8,128)(2,1)S(1)} %slice_bitcast_fusion.1), channel_id=1, source_target_pairs={{0,2},{2,4},{4,6},{6,0},{1,3},{3,5},{5,7},{7,1},{8,10},{10,12},{12... | collective-permute-start | bytes 884744 | tf_op jit(solution)/shard_map/ppermute | solution.py:275
  29.9 6.8 %collective-permute-start.7 = (bf16[128,1152]{1,0:T(8,128)(2,1)S(1)}, bf16[128,1152]{1,0:T(8,128)(2,1)S(1)}, u32[]{:S(2)}, u32[]{:S(2)}) collective-permute-start(bf16[128,1152]{1,0:T(8,128)(2,1)S(1)} %collective-permute-done.4.u2), channel_id=1, source_target_pairs={{0,32},{16,240},{32,64},{48,16},{64,96},{80,48},{96,128},{112,80},... | collective-permute-start | bytes 884744 | tf_op jit(solution)/shard_map/ppermute | solution.py:263
  38.7 6.7 %collective-permute-start.11 = (bf16[4,384,128]{2,1,0:T(8,128)(2,1)S(1)}, bf16[4,384,128]{2,1,0:T(8,128)(2,1)S(1)}, u32[]{:S(2)}, u32[]{:S(2)}) collective-permute-start(bf16[4,384,128]{2,1,0:T(8,128)(2,1)S(1)} %get-tuple-element.85), channel_id=1, source_target_pairs={{0,1},{1,0},{2,3},{3,2},{4,5},{5,4},{6,7},{7,6},{8,9},{9,8},{10,11... | collective-permute-start | bytes 1179656 | tf_op jit(solution)/shard_map/ppermute | solution.py:271
  45.4 8.0 %collective-permute-start.12 = (bf16[2,384,128]{2,1,0:T(8,128)(2,1)S(1)}, bf16[2,384,128]{2,1,0:T(8,128)(2,1)S(1)}, u32[]{:S(2)}, u32[]{:S(2)}) collective-permute-start(bf16[2,384,128]{2,1,0:T(8,128)(2,1)S(1)} %get-tuple-element.86), channel_id=1, source_target_pairs={{0,2},{2,4},{4,6},{6,0},{1,3},{3,5},{5,7},{7,1},{8,10},{10,12},{12... | collective-permute-start | bytes 589832 | tf_op jit(solution)/shard_map/ppermute | solution.py:275
  46.0 10.6 %collective-permute-start.13 = (bf16[2,384,128]{2,1,0:T(8,128)(2,1)S(1)}, bf16[2,384,128]{2,1,0:T(8,128)(2,1)S(1)}, u32[]{:S(2)}, u32[]{:S(2)}) collective-permute-start(bf16[2,384,128]{2,1,0:T(8,128)(2,1)S(1)} %get-tuple-element.87), channel_id=1, source_target_pairs={{0,6},{2,0},{4,2},{6,4},{1,7},{3,1},{5,3},{7,5},{8,14},{10,8},{12,... | collective-permute-start | bytes 589832 | tf_op jit(solution)/shard_map/ppermute | solution.py:275
  48.6 10.0 %collective-permute-start.14 = (bf16[2,384,128]{2,1,0:T(8,128)(2,1)S(1)}, bf16[2,384,128]{2,1,0:T(8,128)(2,1)S(1)}, u32[]{:S(2)}, u32[]{:S(2)}) collective-permute-start(bf16[2,384,128]{2,1,0:T(8,128)(2,1)S(1)} %get-tuple-element.88), channel_id=1, source_target_pairs={{0,4},{2,6},{4,0},{6,2},{1,5},{3,7},{5,1},{7,3},{8,12},{10,14},{12... | collective-permute-start | bytes 589832 | tf_op jit(solution)/shard_map/ppermute | solution.py:275
  60.1 6.4 %collective-permute-start.15 = (bf16[8,81,128]{2,1,0:T(8,128)(2,1)S(1)}, bf16[8,81,128]{2,1,0:T(8,128)(2,1)S(1)}, u32[]{:S(2)}, u32[]{:S(2)}) collective-permute-start(bf16[8,81,128]{2,1,0:T(8,128)(2,1)S(1)} %get-tuple-element.110), channel_id=1, source_target_pairs={{0,8},{16,24},{8,0},{24,16},{1,9},{17,25},{9,1},{25,17},{2,10},{18... | collective-permute-start | bytes 497672 | tf_op jit(solution)/shard_map/ppermute | solution.py:281
  63.1 8.2 %collective-permute-start.16 = (bf16[8,81,128]{2,1,0:T(8,128)(2,1)S(1)}, bf16[8,81,128]{2,1,0:T(8,128)(2,1)S(1)}, u32[]{:S(2)}, u32[]{:S(2)}) collective-permute-start(bf16[8,81,128]{2,1,0:T(8,128)(2,1)S(1)} %get-tuple-element.111), channel_id=1, source_target_pairs={{0,16},{16,8},{8,24},{24,0},{1,17},{17,9},{9,25},{25,1},{2,18},{18... | collective-permute-start | bytes 497672 | tf_op jit(solution)/shard_map/ppermute | solution.py:281
  63.1 8.2 %collective-permute-start.17 = (bf16[8,81,128]{2,1,0:T(8,128)(2,1)S(1)}, bf16[8,81,128]{2,1,0:T(8,128)(2,1)S(1)}, u32[]{:S(2)}, u32[]{:S(2)}) collective-permute-start(bf16[8,81,128]{2,1,0:T(8,128)(2,1)S(1)} %get-tuple-element.112), channel_id=1, source_target_pairs={{0,24},{16,0},{8,16},{24,8},{1,25},{17,1},{9,17},{25,9},{2,26},{18... | collective-permute-start | bytes 497672 | tf_op jit(solution)/shard_map/ppermute | solution.py:281
  83.0 6.1 %collective-permute-start.20 = (bf16[81,128]{1,0:T(8,128)(2,1)S(1)}, bf16[81,128]{1,0:T(8,128)(2,1)S(1)}, u32[]{:S(2)}, u32[]{:S(2)}) collective-permute-start(bf16[81,128]{1,0:T(8,128)(2,1)S(1)} %add_z.1), channel_id=1, source_target_pairs={{0,9},{1,8},{2,11},{3,10},{4,13},{5,12},{6,15},{7,14},{8,1},{9,0},... | collective-permute-start | bytes 62216 | tf_op jit(solution)/shard_map/ppermute | solution.py:291
  87.6 4.2 %collective-permute-start.19 = (bf16[81,128]{1,0:T(8,128)(2,1)S(1)}, bf16[81,128]{1,0:T(8,128)(2,1)S(1)}, u32[]{:S(2)}, u32[]{:S(2)}) collective-permute-start(bf16[81,128]{1,0:T(8,128)(2,1)S(1)} %add_z.1), channel_id=1, source_target_pairs={{0,8},{1,9},{2,10},{3,11},{4,12},{5,13},{6,14},{7,15},{8,0},{9,1},... | collective-permute-start | bytes 62216 | tf_op jit(solution)/shard_map/ppermute | solution.py:291
  88.7 3.1 %collective-permute-start.18 = (bf16[81,128]{1,0:T(8,128)(2,1)S(1)}, bf16[81,128]{1,0:T(8,128)(2,1)S(1)}, u32[]{:S(2)}, u32[]{:S(2)}) collective-permute-start(bf16[81,128]{1,0:T(8,128)(2,1)S(1)} %add_z.1), channel_id=1, source_target_pairs={{0,1},{1,0},{2,3},{3,2},{4,5},{5,4},{6,7},{7,6},{8,9},{9,8},{10,11... | collective-permute-start | bytes 62216 | tf_op jit(solution)/shard_map/ppermute | solution.py:291
  91.8 4.6 %collective-permute-start.23 = (bf16[2,2,81,128]{3,2,1,0:T(8,128)(2,1)S(1)}, bf16[2,2,81,128]{3,2,1,0:T(8,128)(2,1)S(1)}, u32[]{:S(2)}, u32[]{:S(2)}) collective-permute-start(bf16[2,2,81,128]{3,2,1,0:T(8,128)(2,1)S(1)} %bitcast.13), channel_id=1, source_target_pairs={{0,6},{2,0},{4,2},{6,4},{1,7},{3,1},{5,3},{7,5},{8,14},{10,8},{12,... | collective-permute-start | bytes 248840 | tf_op jit(solution)/shard_map/ppermute | solution.py:275
  93.0 5.6 %collective-permute-start.22 = (bf16[2,2,81,128]{3,2,1,0:T(8,128)(2,1)S(1)}, bf16[2,2,81,128]{3,2,1,0:T(8,128)(2,1)S(1)}, u32[]{:S(2)}, u32[]{:S(2)}) collective-permute-start(bf16[2,2,81,128]{3,2,1,0:T(8,128)(2,1)S(1)} %bitcast.14), channel_id=1, source_target_pairs={{0,4},{2,6},{4,0},{6,2},{1,5},{3,7},{5,1},{7,3},{8,12},{10,14},{12... | collective-permute-start | bytes 248840 | tf_op jit(solution)/shard_map/ppermute | solution.py:275
  94.1 6.9 %collective-permute-start.21 = (bf16[2,2,81,128]{3,2,1,0:T(8,128)(2,1)S(1)}, bf16[2,2,81,128]{3,2,1,0:T(8,128)(2,1)S(1)}, u32[]{:S(2)}, u32[]{:S(2)}) collective-permute-start(bf16[2,2,81,128]{3,2,1,0:T(8,128)(2,1)S(1)} %bitcast.15), channel_id=1, source_target_pairs={{0,2},{2,4},{4,6},{6,0},{1,3},{3,5},{5,7},{7,1},{8,10},{10,12},{12... | collective-permute-start | bytes 248840 | tf_op jit(solution)/shard_map/ppermute | solution.py:275

commit v3 on v2

--- a/solution.py
+++ b/solution.py
@@ -79,19 +79,22 @@
     packed[1] = across[1]
 
 
-def project_kernel(
-    image, text, image_head_hbm, text_head_hbm,
-    emb_u, emb_v, unit_u, unit_v, norm_u, norm_v, image_head, text_head, sems,
-):
+def load_kernel(image_head_hbm, text_head_hbm, image_head, text_head, sems):
+    copies = [
+        pltpu.make_async_copy(image_head_hbm, image_head, sems.at[0]),
+        pltpu.make_async_copy(text_head_hbm, text_head, sems.at[1]),
+    ]
+    for copy in copies:
+        copy.start()
+    for copy in copies:
+        copy.wait()
+
+
+def project_kernel(both, image_head, text_head, emb_u, emb_v, unit_u, unit_v, norm_u, norm_v):
     col = lax.axis_index("ylo")
-    image_copy = pltpu.make_async_copy(image_head_hbm, image_head, sems.at[0])
-    text_copy = pltpu.make_async_copy(text_head_hbm, text_head, sems.at[1])
-    image_copy.start()
-    text_copy.start()
-    image_copy.wait()
-    image_unit, image_norm = project(image[...], image_head)
-    text_copy.wait()
-    text_unit, text_norm = project(text[...], text_head)
+    core = lax.axis_index("core")
+    image_unit, image_norm = project(pick(core, both[0], both[1]), image_head)
+    text_unit, text_norm = project(pick(core, both[1], both[0]), text_head)
     u = pick(col, text_unit, image_unit)
     v = pick(col, image_unit, text_unit)
     emb_u[...] = u.astype(BF16)
@@ -159,7 +162,7 @@
 
 def late_kernel(
     scalars, u, v, u3, v3, grad_u, grad_v, unit_u, unit_v, norm_u, norm_v,
-    image_dpre, text_dpre, mine_parts, other_parts, mine_t, other_t,
+    image_dpre, text_dpre, sent0, sent1, sent2, sent3, mine_t, other_t,
 ):
     col = lax.axis_index("ylo")
     core = lax.axis_index("core")
@@ -177,18 +180,18 @@
     text_dpre[...] = text.astype(BF16)
     mine_t[...] = pick(core, image, text).T.astype(BF16)
     other_t[...] = pick(core, text, image).T.astype(BF16)
-    for step in range(NX):
+    for step, sent in enumerate((sent0, sent1, sent2, sent3)):
         to = lax.rem(at + step, NX)
         rows = pl.ds(pl.multiple_of(to * MAIN, MAIN), MAIN)
-        for turned, parts in ((mine_t, mine_parts), (other_t, other_parts)):
-            parts[step, :MAIN, :] = turned[rows, :]
-            parts[step, MAIN:, :] = turned[TAIL_AT:, :]
-
-
-def pack_parts_kernel(mine, across, *packed):
-    for step, part in enumerate(packed):
-        part[0] = mine[step]
-        part[1] = across[step]
+        for place, turned in enumerate((mine_t, other_t)):
+            sent[place, :MAIN, :] = turned[rows, :]
+            sent[place, MAIN:, :] = turned[TAIL_AT:, :]
+
+
+def others_kernel(*refs):
+    parts, others = refs[:-1], refs[-1]
+    for step, part in enumerate(parts):
+        others[step] = part[1]
 
 
 def feats_grad_kernel(image_dpre, text_dpre, image_head, text_head, image_out, text_out):
@@ -197,13 +200,14 @@
 
 
 def head_kernel(feats_t, *refs):
-    parts, pieces, right, total, tails = refs[:NX], refs[NX:NX + NY], *refs[NX + NY:]
+    across, parts, refs = refs[0], refs[1:NX + 1], refs[NX + 1:]
+    pieces, right, total, tails = refs[:NY], *refs[NY:]
     at = lax.axis_index("x")
     y = NYLO * lax.axis_index("yhi") + lax.axis_index("ylo")
     for place, part in enumerate(parts):
-        for side in range(NCORE):
-            start = (place * NCORE + side) * ROWS
-            right[:, start:start + ROWS] = part[side]
+        start = place * NCORE * ROWS
+        right[:, start:start + ROWS] = part[0]
+        right[:, start + ROWS:start + 2 * ROWS] = across[place]
     total[...] = nt(feats_t[...], right[...])
     tails[...] = total[:, MAIN:]
     for step, piece in enumerate(pieces):
@@ -305,51 +309,45 @@
     raw_v0 = y_swap(raw_u)
     packed = call(pack_feats_kernel, "pack_feats", shape((2, ROWS, D)), (both, core_swap(both)))
     feats_1, feats_3 = x_turn(packed, 1), x_turn(packed, 3)
-    u, v, unit_u, unit_v, norm_u, norm_v, image_head, text_head = call(
-        project_kernel, "project",
-        [block, block, block32, block32, column, column, shape((D, D)), shape((D, D))],
-        (image, text, image_head, text_head),
-        in_specs=[VMEM_SPEC] * 2 + [HBM_SPEC] * 2,
-        scratch=[pltpu.SemaphoreType.DMA((2,))], mib=46,
-    )
-    image_1, text_1, raw_v0, packed = lax.optimization_barrier((image_1, text_1, raw_v0, packed))
+    image_head, text_head = call(
+        load_kernel, "load", [shape((D, D)), shape((D, D))], (image_head, text_head),
+        in_specs=[HBM_SPEC] * 2, scratch=[pltpu.SemaphoreType.DMA((2,))], mib=46,
+    )
+    image_1, text_1, packed = lax.optimization_barrier((image_1, text_1, packed))
     u1, v1 = call(
         project_came_kernel, "project_came", [block, block],
         (image_1, text_1, image_head, text_head),
     )
     u2 = y_swap(v1)
-    v3 = y_swap(u1)
-    raw_v0, u1 = lax.optimization_barrier((raw_v0, u1))
+    raw_v0, both, u1 = lax.optimization_barrier((raw_v0, both, u1))
+    u, v, unit_u, unit_v, norm_u, norm_v = call(
+        project_kernel, "project", [block, block, block32, block32, column, column],
+        (both, image_head, text_head),
+    )
     grad_u, grad_v = call(
         early_kernel, "early", [block32, block32],
         (scalars, u, v, u1, v1, raw_v0, image_head, text_head),
         in_specs=[SMEM_SPEC] + [VMEM_SPEC] * 7,
         scratch=[pltpu.VMEM((ROWS, D), BF16)],
     )
-    u2, grad_u, grad_v, feats_1, feats_3 = lax.optimization_barrier(
-        (u2, grad_u, grad_v, feats_1, feats_3)
+    u2, u1, grad_u, grad_v, feats_1, feats_3 = lax.optimization_barrier(
+        (u2, u1, grad_u, grad_v, feats_1, feats_3)
     )
     u3 = u_shift(u2)
+    v3 = y_swap(u1)
     feats_2 = (x_turn(feats_1[0], 1), x_turn(feats_3[1], 3))
     grad_v = call(
         middle_kernel, "middle", block32, (scalars, v, u2, grad_v),
         in_specs=[SMEM_SPEC] + [VMEM_SPEC] * 3,
     )
-    u3, v3, feats_2 = lax.optimization_barrier((u3, v3, feats_2))
-    parts = shape((NX, SENT, ROWS))
-    image_dpre, text_dpre, mine_parts, other_parts = call(
-        late_kernel, "late", [block, block, parts, parts],
+    sent = shape((2, SENT, ROWS))
+    image_dpre, text_dpre, *parts = call(
+        late_kernel, "late", [block, block, sent, sent, sent, sent],
         (scalars, u, v, u3, v3, grad_u, grad_v, unit_u, unit_v, norm_u, norm_v),
         in_specs=[SMEM_SPEC] + [VMEM_SPEC] * 10,
         scratch=[pltpu.VMEM((D, ROWS), BF16)] * 2,
     )
-    across = core_swap(other_parts)
-    parts = call(
-        pack_parts_kernel, "pack_parts", [shape((2, SENT, ROWS))] * NX, (mine_parts, across)
-    )
-    feats_1, feats_2, feats_3, image_dpre, text_dpre = lax.optimization_barrier(
-        (feats_1, feats_2, feats_3, image_dpre, text_dpre)
-    )
+    parts, feats_2 = lax.optimization_barrier((parts, feats_2))
     image_out, text_out = call(
         feats_grad_kernel, "feats_grad", [block, block],
         (image_dpre, text_dpre, image_head, text_head),
@@ -361,8 +359,11 @@
     came, image_out, text_out, feats_t = lax.optimization_barrier(
         (came, image_out, text_out, feats_t)
     )
+    parts = [parts[0]] + came
+    others = call(others_kernel, "others", shape((NX, SENT, ROWS)), parts)
     pieces = call(
-        head_kernel, "head", [shape((NZ, PIECE, LANES))] * NY, [feats_t, parts[0]] + came,
+        head_kernel, "head", [shape((NZ, PIECE, LANES))] * NY,
+        [feats_t, core_swap(others)] + parts,
         scratch=[
             pltpu.VMEM((SENT, NX * NCORE * ROWS), BF16),
             pltpu.VMEM((D, SENT), F32),

time: 103 us -> 98.6 us (0.957)
  waiting for transfers between devices: 31.9 us -> 26.1 us
  local copies, waits for them, and re-layouts: 0.05 us -> 2.75 us
  Pallas kernels: 19 us -> 17.7 us
    ppermute x10, waiting for transfers between devices: 16.4 us -> 10.1 us  [x_turn(): return lax.ppermute(array, 'x', [(i, (i + by) % NX) for i in range(NX)])]
    ppermute x3, starting transfers between devices: 2.88 us -> 5.6 us  [y_swap(): return lax.ppermute(array, 'ylo', [(0, 1), (1, 0)])]
    unnamed x0 -> x4, local copies, waits for them, and re-layouts: none -> 2.71 us
    ppermute x3, waiting for transfers between devices: 4.22 us -> 1.58 us  [y_swap(): return lax.ppermute(array, 'ylo', [(0, 1), (1, 0)])]
    ppermute x1, waiting for transfers between devices: 0.01 us -> 1.68 us  [u_shift(): return lax.ppermute(array, BLK, pairs)]
    ppermute x2, starting transfers between devices: 8.67 us -> 7.31 us  [core_swap(): return lax.ppermute(array, 'core', [(0, 1), (1, 0)])]
    pallas_call x14 -> x15, Pallas kernels: 19 us -> 17.7 us  [call(): pl.pallas_call(kernel, out_shape=out_shape, in_specs=in_specs or [pl.Bloc...]
  transfers between devices with their start and end apart: 24 -> 24, of which waited for: 17 -> 15; matrix products, arithmetic and copies ran while one was open for 0% -> 0% of each run, Pallas kernels for 12% -> 14%
where the time goes in v3:
time: 98.6 us; the launch traced here: 98.3 us
  starting transfers between devices  38.1 us (39%)
  waiting for transfers between devices  26.1 us (26%)
  Pallas kernels  17.7 us (18%)
  blocking collectives  11.5 us (12%)
  local copies, waits for them, and re-layouts  2.75 us (3%)
  between operations  2.09 us (2%)
    pallas_call x15, Pallas kernels, call(): pl.pallas_call(kernel, out_shape=out_shape, in_specs=in_specs or [pl.Bloc...  17.7 us
    all_to_all x1, blocking collectives, body(): pieces = lax.all_to_all(pieces, 'z', 0, 0, tiled=True)  11.5 us
    ppermute x10, waiting for transfers between devices, x_turn(): return lax.ppermute(array, 'x', [(i, (i + by) % NX) for i in range(NX)])  10.1 us
    ppermute x10, starting transfers between devices, x_turn(): return lax.ppermute(array, 'x', [(i, (i + by) % NX) for i in range(NX)])  10.1 us
    ppermute x2, starting transfers between devices, core_swap(): return lax.ppermute(array, 'core', [(0, 1), (1, 0)])  7.31 us
    ppermute x3, waiting for transfers between devices, y_turn(): return lax.ppermute(array, ('ylo', 'yhi'), pairs)  6.47 us
    ppermute x3, starting transfers between devices, half_swap(): return lax.ppermute(array, REP, pairs)  5.84 us
    ppermute x3, starting transfers between devices, y_swap(): return lax.ppermute(array, 'ylo', [(0, 1), (1, 0)])  5.6 us
  transfers between devices with their start and end apart: 24, of which 15 were waited for; matrix products, arithmetic and copies ran while one was open for 0% of the time, Pallas kernels for 14%

profile of v3, /device:TPU:1, one launch (start us, length us, event | category | flops | bytes accessed | tf_op | source)
XLA Modules:
  0.0 98.3 jit_solution(9188134127748949154)
XLA Ops:
  2.6 3.3 %collective-permute-start.3 = (bf16[2,128,1152]{2,1,0:T(8,128)(2,1)S(1)}, bf16[2,128,1152]{2,1,0:T(8,128)(2,1)S(1)}, u32[]{:S(2)}, u32[]{:S(2)}) collective-permute-start(bf16[2,128,1152]{2,1,0:T(8,128)(2,1)S(1)} %get-tuple-element.60.both), channel_id=1, source_target_pairs={{0,1},{1,0},{2,3},{3,2},{4,5},{5,4},{6,7},{7,6},{8,9},{9,8},{10,11... | collective-permute-start | bytes 1769480 | tf_op jit(solution)/shard_map/ppermute | solution.py:275
  6.0 3.9 %collective-permute-start.1 = (bf16[128,1152]{1,0:T(8,128)(2,1)}, bf16[128,1152]{1,0:T(8,128)(2,1)S(1)}, u32[]{:S(2)}, u32[]{:S(2)}) collective-permute-start(bf16[128,1152]{1,0:T(8,128)(2,1)} %bitcast.17), channel_id=1, source_target_pairs={{0,224},{32,0},{64,32},{96,64},{128,96},{160,128},{192,160},{224,1... | collective-permute-start | bytes 884744 | tf_op jit(solution)/shard_map/ppermute | solution.py:259
  11.2 1.5 %collective-permute-start.6 = (bf16[2,128,1152]{2,1,0:T(8,128)(2,1)S(1)}, bf16[2,128,1152]{2,1,0:T(8,128)(2,1)S(1)}, u32[]{:S(2)}, u32[]{:S(2)}) collective-permute-start(bf16[2,128,1152]{2,1,0:T(8,128)(2,1)S(1)} %pack_feats.1.refs_0_), channel_id=1, source_target_pairs={{0,6},{2,0},{4,2},{6,4},{1,7},{3,1},{5,3},{7,5},{8,14},{10,8},{12,... | collective-permute-start | bytes 1769480 | tf_op jit(solution)/shard_map/ppermute | solution.py:279
  13.9 1.7 %copy-done = bf16[1152,1152]{1,0:T(8,128)(2,1)S(1)} copy-done((bf16[1152,1152]{1,0:T(8,128)(2,1)S(1)}, bf16[1152,1152]{1,0:T(8,128)(2,1)}, u32[]{:S(2)}) %copy-start) | copy-done | bytes 2654232
  15.7 2.0 %load.1 = (bf16[1152,1152]{1,0:T(8,128)(2,1)S(1)}, bf16[1152,1152]{1,0:T(8,128)(2,1)S(1)}) custom-call(bf16[1152,1152]{1,0:T(8,128)(2,1)S(1)} %copy-done, bf16[1152,1152]{1,0:T(8,128)(2,1)} %text_head_hbm.1), custom_call_target="tpu_custom_call" | custom-call | flops 1 | bytes 1 | tf_op jit(solution)/shard_map/load/pallas_call | solution.py:32
  17.7 1.8 %collective-permute-done.2.text = bf16[128,1152]{1,0:T(8,128)(2,1)S(1)} collective-permute-done((bf16[128,1152]{1,0:T(8,128)(2,1)}, bf16[128,1152]{1,0:T(8,128)(2,1)S(1)}, u32[]{:S(2)}, u32[]{:S(2)}) %collective-permute-start.2) | collective-permute-done | bytes 294944 | tf_op jit(solution)/shard_map/ppermute | solution.py:259
  20.7 1.4 %collective-permute-start.4 = (bf16[128,1152]{1,0:T(8,128)(2,1)S(1)}, bf16[128,1152]{1,0:T(8,128)(2,1)S(1)}, u32[]{:S(2)}, u32[]{:S(2)}) collective-permute-start(bf16[128,1152]{1,0:T(8,128)(2,1)S(1)} %get-tuple-element.63.v1), channel_id=1, source_target_pairs={{0,16},{16,0},{1,17},{17,1},{2,18},{18,2},{3,19},{19,3},{4,20},{20... | collective-permute-start | bytes 884744 | tf_op jit(solution)/shard_map/ppermute | solution.py:271
  24.7 2.9 %early.1 = (f32[128,1152]{1,0:T(8,128)S(1)}, f32[128,1152]{1,0:T(8,128)S(1)}) custom-call(f32[2]{0:T(128)S(1)} %pad_maximum_fusion.1.scalars, bf16[128,1152]{1,0:T(8,128)(2,1)S(1)} %get-tuple-element.61.u, bf16[128,1152]{1,0:T(8,128)(2,1)S(1)} %get-tuple-element.62.v, bf16[128,1152]{1,0:T(8,128)(2,1)S(1)} %get-tuple-element.69.u1, ...), custom_call_target="tpu_custom_call" | custom-call | flops 1 | bytes 1 | tf_op jit(solution)/shard_map/early/pallas_call | solution.py:32
  28.1 2.9 %collective-permute-start.8 = (bf16[128,1152]{1,0:T(8,128)(2,1)S(1)}, bf16[128,1152]{1,0:T(8,128)(2,1)S(1)}, u32[]{:S(2)}, u32[]{:S(2)}) collective-permute-start(bf16[128,1152]{1,0:T(8,128)(2,1)S(1)} %get-tuple-element.69.u1), channel_id=1, source_target_pairs={{0,16},{16,0},{1,17},{17,1},{2,18},{18,2},{3,19},{19,3},{4,20},{20... | collective-permute-start | bytes 884744 | tf_op jit(solution)/shard_map/ppermute | solution.py:271
  31.1 1.6 %collective-permute-start.10 = (bf16[128,1152]{1,0:T(8,128)(2,1)S(1)}, bf16[128,1152]{1,0:T(8,128)(2,1)S(1)}, u32[]{:S(2)}, u32[]{:S(2)}) collective-permute-start(bf16[128,1152]{1,0:T(8,128)(2,1)S(1)} %slice_bitcast_fusion), channel_id=1, source_target_pairs={{0,6},{2,0},{4,2},{6,4},{1,7},{3,1},{5,3},{7,5},{8,14},{10,8},{12,... | collective-permute-start | bytes 884744 | tf_op jit(solution)/shard_map/ppermute | solution.py:279
  34.0 1.7 %collective-permute-done.7.u3 = bf16[128,1152]{1,0:T(8,128)(2,1)S(1)} collective-permute-done((bf16[128,1152]{1,0:T(8,128)(2,1)S(1)}, bf16[128,1152]{1,0:T(8,128)(2,1)S(1)}, u32[]{:S(2)}, u32[]{:S(2)}) %collective-permute-start.7) | collective-permute-done | bytes 294944 | tf_op jit(solution)/shard_map/ppermute | solution.py:267
  36.8 2.0 %late.1 = (bf16[128,1152]{1,0:T(8,128)(2,1)S(1)}, bf16[128,1152]{1,0:T(8,128)(2,1)S(1)}, bf16[2,384,128]{2,1,0:T(8,128)(2,1)S(1)}, bf16[2,384,128]{2,1,0:T(8,128...) custom-call(f32[2]{0:T(128)S(1)} %pad_maximum_fusion.1.scalars, ...), custom_call_target="tpu_custom_call" | custom-call | flops 1 | bytes 1 | tf_op jit(solution)/shard_map/late/pallas_call | solution.py:32
  40.1 2.7 %collective-permute-start.12 = (bf16[2,384,128]{2,1,0:T(8,128)(2,1)S(1)}, bf16[2,384,128]{2,1,0:T(8,128)(2,1)S(1)}, u32[]{:S(2)}, u32[]{:S(2)}) collective-permute-start(bf16[2,384,128]{2,1,0:T(8,128)(2,1)S(1)} %get-tuple-element.83), channel_id=1, source_target_pairs={{0,6},{2,0},{4,2},{6,4},{1,7},{3,1},{5,3},{7,5},{8,14},{10,8},{12,... | collective-permute-start | bytes 589832 | tf_op jit(solution)/shard_map/ppermute | solution.py:279
  42.7 2.4 %feats_grad.1 = (bf16[128,1152]{1,0:T(8,128)(2,1)}, bf16[128,1152]{1,0:T(8,128)(2,1)}) custom-call(bf16[128,1152]{1,0:T(8,128)(2,1)S(1)} %get-tuple-element.85.image_dpre, bf16[128,1152]{1,0:T(8,128)(2,1)S(1)} %get-tuple-element.86.text_dpre, bf16[1152,1152]{1,0:T(8,128)(2,1)S(1)} %get-tuple-element.57.image_head, ...), custom_call_target="tpu_custom_call" | custom-call | flops 1 | bytes 1 | tf_op jit(solution)/shard_map/feats_grad/pallas_call | solution.py:32
  45.9 1.6 %collective-permute-done.12.refs_2_.refs_3_ = bf16[2,384,128]{2,1,0:T(8,128)(2,1)S(1)} collective-permute-done((bf16[2,384,128]{2,1,0:T(8,128)(2,1)S(1)}, bf16[2,384,128]{2,1,0:T(8,128)(2,1)S(1)}, u32[]{:S(2)}, u32[]{:S(2)}) %collective-permute-start.12) | collective-permute-done | bytes 196640 | tf_op jit(solution)/shard_map/ppermute | solution.py:279
  47.5 2.8 %collective-permute-done.13.refs_3_.refs_4_ = bf16[2,384,128]{2,1,0:T(8,128)(2,1)S(1)} collective-permute-done((bf16[2,384,128]{2,1,0:T(8,128)(2,1)S(1)}, bf16[2,384,128]{2,1,0:T(8,128)(2,1)S(1)}, u32[]{:S(2)}, u32[]{:S(2)}) %collective-permute-start.13) | collective-permute-done | bytes 196640 | tf_op jit(solution)/shard_map/ppermute | solution.py:279
  50.3 4.0 %collective-permute-start.14 = (bf16[4,384,128]{2,1,0:T(8,128)(2,1)S(1)}, bf16[4,384,128]{2,1,0:T(8,128)(2,1)S(1)}, u32[]{:S(2)}, u32[]{:S(2)}) collective-permute-start(bf16[4,384,128]{2,1,0:T(8,128)(2,1)S(1)} %others.1), channel_id=1, source_target_pairs={{0,1},{1,0},{2,3},{3,2},{4,5},{5,4},{6,7},{7,6},{8,9},{9,8},{10,11... | collective-permute-start | bytes 1179656 | tf_op jit(solution)/shard_map/ppermute | solution.py:275
  54.3 1.3 %collective-permute-done.14.refs_0_ = bf16[4,384,128]{2,1,0:T(8,128)(2,1)S(1)} collective-permute-done((bf16[4,384,128]{2,1,0:T(8,128)(2,1)S(1)}, bf16[4,384,128]{2,1,0:T(8,128)(2,1)S(1)}, u32[]{:S(2)}, u32[]{:S(2)}) %collective-permute-start.14) | collective-permute-done | bytes 393248 | tf_op jit(solution)/shard_map/ppermute | solution.py:275
  55.6 1.6 %head.1 = (bf16[8,81,128]{2,1,0:T(8,128)(2,1)S(1)}, bf16[8,81,128]{2,1,0:T(8,128)(2,1)S(1)}, bf16[8,81,128]{2,1,0:T(8,128)(2,1)S(1)}, bf16[8,81,128]{2,1,0:T(8,128)(2,1)S(1)}) custom-call(bf16[1152,1024]{1,0:T(8,128)(2,1)S(1)} %turn.1.feats_t, bf16[4,384,128]{2,1,0:T(8,128)(2,1)S(1)} %collective-permute-done.14.refs_0_, ...), custom_call_target="tpu_custom_call" | custom-call | flops 1 | bytes 1 | tf_op jit(solution)/shard_map/head/pallas_call | solution.py:32
  57.2 2.7 %collective-permute-start.15 = (bf16[8,81,128]{2,1,0:T(8,128)(2,1)S(1)}, bf16[8,81,128]{2,1,0:T(8,128)(2,1)S(1)}, u32[]{:S(2)}, u32[]{:S(2)}) collective-permute-start(bf16[8,81,128]{2,1,0:T(8,128)(2,1)S(1)} %get-tuple-element.100), channel_id=1, source_target_pairs={{0,8},{16,24},{8,0},{24,16},{1,9},{17,25},{9,1},{25,17},{2,10},{18... | collective-permute-start | bytes 497672 | tf_op jit(solution)/shard_map/ppermute | solution.py:285
  59.9 2.7 %collective-permute-start.17 = (bf16[8,81,128]{2,1,0:T(8,128)(2,1)S(1)}, bf16[8,81,128]{2,1,0:T(8,128)(2,1)S(1)}, u32[]{:S(2)}, u32[]{:S(2)}) collective-permute-start(bf16[8,81,128]{2,1,0:T(8,128)(2,1)S(1)} %get-tuple-element.102), channel_id=1, source_target_pairs={{0,24},{16,0},{8,16},{24,8},{1,25},{17,1},{9,17},{25,9},{2,26},{18... | collective-permute-start | bytes 497672 | tf_op jit(solution)/shard_map/ppermute | solution.py:285
  62.6 2.0 %collective-permute-done.15.refs_1_ = bf16[8,81,128]{2,1,0:T(8,128)(2,1)S(1)} collective-permute-done((bf16[8,81,128]{2,1,0:T(8,128)(2,1)S(1)}, bf16[8,81,128]{2,1,0:T(8,128)(2,1)S(1)}, u32[]{:S(2)}, u32[]{:S(2)}) %collective-permute-start.15) | collective-permute-done | bytes 165920 | tf_op jit(solution)/shard_map/ppermute | solution.py:285
  64.6 4.5 %collective-permute-done.16.refs_2_ = bf16[8,81,128]{2,1,0:T(8,128)(2,1)S(1)} collective-permute-done((bf16[8,81,128]{2,1,0:T(8,128)(2,1)S(1)}, bf16[8,81,128]{2,1,0:T(8,128)(2,1)S(1)}, u32[]{:S(2)}, u32[]{:S(2)}) %collective-permute-start.16) | collective-permute-done | bytes 165920 | tf_op jit(solution)/shard_map/ppermute | solution.py:285
  69.2 11.5 %all_to_all.5.pieces = bf16[8,81,128]{2,1,0:T(8,128)(2,1)S(1)} all-to-all(bf16[8,81,128]{2,1,0:T(8,128)(2,1)S(1)} %add_y.1), channel_id=1, replica_groups=mesh['z'=8,'ylo'=2,'yhi'=2,'x'=4,'core'=2] {'z'}, dimensions={0} | all-to-all | bytes 331776 | tf_op jit(solution)/shard_map/all_to_all | solution.py:375
  80.7 2.6 %collective-permute-start.18 = (bf16[81,128]{1,0:T(8,128)(2,1)S(1)}, bf16[81,128]{1,0:T(8,128)(2,1)S(1)}, u32[]{:S(2)}, u32[]{:S(2)}) collective-permute-start(bf16[81,128]{1,0:T(8,128)(2,1)S(1)} %add_z.1), channel_id=1, source_target_pairs={{0,1},{1,0},{2,3},{3,2},{4,5},{5,4},{6,7},{7,6},{8,9},{9,8},{10,11... | collective-permute-start | bytes 62216 | tf_op jit(solution)/shard_map/ppermute | solution.py:295
  83.3 1.6 %collective-permute-start.19 = (bf16[81,128]{1,0:T(8,128)(2,1)S(1)}, bf16[81,128]{1,0:T(8,128)(2,1)S(1)}, u32[]{:S(2)}, u32[]{:S(2)}) collective-permute-start(bf16[81,128]{1,0:T(8,128)(2,1)S(1)} %add_z.1), channel_id=1, source_target_pairs={{0,8},{1,9},{2,10},{3,11},{4,12},{5,13},{6,14},{7,15},{8,0},{9,1},... | collective-permute-start | bytes 62216 | tf_op jit(solution)/shard_map/ppermute | solution.py:295
  84.9 1.6 %collective-permute-start.20 = (bf16[81,128]{1,0:T(8,128)(2,1)S(1)}, bf16[81,128]{1,0:T(8,128)(2,1)S(1)}, u32[]{:S(2)}, u32[]{:S(2)}) collective-permute-start(bf16[81,128]{1,0:T(8,128)(2,1)S(1)} %add_z.1), channel_id=1, source_target_pairs={{0,9},{1,8},{2,11},{3,10},{4,13},{5,12},{6,15},{7,14},{8,1},{9,0},... | collective-permute-start | bytes 62216 | tf_op jit(solution)/shard_map/ppermute | solution.py:295
  87.5 2.2 %collective-permute-done.20 = bf16[81,128]{1,0:T(8,128)(2,1)S(1)} collective-permute-done((bf16[81,128]{1,0:T(8,128)(2,1)S(1)}, bf16[81,128]{1,0:T(8,128)(2,1)S(1)}, u32[]{:S(2)}, u32[]{:S(2)}) %collective-permute-start.20) | collective-permute-done | bytes 20768 | tf_op jit(solution)/shard_map/ppermute | solution.py:295
  89.7 2.7 %collective-permute-start.22 = (bf16[2,2,81,128]{3,2,1,0:T(8,128)(2,1)S(1)}, bf16[2,2,81,128]{3,2,1,0:T(8,128)(2,1)S(1)}, u32[]{:S(2)}, u32[]{:S(2)}) collective-permute-start(bf16[2,2,81,128]{3,2,1,0:T(8,128)(2,1)S(1)} %bitcast.14), channel_id=1, source_target_pairs={{0,4},{2,6},{4,0},{6,2},{1,5},{3,7},{5,1},{7,3},{8,12},{10,14},{12... | collective-permute-start | bytes 248840 | tf_op jit(solution)/shard_map/ppermute | solution.py:279
  92.4 2.3 %collective-permute-done.21.refs_1_ = bf16[2,2,81,128]{3,2,1,0:T(8,128)(2,1)S(1)} collective-permute-done((bf16[2,2,81,128]{3,2,1,0:T(8,128)(2,1)S(1)}, bf16[2,2,81,128]{3,2,1,0:T(8,128)(2,1)S(1)}, u32[]{:S(2)}, u32[]{:S(2)}) %collective-permute-start.21) | collective-permute-done | bytes 82976 | tf_op jit(solution)/shard_map/ppermute | solution.py:279
  94.8 2.0 %collective-permute-done.22.refs_2_ = bf16[2,2,81,128]{3,2,1,0:T(8,128)(2,1)S(1)} collective-permute-done((bf16[2,2,81,128]{3,2,1,0:T(8,128)(2,1)S(1)}, bf16[2,2,81,128]{3,2,1,0:T(8,128)(2,1)S(1)}, u32[]{:S(2)}, u32[]{:S(2)}) %collective-permute-start.22) | collective-permute-done | bytes 82976 | tf_op jit(solution)/shard_map/ppermute | solution.py:279
  96.9 1.3 %place.1 = f32[72,2,1152]{2,1,0:T(2,128)} custom-call(bf16[2,2,81,128]{3,2,1,0:T(8,128)(2,1)S(1)} %bitcast.16, bf16[2,2,81,128]{3,2,1,0:T(8,128)(2,1)S(1)} %collective-permute-done.21.refs_1_, bf16[2,2,81,128]{3,2,1,0:T(8,128)(2,1)S(1)} %collective-permute-done.22.refs_2_, bf16[2,2,81,128]{3,2,1,0:T(8,128)(2,1)S(1)} %collective-permute-done.23.refs_3_), custom_call_target="tpu_custom_call" | custom-call | flops 1 | bytes 1 | tf_op jit(solution)/shard_map/place/pallas_call | solution.py:32
  (40 shorter events, 13.6 us)
Async XLA Ops:
  0.6 1.0 copy-start.1
  2.6 7.2 %collective-permute-start.3 = (bf16[2,128,1152]{2,1,0:T(8,128)(2,1)S(1)}, bf16[2,128,1152]{2,1,0:T(8,128)(2,1)S(1)}, u32[]{:S(2)}, u32[]{:S(2)}) collective-permute-start(bf16[2,128,1152]{2,1,0:T(8,128)(2,1)S(1)} %get-tuple-element.60.both), channel_id=1, source_target_pairs={{0,1},{1,0},{2,3},{3,2},{4,5},{5,4},{6,7},{7,6},{8,9},{9,8},{10,11... | collective-permute-start | bytes 1769480 | tf_op jit(solution)/shard_map/ppermute | solution.py:275
  6.0 11.7 %collective-permute-start.1 = (bf16[128,1152]{1,0:T(8,128)(2,1)}, bf16[128,1152]{1,0:T(8,128)(2,1)S(1)}, u32[]{:S(2)}, u32[]{:S(2)}) collective-permute-start(bf16[128,1152]{1,0:T(8,128)(2,1)} %bitcast.17), channel_id=1, source_target_pairs={{0,224},{32,0},{64,32},{96,64},{128,96},{160,128},{192,160},{224,1... | collective-permute-start | bytes 884744 | tf_op jit(solution)/shard_map/ppermute | solution.py:259
  9.8 9.7 %collective-permute-start.2 = (bf16[128,1152]{1,0:T(8,128)(2,1)}, bf16[128,1152]{1,0:T(8,128)(2,1)S(1)}, u32[]{:S(2)}, u32[]{:S(2)}) collective-permute-start(bf16[128,1152]{1,0:T(8,128)(2,1)} %bitcast.1.text), channel_id=1, source_target_pairs={{0,32},{32,64},{64,96},{96,128},{128,160},{160,192},{192,224},{224... | collective-permute-start | bytes 884744 | tf_op jit(solution)/shard_map/ppermute | solution.py:259
  9.9 18.2 %collective-permute-start.5 = (bf16[2,128,1152]{2,1,0:T(8,128)(2,1)S(1)}, bf16[2,128,1152]{2,1,0:T(8,128)(2,1)S(1)}, u32[]{:S(2)}, u32[]{:S(2)}) collective-permute-start(bf16[2,128,1152]{2,1,0:T(8,128)(2,1)S(1)} %pack_feats.1.refs_0_), channel_id=1, source_target_pairs={{0,2},{2,4},{4,6},{6,0},{1,3},{3,5},{5,7},{7,1},{8,10},{10,12},{12... | collective-permute-start | bytes 1769480 | tf_op jit(solution)/shard_map/ppermute | solution.py:279
  11.2 16.9 %collective-permute-start.6 = (bf16[2,128,1152]{2,1,0:T(8,128)(2,1)S(1)}, bf16[2,128,1152]{2,1,0:T(8,128)(2,1)S(1)}, u32[]{:S(2)}, u32[]{:S(2)}) collective-permute-start(bf16[2,128,1152]{2,1,0:T(8,128)(2,1)S(1)} %pack_feats.1.refs_0_), channel_id=1, source_target_pairs={{0,6},{2,0},{4,2},{6,4},{1,7},{3,1},{5,3},{7,5},{8,14},{10,8},{12,... | collective-permute-start | bytes 1769480 | tf_op jit(solution)/shard_map/ppermute | solution.py:279
  12.6 10.8 %collective-permute-start = (bf16[128,1152]{1,0:T(8,128)(2,1)S(1)}, bf16[128,1152]{1,0:T(8,128)(2,1)S(1)}, u32[]{:S(2)}, u32[]{:S(2)}) collective-permute-start(bf16[128,1152]{1,0:T(8,128)(2,1)S(1)} %get-tuple-element.53), channel_id=1, source_target_pairs={{0,16},{16,0},{1,17},{17,1},{2,18},{18,2},{3,19},{19,3},{4,20},{20... | collective-permute-start | bytes 884744 | tf_op jit(solution)/shard_map/ppermute | solution.py:271
  13.9 1.7 %copy-start = (bf16[1152,1152]{1,0:T(8,128)(2,1)S(1)}, bf16[1152,1152]{1,0:T(8,128)(2,1)}, u32[]{:S(2)}) copy-start(bf16[1152,1152]{1,0:T(8,128)(2,1)} %image_head_hbm.1) | copy-start | bytes 7962628
  20.7 7.4 %collective-permute-start.4 = (bf16[128,1152]{1,0:T(8,128)(2,1)S(1)}, bf16[128,1152]{1,0:T(8,128)(2,1)S(1)}, u32[]{:S(2)}, u32[]{:S(2)}) collective-permute-start(bf16[128,1152]{1,0:T(8,128)(2,1)S(1)} %get-tuple-element.63.v1), channel_id=1, source_target_pairs={{0,16},{16,0},{1,17},{17,1},{2,18},{18,2},{3,19},{19,3},{4,20},{20... | collective-permute-start | bytes 884744 | tf_op jit(solution)/shard_map/ppermute | solution.py:271
  28.1 7.6 %collective-permute-start.7 = (bf16[128,1152]{1,0:T(8,128)(2,1)S(1)}, bf16[128,1152]{1,0:T(8,128)(2,1)S(1)}, u32[]{:S(2)}, u32[]{:S(2)}) collective-permute-start(bf16[128,1152]{1,0:T(8,128)(2,1)S(1)} %collective-permute-done.4.u2), channel_id=1, source_target_pairs={{0,32},{16,240},{32,64},{48,16},{64,96},{80,48},{96,128},{112,80},... | collective-permute-start | bytes 884744 | tf_op jit(solution)/shard_map/ppermute | solution.py:267
  28.1 8.7 %collective-permute-start.8 = (bf16[128,1152]{1,0:T(8,128)(2,1)S(1)}, bf16[128,1152]{1,0:T(8,128)(2,1)S(1)}, u32[]{:S(2)}, u32[]{:S(2)}) collective-permute-start(bf16[128,1152]{1,0:T(8,128)(2,1)S(1)} %get-tuple-element.69.u1), channel_id=1, source_target_pairs={{0,16},{16,0},{1,17},{17,1},{2,18},{18,2},{3,19},{19,3},{4,20},{20... | collective-permute-start | bytes 884744 | tf_op jit(solution)/shard_map/ppermute | solution.py:271
  31.1 7.7 %collective-permute-start.10 = (bf16[128,1152]{1,0:T(8,128)(2,1)S(1)}, bf16[128,1152]{1,0:T(8,128)(2,1)S(1)}, u32[]{:S(2)}, u32[]{:S(2)}) collective-permute-start(bf16[128,1152]{1,0:T(8,128)(2,1)S(1)} %slice_bitcast_fusion), channel_id=1, source_target_pairs={{0,6},{2,0},{4,2},{6,4},{1,7},{3,1},{5,3},{7,5},{8,14},{10,8},{12,... | collective-permute-start | bytes 884744 | tf_op jit(solution)/shard_map/ppermute | solution.py:279
  32.7 7.4 %collective-permute-start.9 = (bf16[128,1152]{1,0:T(8,128)(2,1)S(1)}, bf16[128,1152]{1,0:T(8,128)(2,1)S(1)}, u32[]{:S(2)}, u32[]{:S(2)}) collective-permute-start(bf16[128,1152]{1,0:T(8,128)(2,1)S(1)} %slice_bitcast_fusion.1), channel_id=1, source_target_pairs={{0,2},{2,4},{4,6},{6,0},{1,3},{3,5},{5,7},{7,1},{8,10},{10,12},{12... | collective-permute-start | bytes 884744 | tf_op jit(solution)/shard_map/ppermute | solution.py:279
  40.1 5.8 %collective-permute-start.11 = (bf16[2,384,128]{2,1,0:T(8,128)(2,1)S(1)}, bf16[2,384,128]{2,1,0:T(8,128)(2,1)S(1)}, u32[]{:S(2)}, u32[]{:S(2)}) collective-permute-start(bf16[2,384,128]{2,1,0:T(8,128)(2,1)S(1)} %get-tuple-element.82), channel_id=1, source_target_pairs={{0,2},{2,4},{4,6},{6,0},{1,3},{3,5},{5,7},{7,1},{8,10},{10,12},{12... | collective-permute-start | bytes 589832 | tf_op jit(solution)/shard_map/ppermute | solution.py:279
  40.1 7.4 %collective-permute-start.12 = (bf16[2,384,128]{2,1,0:T(8,128)(2,1)S(1)}, bf16[2,384,128]{2,1,0:T(8,128)(2,1)S(1)}, u32[]{:S(2)}, u32[]{:S(2)}) collective-permute-start(bf16[2,384,128]{2,1,0:T(8,128)(2,1)S(1)} %get-tuple-element.83), channel_id=1, source_target_pairs={{0,6},{2,0},{4,2},{6,4},{1,7},{3,1},{5,3},{7,5},{8,14},{10,8},{12,... | collective-permute-start | bytes 589832 | tf_op jit(solution)/shard_map/ppermute | solution.py:279
  42.7 7.5 %collective-permute-start.13 = (bf16[2,384,128]{2,1,0:T(8,128)(2,1)S(1)}, bf16[2,384,128]{2,1,0:T(8,128)(2,1)S(1)}, u32[]{:S(2)}, u32[]{:S(2)}) collective-permute-start(bf16[2,384,128]{2,1,0:T(8,128)(2,1)S(1)} %get-tuple-element.84), channel_id=1, source_target_pairs={{0,4},{2,6},{4,0},{6,2},{1,5},{3,7},{5,1},{7,3},{8,12},{10,14},{12... | collective-permute-start | bytes 589832 | tf_op jit(solution)/shard_map/ppermute | solution.py:279
  50.3 5.3 %collective-permute-start.14 = (bf16[4,384,128]{2,1,0:T(8,128)(2,1)S(1)}, bf16[4,384,128]{2,1,0:T(8,128)(2,1)S(1)}, u32[]{:S(2)}, u32[]{:S(2)}) collective-permute-start(bf16[4,384,128]{2,1,0:T(8,128)(2,1)S(1)} %others.1), channel_id=1, source_target_pairs={{0,1},{1,0},{2,3},{3,2},{4,5},{5,4},{6,7},{7,6},{8,9},{9,8},{10,11... | collective-permute-start | bytes 1179656 | tf_op jit(solution)/shard_map/ppermute | solution.py:275
  57.2 7.4 %collective-permute-start.15 = (bf16[8,81,128]{2,1,0:T(8,128)(2,1)S(1)}, bf16[8,81,128]{2,1,0:T(8,128)(2,1)S(1)}, u32[]{:S(2)}, u32[]{:S(2)}) collective-permute-start(bf16[8,81,128]{2,1,0:T(8,128)(2,1)S(1)} %get-tuple-element.100), channel_id=1, source_target_pairs={{0,8},{16,24},{8,0},{24,16},{1,9},{17,25},{9,1},{25,17},{2,10},{18... | collective-permute-start | bytes 497672 | tf_op jit(solution)/shard_map/ppermute | solution.py:285
  59.9 9.1 %collective-permute-start.16 = (bf16[8,81,128]{2,1,0:T(8,128)(2,1)S(1)}, bf16[8,81,128]{2,1,0:T(8,128)(2,1)S(1)}, u32[]{:S(2)}, u32[]{:S(2)}) collective-permute-start(bf16[8,81,128]{2,1,0:T(8,128)(2,1)S(1)} %get-tuple-element.101), channel_id=1, source_target_pairs={{0,16},{16,8},{8,24},{24,0},{1,17},{17,9},{9,25},{25,1},{2,18},{18... | collective-permute-start | bytes 497672 | tf_op jit(solution)/shard_map/ppermute | solution.py:285
  59.9 9.1 %collective-permute-start.17 = (bf16[8,81,128]{2,1,0:T(8,128)(2,1)S(1)}, bf16[8,81,128]{2,1,0:T(8,128)(2,1)S(1)}, u32[]{:S(2)}, u32[]{:S(2)}) collective-permute-start(bf16[8,81,128]{2,1,0:T(8,128)(2,1)S(1)} %get-tuple-element.102), channel_id=1, source_target_pairs={{0,24},{16,0},{8,16},{24,8},{1,25},{17,1},{9,17},{25,9},{2,26},{18... | collective-permute-start | bytes 497672 | tf_op jit(solution)/shard_map/ppermute | solution.py:285
  80.7 5.8 %collective-permute-start.18 = (bf16[81,128]{1,0:T(8,128)(2,1)S(1)}, bf16[81,128]{1,0:T(8,128)(2,1)S(1)}, u32[]{:S(2)}, u32[]{:S(2)}) collective-permute-start(bf16[81,128]{1,0:T(8,128)(2,1)S(1)} %add_z.1), channel_id=1, source_target_pairs={{0,1},{1,0},{2,3},{3,2},{4,5},{5,4},{6,7},{7,6},{8,9},{9,8},{10,11... | collective-permute-start | bytes 62216 | tf_op jit(solution)/shard_map/ppermute | solution.py:295
  83.3 4.2 %collective-permute-start.19 = (bf16[81,128]{1,0:T(8,128)(2,1)S(1)}, bf16[81,128]{1,0:T(8,128)(2,1)S(1)}, u32[]{:S(2)}, u32[]{:S(2)}) collective-permute-start(bf16[81,128]{1,0:T(8,128)(2,1)S(1)} %add_z.1), channel_id=1, source_target_pairs={{0,8},{1,9},{2,10},{3,11},{4,12},{5,13},{6,14},{7,15},{8,0},{9,1},... | collective-permute-start | bytes 62216 | tf_op jit(solution)/shard_map/ppermute | solution.py:295
  84.9 4.7 %collective-permute-start.20 = (bf16[81,128]{1,0:T(8,128)(2,1)S(1)}, bf16[81,128]{1,0:T(8,128)(2,1)S(1)}, u32[]{:S(2)}, u32[]{:S(2)}) collective-permute-start(bf16[81,128]{1,0:T(8,128)(2,1)S(1)} %add_z.1), channel_id=1, source_target_pairs={{0,9},{1,8},{2,11},{3,10},{4,13},{5,12},{6,15},{7,14},{8,1},{9,0},... | collective-permute-start | bytes 62216 | tf_op jit(solution)/shard_map/ppermute | solution.py:295
  89.6 5.1 %collective-permute-start.21 = (bf16[2,2,81,128]{3,2,1,0:T(8,128)(2,1)S(1)}, bf16[2,2,81,128]{3,2,1,0:T(8,128)(2,1)S(1)}, u32[]{:S(2)}, u32[]{:S(2)}) collective-permute-start(bf16[2,2,81,128]{3,2,1,0:T(8,128)(2,1)S(1)} %bitcast.13), channel_id=1, source_target_pairs={{0,2},{2,4},{4,6},{6,0},{1,3},{3,5},{5,7},{7,1},{8,10},{10,12},{12... | collective-permute-start | bytes 248840 | tf_op jit(solution)/shard_map/ppermute | solution.py:279
  89.7 7.0 %collective-permute-start.22 = (bf16[2,2,81,128]{3,2,1,0:T(8,128)(2,1)S(1)}, bf16[2,2,81,128]{3,2,1,0:T(8,128)(2,1)S(1)}, u32[]{:S(2)}, u32[]{:S(2)}) collective-permute-start(bf16[2,2,81,128]{3,2,1,0:T(8,128)(2,1)S(1)} %bitcast.14), channel_id=1, source_target_pairs={{0,4},{2,6},{4,0},{6,2},{1,5},{3,7},{5,1},{7,3},{8,12},{10,14},{12... | collective-permute-start | bytes 248840 | tf_op jit(solution)/shard_map/ppermute | solution.py:279
  92.4 4.5 %collective-permute-start.23 = (bf16[2,2,81,128]{3,2,1,0:T(8,128)(2,1)S(1)}, bf16[2,2,81,128]{3,2,1,0:T(8,128)(2,1)S(1)}, u32[]{:S(2)}, u32[]{:S(2)}) collective-permute-start(bf16[2,2,81,128]{3,2,1,0:T(8,128)(2,1)S(1)} %bitcast.15), channel_id=1, source_target_pairs={{0,6},{2,0},{4,2},{6,4},{1,7},{3,1},{5,3},{7,5},{8,14},{10,8},{12,... | collective-permute-start | bytes 248840 | tf_op jit(solution)/shard_map/ppermute | solution.py:279

commit v4 on v3

--- a/solution.py
+++ b/solution.py
@@ -114,11 +114,12 @@
 
 
 def turn_kernel(*refs):
-    parts, turned = refs[:-1], refs[-1]
+    parts, turned = refs[:-2], refs[-2:]
     blocks = [part[side] for part in parts[:-2] for side in range(NCORE)]
     blocks += [part[...] for part in parts[-2:]]
     for place, rows in enumerate(blocks):
-        turned[:, place * ROWS:(place + 1) * ROWS] = rows.astype(F32).T.astype(BF16)
+        step, side = divmod(place, NCORE)
+        turned[side][:, step * ROWS:(step + 1) * ROWS] = rows.astype(F32).T.astype(BF16)
 
 
 def pair_weights(own, other, scalars, same):
@@ -199,16 +200,20 @@
     text_out[...] = nt(text_dpre[...], text_head[...]).astype(BF16)
 
 
-def head_kernel(feats_t, *refs):
-    across, parts, refs = refs[0], refs[1:NX + 1], refs[NX + 1:]
+def own_head_kernel(feats_t, *refs):
+    parts, total, right = refs[:NX], refs[NX], refs[NX + 1]
+    for place, part in enumerate(parts):
+        right[:, place * ROWS:(place + 1) * ROWS] = part[0]
+    total[...] = nt(feats_t[...], right[...])
+
+
+def head_kernel(feats_t, across, own, *refs):
     pieces, right, total, tails = refs[:NY], *refs[NY:]
     at = lax.axis_index("x")
     y = NYLO * lax.axis_index("yhi") + lax.axis_index("ylo")
-    for place, part in enumerate(parts):
-        start = place * NCORE * ROWS
-        right[:, start:start + ROWS] = part[0]
-        right[:, start + ROWS:start + 2 * ROWS] = across[place]
-    total[...] = nt(feats_t[...], right[...])
+    for place in range(NX):
+        right[:, place * ROWS:(place + 1) * ROWS] = across[place]
+    total[...] = own[...] + nt(feats_t[...], right[...])
     tails[...] = total[:, MAIN:]
     for step, piece in enumerate(pieces):
         to = lax.rem(y + step, NY)
@@ -239,20 +244,21 @@
     out[...] = total.astype(BF16)
 
 
-def place_kernel(*refs):
-    parts, out = refs[:-1], refs[-1]
+def place_kernel(mine, other, out):
     core = lax.axis_index("core")
     at = lax.axis_index("x")
     half_at = lax.axis_index("yhi")
-    for step, part in enumerate(parts):
+    for step in range(NX):
         came_x = lax.rem(at + NX - step, NX)
         for flip in range(NYHI):
             index = NYHI * came_x + lax.rem(half_at + flip, NYHI)
-            mine = part[flip, 0].astype(F32)
-            other = part[flip, 1].astype(F32)
-            both = jnp.stack([pick(core, mine, other), pick(core, other, mine)], axis=1)
-            out[:, :, pl.ds(pl.multiple_of(index * LANES, LANES), LANES)] = both[:PER_BLK]
-            out[pl.ds(index * TAIL_ROWS, TAIL_ROWS), :, TAIL_AT:] = both[PER_BLK:PER_BLK + TAIL_ROWS]
+            own = mine[step, flip].astype(F32)
+            across = other[step, flip].astype(F32)
+            lanes = pl.ds(pl.multiple_of(index * LANES, LANES), LANES)
+            rows = pl.ds(index * TAIL_ROWS, TAIL_ROWS)
+            for head, part in enumerate((pick(core, own, across), pick(core, across, own))):
+                out[:, head, lanes] = part[:PER_BLK]
+                out[rows, head, TAIL_AT:] = part[PER_BLK:]
 
 
 def z_shift(array, by):
@@ -285,14 +291,8 @@
     return lax.ppermute(array, ("ylo", "yhi"), pairs)
 
 
-def half_swap(array, flip, swap):
-    pairs = []
-    for half in range(NYHI):
-        for x in range(NX):
-            for core in range(NCORE):
-                start = (half * NX + x) * NCORE + core
-                pairs.append((start, ((half ^ flip) * NX + x) * NCORE + (core ^ swap)))
-    return lax.ppermute(array, REP, pairs)
+def half_swap(array):
+    return lax.ppermute(array, "yhi", [(0, 1), (1, 0)])
 
 
 def body(image_feats, text_feats, image_head, text_head, log_scale, bias):
@@ -347,25 +347,29 @@
         in_specs=[SMEM_SPEC] + [VMEM_SPEC] * 10,
         scratch=[pltpu.VMEM((D, ROWS), BF16)] * 2,
     )
-    parts, feats_2 = lax.optimization_barrier((parts, feats_2))
+    image_dpre, text_dpre, feats_2 = lax.optimization_barrier((image_dpre, text_dpre, feats_2))
     image_out, text_out = call(
         feats_grad_kernel, "feats_grad", [block, block],
         (image_dpre, text_dpre, image_head, text_head),
     )
-    feats_t = call(
-        turn_kernel, "turn", shape((D, NX * NCORE * ROWS)), (packed, feats_1, feats_3, *feats_2)
+    feats_own, feats_across = call(
+        turn_kernel, "turn", [shape((D, NX * ROWS))] * 2, (packed, feats_1, feats_3, *feats_2)
     )
     came = [x_turn(parts[1], 1), x_turn(parts[3], 3), x_turn(parts[2], 2)]
-    came, image_out, text_out, feats_t = lax.optimization_barrier(
-        (came, image_out, text_out, feats_t)
+    came, image_out, text_out, feats_own, feats_across = lax.optimization_barrier(
+        (came, image_out, text_out, feats_own, feats_across)
     )
     parts = [parts[0]] + came
     others = call(others_kernel, "others", shape((NX, SENT, ROWS)), parts)
+    across = core_swap(others)
+    own_head = call(
+        own_head_kernel, "own_head", shape((D, SENT), F32), [feats_own] + parts,
+        scratch=[pltpu.VMEM((SENT, NX * ROWS), BF16)],
+    )
     pieces = call(
-        head_kernel, "head", [shape((NZ, PIECE, LANES))] * NY,
-        [feats_t, core_swap(others)] + parts,
+        head_kernel, "head", [shape((NZ, PIECE, LANES))] * NY, (feats_across, across, own_head),
         scratch=[
-            pltpu.VMEM((SENT, NX * NCORE * ROWS), BF16),
+            pltpu.VMEM((SENT, NX * ROWS), BF16),
             pltpu.VMEM((D, SENT), F32),
             pltpu.VMEM((D, LANES), F32),
         ],
@@ -374,9 +378,9 @@
     pieces = call(add_kernel, "add_y", shape((NZ, PIECE, LANES)), pieces)
     pieces = lax.all_to_all(pieces, "z", 0, 0, tiled=True)
     mine = call(add_z_kernel, "add_z", shape((PIECE, LANES)), (pieces,))
-    four = jnp.stack([mine] + [half_swap(mine, flip, swap) for flip, swap in ((0, 1), (1, 0), (1, 1))])
-    four = four.reshape(NYHI, NCORE, PIECE, LANES)
-    places = [four] + [x_turn(four, by) for by in (1, 2, 3)]
+    two = jnp.stack([mine, half_swap(mine)])
+    eight = jnp.stack([two] + [x_turn(two, by) for by in range(1, NX)])
+    places = (eight, core_swap(eight))
     head_grads = call(place_kernel, "place", shape((PER_BLK, 2, D), F32), places)
     return (image_out[None], text_out[None], head_grads)
 

time: 98.6 us -> 96.2 us (0.976)
  waiting for transfers between devices: 26.1 us -> 22.7 us
  starting transfers between devices: 38.1 us -> 40 us
    ppermute x2 -> x3, starting transfers between devices: 7.31 us -> 13.1 us  [core_swap(): return lax.ppermute(array, 'core', [(0, 1), (1, 0)])]
    ppermute x3 -> x1, starting transfers between devices: 5.84 us -> 1.28 us  [half_swap(): return lax.ppermute(array, 'yhi', [(0, 1), (1, 0)])]
    ppermute x10, waiting for transfers between devices: 10.1 us -> 8.26 us  [x_turn(): return lax.ppermute(array, 'x', [(i, (i + by) % NX) for i in range(NX)])]
    ppermute x1, waiting for transfers between devices: 1.68 us -> 0.52 us  [u_shift(): return lax.ppermute(array, BLK, pairs)]
    unnamed x4 -> x2, local copies, waits for them, and re-layouts: 2.71 us -> 1.75 us
    pallas_call x15 -> x16, Pallas kernels: 17.7 us -> 17.9 us  [call(): pl.pallas_call(kernel, out_shape=out_shape, in_specs=in_specs or [pl.Bloc...]
    ppermute x3 -> x1, waiting for transfers between devices: 3.09 us -> 2.97 us  [half_swap(): return lax.ppermute(array, 'yhi', [(0, 1), (1, 0)])]
  transfers between devices with their start and end apart: 24 -> 23, of which waited for: 15 -> 13; matrix products, arithmetic and copies ran while one was open for 0% -> 0% of each run, Pallas kernels for 14% -> 15%
where the time goes in v4:
time: 96.2 us; the launch traced here: 96 us
  starting transfers between devices  40 us (42%)
  waiting for transfers between devices  22.7 us (24%)
  Pallas kernels  17.9 us (19%)
  blocking collectives  11.3 us (12%)
  between operations  2.06 us (2%)
  local copies, waits for them, and re-layouts  1.8 us (2%)
    pallas_call x16, Pallas kernels, call(): pl.pallas_call(kernel, out_shape=out_shape, in_specs=in_specs or [pl.Bloc...  17.9 us
    ppermute x3, starting transfers between devices, core_swap(): return lax.ppermute(array, 'core', [(0, 1), (1, 0)])  13.1 us
    all_to_all x1, blocking collectives, body(): pieces = lax.all_to_all(pieces, 'z', 0, 0, tiled=True)  11.3 us
    ppermute x10, starting transfers between devices, x_turn(): return lax.ppermute(array, 'x', [(i, (i + by) % NX) for i in range(NX)])  10.5 us
    ppermute x10, waiting for transfers between devices, x_turn(): return lax.ppermute(array, 'x', [(i, (i + by) % NX) for i in range(NX)])  8.26 us
    ppermute x3, waiting for transfers between devices, y_turn(): return lax.ppermute(array, ('ylo', 'yhi'), pairs)  6.01 us
    ppermute x3, starting transfers between devices, y_turn(): return lax.ppermute(array, ('ylo', 'yhi'), pairs)  5.68 us
    ppermute x3, starting transfers between devices, y_swap(): return lax.ppermute(array, 'ylo', [(0, 1), (1, 0)])  5.6 us
  transfers between devices with their start and end apart: 23, of which 13 were waited for; matrix products, arithmetic and copies ran while one was open for 0% of the time, Pallas kernels for 15%

profile of v4, /device:TPU:1, one launch (start us, length us, event | category | flops | bytes accessed | tf_op | source)
XLA Modules:
  0.0 96.0 jit_solution(15152596540636837704)
XLA Ops:
  0.6 1.1 %choose.1 = (bf16[2,128,1152]{2,1,0:T(8,128)(2,1)S(1)}, bf16[128,1152]{1,0:T(8,128)(2,1)S(1)}) custom-call(bf16[128,1152]{1,0:T(8,128)(2,1)} %bitcast.image, bf16[128,1152]{1,0:T(8,128)(2,1)} %bitcast.1.text), custom_call_target="tpu_custom_call" | custom-call | flops 1 | bytes 1 | tf_op jit(solution)/shard_map/choose/pallas_call | solution.py:32
  1.8 3.3 %collective-permute-start.3 = (bf16[2,128,1152]{2,1,0:T(8,128)(2,1)S(1)}, bf16[2,128,1152]{2,1,0:T(8,128)(2,1)S(1)}, u32[]{:S(2)}, u32[]{:S(2)}) collective-permute-start(bf16[2,128,1152]{2,1,0:T(8,128)(2,1)S(1)} %get-tuple-element.61.both), channel_id=1, source_target_pairs={{0,1},{1,0},{2,3},{3,2},{4,5},{5,4},{6,7},{7,6},{8,9},{9,8},{10,11... | collective-permute-start | bytes 1769480 | tf_op jit(solution)/shard_map/ppermute | solution.py:281
  5.1 3.9 %collective-permute-start.1 = (bf16[128,1152]{1,0:T(8,128)(2,1)}, bf16[128,1152]{1,0:T(8,128)(2,1)S(1)}, u32[]{:S(2)}, u32[]{:S(2)}) collective-permute-start(bf16[128,1152]{1,0:T(8,128)(2,1)} %bitcast.image), channel_id=1, source_target_pairs={{0,224},{32,0},{64,32},{96,64},{128,96},{160,128},{192,160},{224,1... | collective-permute-start | bytes 884744 | tf_op jit(solution)/shard_map/ppermute | solution.py:265
  9.0 1.3 %collective-permute-start.5 = (bf16[2,128,1152]{2,1,0:T(8,128)(2,1)S(1)}, bf16[2,128,1152]{2,1,0:T(8,128)(2,1)S(1)}, u32[]{:S(2)}, u32[]{:S(2)}) collective-permute-start(bf16[2,128,1152]{2,1,0:T(8,128)(2,1)S(1)} %pack_feats.1.refs_0_), channel_id=1, source_target_pairs={{0,2},{2,4},{4,6},{6,0},{1,3},{3,5},{5,7},{7,1},{8,10},{10,12},{12... | collective-permute-start | bytes 1769480 | tf_op jit(solution)/shard_map/ppermute | solution.py:285
  10.3 1.5 %collective-permute-start.6 = (bf16[2,128,1152]{2,1,0:T(8,128)(2,1)S(1)}, bf16[2,128,1152]{2,1,0:T(8,128)(2,1)S(1)}, u32[]{:S(2)}, u32[]{:S(2)}) collective-permute-start(bf16[2,128,1152]{2,1,0:T(8,128)(2,1)S(1)} %pack_feats.1.refs_0_), channel_id=1, source_target_pairs={{0,6},{2,0},{4,2},{6,4},{1,7},{3,1},{5,3},{7,5},{8,14},{10,8},{12,... | collective-permute-start | bytes 1769480 | tf_op jit(solution)/shard_map/ppermute | solution.py:285
  11.8 1.3 %collective-permute-start = (bf16[128,1152]{1,0:T(8,128)(2,1)S(1)}, bf16[128,1152]{1,0:T(8,128)(2,1)S(1)}, u32[]{:S(2)}, u32[]{:S(2)}) collective-permute-start(bf16[128,1152]{1,0:T(8,128)(2,1)S(1)} %get-tuple-element.54), channel_id=1, source_target_pairs={{0,16},{16,0},{1,17},{17,1},{2,18},{18,2},{3,19},{19,3},{4,20},{20... | collective-permute-start | bytes 884744 | tf_op jit(solution)/shard_map/ppermute | solution.py:277
  13.1 1.7 %copy-done = bf16[1152,1152]{1,0:T(8,128)(2,1)S(1)} copy-done((bf16[1152,1152]{1,0:T(8,128)(2,1)S(1)}, bf16[1152,1152]{1,0:T(8,128)(2,1)}, u32[]{:S(2)}) %copy-start) | copy-done | bytes 2654232
  14.8 2.0 %load.1 = (bf16[1152,1152]{1,0:T(8,128)(2,1)S(1)}, bf16[1152,1152]{1,0:T(8,128)(2,1)S(1)}) custom-call(bf16[1152,1152]{1,0:T(8,128)(2,1)S(1)} %copy-done, bf16[1152,1152]{1,0:T(8,128)(2,1)} %text_head_hbm.1), custom_call_target="tpu_custom_call" | custom-call | flops 1 | bytes 1 | tf_op jit(solution)/shard_map/load/pallas_call | solution.py:32
  16.8 1.8 %collective-permute-done.2.text = bf16[128,1152]{1,0:T(8,128)(2,1)S(1)} collective-permute-done((bf16[128,1152]{1,0:T(8,128)(2,1)}, bf16[128,1152]{1,0:T(8,128)(2,1)S(1)}, u32[]{:S(2)}, u32[]{:S(2)}) %collective-permute-start.2) | collective-permute-done | bytes 294944 | tf_op jit(solution)/shard_map/ppermute | solution.py:265
  18.6 1.2 %project_came.1 = (bf16[128,1152]{1,0:T(8,128)(2,1)S(1)}, bf16[128,1152]{1,0:T(8,128)(2,1)S(1)}) custom-call(bf16[128,1152]{1,0:T(8,128)(2,1)S(1)} %collective-permute-done.1.image, bf16[128,1152]{1,0:T(8,128)(2,1)S(1)} %collective-permute-done.2.text, bf16[1152,1152]{1,0:T(8,128)(2,1)S(1)} %get-tuple-element.58.image_head, ...), custom_call_target="tpu_custom_call" | custom-call | flops 1 | bytes 1 | tf_op jit(solution)/shard_map/project_came/pallas_call | solution.py:32
  19.8 1.4 %collective-permute-start.4 = (bf16[128,1152]{1,0:T(8,128)(2,1)S(1)}, bf16[128,1152]{1,0:T(8,128)(2,1)S(1)}, u32[]{:S(2)}, u32[]{:S(2)}) collective-permute-start(bf16[128,1152]{1,0:T(8,128)(2,1)S(1)} %get-tuple-element.64.v1), channel_id=1, source_target_pairs={{0,16},{16,0},{1,17},{17,1},{2,18},{18,2},{3,19},{19,3},{4,20},{20... | collective-permute-start | bytes 884744 | tf_op jit(solution)/shard_map/ppermute | solution.py:277
  22.6 1.3 %project.1 = (bf16[128,1152]{1,0:T(8,128)(2,1)S(1)}, bf16[128,1152]{1,0:T(8,128)(2,1)S(1)}, f32[128,1152]{1,0:T(8,128)S(1)}, f32[128,1152]{1,0:T(8,128)S(1)}, f3...) custom-call(bf16[2,128,1152]{2,1,0:T(8,128)(2,1)S(1)} %get-tuple-element.61.both, ...), custom_call_target="tpu_custom_call" | custom-call | flops 1 | bytes 1 | tf_op jit(solution)/shard_map/project/pallas_call | solution.py:32
  23.9 2.9 %early.1 = (f32[128,1152]{1,0:T(8,128)S(1)}, f32[128,1152]{1,0:T(8,128)S(1)}) custom-call(f32[2]{0:T(128)S(1)} %pad_maximum_fusion.2.scalars, bf16[128,1152]{1,0:T(8,128)(2,1)S(1)} %get-tuple-element.62.u, bf16[128,1152]{1,0:T(8,128)(2,1)S(1)} %get-tuple-element.63.v, bf16[128,1152]{1,0:T(8,128)(2,1)S(1)} %get-tuple-element.70.u1, ...), custom_call_target="tpu_custom_call" | custom-call | flops 1 | bytes 1 | tf_op jit(solution)/shard_map/early/pallas_call | solution.py:32
  27.3 2.9 %collective-permute-start.8 = (bf16[128,1152]{1,0:T(8,128)(2,1)S(1)}, bf16[128,1152]{1,0:T(8,128)(2,1)S(1)}, u32[]{:S(2)}, u32[]{:S(2)}) collective-permute-start(bf16[128,1152]{1,0:T(8,128)(2,1)S(1)} %get-tuple-element.70.u1), channel_id=1, source_target_pairs={{0,16},{16,0},{1,17},{17,1},{2,18},{18,2},{3,19},{19,3},{4,20},{20... | collective-permute-start | bytes 884744 | tf_op jit(solution)/shard_map/ppermute | solution.py:277
  30.5 2.7 %collective-permute-start.13 = (bf16[128,1152]{1,0:T(8,128)(2,1)S(1)}, bf16[128,1152]{1,0:T(8,128)(2,1)S(1)}, u32[]{:S(2)}, u32[]{:S(2)}) collective-permute-start(bf16[128,1152]{1,0:T(8,128)(2,1)S(1)} %slice_bitcast_fusion), channel_id=1, source_target_pairs={{0,6},{2,0},{4,2},{6,4},{1,7},{3,1},{5,3},{7,5},{8,14},{10,8},{12,... | collective-permute-start | bytes 884744 | tf_op jit(solution)/shard_map/ppermute | solution.py:285
  35.9 2.0 %late.1 = (bf16[128,1152]{1,0:T(8,128)(2,1)S(1)}, bf16[128,1152]{1,0:T(8,128)(2,1)S(1)}, bf16[2,384,128]{2,1,0:T(8,128)(2,1)S(1)}, bf16[2,384,128]{2,1,0:T(8,128...) custom-call(f32[2]{0:T(128)S(1)} %pad_maximum_fusion.2.scalars, ...), custom_call_target="tpu_custom_call" | custom-call | flops 1 | bytes 1 | tf_op jit(solution)/shard_map/late/pallas_call | solution.py:32
  37.9 1.5 %collective-permute-start.10 = (bf16[2,384,128]{2,1,0:T(8,128)(2,1)S(1)}, bf16[2,384,128]{2,1,0:T(8,128)(2,1)S(1)}, u32[]{:S(2)}, u32[]{:S(2)}) collective-permute-start(bf16[2,384,128]{2,1,0:T(8,128)(2,1)S(1)} %get-tuple-element.78), channel_id=1, source_target_pairs={{0,6},{2,0},{4,2},{6,4},{1,7},{3,1},{5,3},{7,5},{8,14},{10,8},{12,... | collective-permute-start | bytes 589832 | tf_op jit(solution)/shard_map/ppermute | solution.py:285
  40.6 2.4 %feats_grad.1 = (bf16[128,1152]{1,0:T(8,128)(2,1)}, bf16[128,1152]{1,0:T(8,128)(2,1)}) custom-call(bf16[128,1152]{1,0:T(8,128)(2,1)S(1)} %get-tuple-element.84.image_dpre, bf16[128,1152]{1,0:T(8,128)(2,1)S(1)} %get-tuple-element.85.text_dpre, bf16[1152,1152]{1,0:T(8,128)(2,1)S(1)} %get-tuple-element.58.image_head, ...), custom_call_target="tpu_custom_call" | custom-call | flops 1 | bytes 1 | tf_op jit(solution)/shard_map/feats_grad/pallas_call | solution.py:32
  43.7 1.9 %collective-permute-done.11.refs_3_ = bf16[2,384,128]{2,1,0:T(8,128)(2,1)S(1)} collective-permute-done((bf16[2,384,128]{2,1,0:T(8,128)(2,1)S(1)}, bf16[2,384,128]{2,1,0:T(8,128)(2,1)S(1)}, u32[]{:S(2)}, u32[]{:S(2)}) %collective-permute-start.11) | collective-permute-done | bytes 196640 | tf_op jit(solution)/shard_map/ppermute | solution.py:285
  45.6 2.8 %collective-permute-done.9.refs_1_ = bf16[2,384,128]{2,1,0:T(8,128)(2,1)S(1)} collective-permute-done((bf16[2,384,128]{2,1,0:T(8,128)(2,1)S(1)}, bf16[2,384,128]{2,1,0:T(8,128)(2,1)S(1)}, u32[]{:S(2)}, u32[]{:S(2)}) %collective-permute-start.9) | collective-permute-done | bytes 196640 | tf_op jit(solution)/shard_map/ppermute | solution.py:285
  48.4 4.2 %collective-permute-start.14 = (bf16[4,384,128]{2,1,0:T(8,128)(2,1)S(1)}, bf16[4,384,128]{2,1,0:T(8,128)(2,1)S(1)}, u32[]{:S(2)}, u32[]{:S(2)}) collective-permute-start(bf16[4,384,128]{2,1,0:T(8,128)(2,1)S(1)} %others.1), channel_id=1, source_target_pairs={{0,1},{1,0},{2,3},{3,2},{4,5},{5,4},{6,7},{7,6},{8,9},{9,8},{10,11... | collective-permute-start | bytes 1179656 | tf_op jit(solution)/shard_map/ppermute | solution.py:281
  54.9 3.0 %collective-permute-start.15 = (bf16[8,81,128]{2,1,0:T(8,128)(2,1)S(1)}, bf16[8,81,128]{2,1,0:T(8,128)(2,1)S(1)}, u32[]{:S(2)}, u32[]{:S(2)}) collective-permute-start(bf16[8,81,128]{2,1,0:T(8,128)(2,1)S(1)} %get-tuple-element.102), channel_id=1, source_target_pairs={{0,8},{16,24},{8,0},{24,16},{1,9},{17,25},{9,1},{25,17},{2,10},{18... | collective-permute-start | bytes 497672 | tf_op jit(solution)/shard_map/ppermute | solution.py:291
  57.9 2.7 %collective-permute-start.17 = (bf16[8,81,128]{2,1,0:T(8,128)(2,1)S(1)}, bf16[8,81,128]{2,1,0:T(8,128)(2,1)S(1)}, u32[]{:S(2)}, u32[]{:S(2)}) collective-permute-start(bf16[8,81,128]{2,1,0:T(8,128)(2,1)S(1)} %get-tuple-element.104), channel_id=1, source_target_pairs={{0,24},{16,0},{8,16},{24,8},{1,25},{17,1},{9,17},{25,9},{2,26},{18... | collective-permute-start | bytes 497672 | tf_op jit(solution)/shard_map/ppermute | solution.py:291
  60.5 1.7 %collective-permute-done.15.refs_1_ = bf16[8,81,128]{2,1,0:T(8,128)(2,1)S(1)} collective-permute-done((bf16[8,81,128]{2,1,0:T(8,128)(2,1)S(1)}, bf16[8,81,128]{2,1,0:T(8,128)(2,1)S(1)}, u32[]{:S(2)}, u32[]{:S(2)}) %collective-permute-start.15) | collective-permute-done | bytes 165920 | tf_op jit(solution)/shard_map/ppermute | solution.py:291
  62.2 4.3 %collective-permute-done.16.refs_2_ = bf16[8,81,128]{2,1,0:T(8,128)(2,1)S(1)} collective-permute-done((bf16[8,81,128]{2,1,0:T(8,128)(2,1)S(1)}, bf16[8,81,128]{2,1,0:T(8,128)(2,1)S(1)}, u32[]{:S(2)}, u32[]{:S(2)}) %collective-permute-start.16) | collective-permute-done | bytes 165920 | tf_op jit(solution)/shard_map/ppermute | solution.py:291
  66.6 11.3 %all_to_all.5.pieces = bf16[8,81,128]{2,1,0:T(8,128)(2,1)S(1)} all-to-all(bf16[8,81,128]{2,1,0:T(8,128)(2,1)S(1)} %add_y.1), channel_id=1, replica_groups=mesh['z'=8,'ylo'=2,'yhi'=2,'x'=4,'core'=2] {'z'}, dimensions={0} | all-to-all | bytes 331776 | tf_op jit(solution)/shard_map/all_to_all | solution.py:379
  78.0 1.3 %collective-permute-start.18 = (bf16[81,128]{1,0:T(8,128)(2,1)S(1)}, bf16[81,128]{1,0:T(8,128)(2,1)S(1)}, u32[]{:S(2)}, u32[]{:S(2)}) collective-permute-start(bf16[81,128]{1,0:T(8,128)(2,1)S(1)} %add_z.1), channel_id=1, source_target_pairs={{0,8},{8,0},{1,9},{9,1},{2,10},{10,2},{3,11},{11,3},{4,12},{12,4},... | collective-permute-start | bytes 62216 | tf_op jit(solution)/shard_map/ppermute | solution.py:295
  79.3 3.0 %collective-permute-done.18 = bf16[81,128]{1,0:T(8,128)(2,1)S(1)} collective-permute-done((bf16[81,128]{1,0:T(8,128)(2,1)S(1)}, bf16[81,128]{1,0:T(8,128)(2,1)S(1)}, u32[]{:S(2)}, u32[]{:S(2)}) %collective-permute-start.18) | collective-permute-done | bytes 20768 | tf_op jit(solution)/shard_map/ppermute | solution.py:295
  84.4 2.4 %collective-permute-done.20 = bf16[2,81,128]{2,1,0:T(8,128)(2,1)S(1)} collective-permute-done((bf16[2,81,128]{2,1,0:T(8,128)(2,1)S(1)}, bf16[2,81,128]{2,1,0:T(8,128)(2,1)S(1)}, u32[]{:S(2)}, u32[]{:S(2)}) %collective-permute-start.20) | collective-permute-done | bytes 41504 | tf_op jit(solution)/shard_map/ppermute | solution.py:285
  86.7 1.2 %collective-permute-done.19 = bf16[2,81,128]{2,1,0:T(8,128)(2,1)S(1)} collective-permute-done((bf16[2,81,128]{2,1,0:T(8,128)(2,1)S(1)}, bf16[2,81,128]{2,1,0:T(8,128)(2,1)S(1)}, u32[]{:S(2)}, u32[]{:S(2)}) %collective-permute-start.19) | collective-permute-done | bytes 41504 | tf_op jit(solution)/shard_map/ppermute | solution.py:285
  87.9 5.6 %collective-permute-start.22 = (bf16[4,2,81,128]{3,2,1,0:T(8,128)(2,1)S(1)}, bf16[4,2,81,128]{3,2,1,0:T(8,128)(2,1)S(1)}, u32[]{:S(2)}, u32[]{:S(2)}) collective-permute-start(bf16[4,2,81,128]{3,2,1,0:T(8,128)(2,1)S(1)} %pad_maximum_fusion.mine), channel_id=1, source_target_pairs={{0,1},{1,0},{2,3},{3,2},{4,5},{5,4},{6,7},{7,6},{8,9},{9,8},{10,11... | collective-permute-start | bytes 497672 | tf_op jit(solution)/shard_map/ppermute | solution.py:281
  94.6 1.4 %place.1 = f32[72,2,1152]{2,1,0:T(2,128)} custom-call(bf16[4,2,81,128]{3,2,1,0:T(8,128)(2,1)S(1)} %pad_maximum_fusion.mine, bf16[4,2,81,128]{3,2,1,0:T(8,128)(2,1)S(1)} %collective-permute-done.22.other), custom_call_target="tpu_custom_call" | custom-call | flops 1 | bytes 1 | tf_op jit(solution)/shard_map/place/pallas_call | solution.py:32
  (38 shorter events, 11.1 us)
Async XLA Ops:
  1.8 7.2 %collective-permute-start.3 = (bf16[2,128,1152]{2,1,0:T(8,128)(2,1)S(1)}, bf16[2,128,1152]{2,1,0:T(8,128)(2,1)S(1)}, u32[]{:S(2)}, u32[]{:S(2)}) collective-permute-start(bf16[2,128,1152]{2,1,0:T(8,128)(2,1)S(1)} %get-tuple-element.61.both), channel_id=1, source_target_pairs={{0,1},{1,0},{2,3},{3,2},{4,5},{5,4},{6,7},{7,6},{8,9},{9,8},{10,11... | collective-permute-start | bytes 1769480 | tf_op jit(solution)/shard_map/ppermute | solution.py:281
  5.1 11.7 %collective-permute-start.1 = (bf16[128,1152]{1,0:T(8,128)(2,1)}, bf16[128,1152]{1,0:T(8,128)(2,1)S(1)}, u32[]{:S(2)}, u32[]{:S(2)}) collective-permute-start(bf16[128,1152]{1,0:T(8,128)(2,1)} %bitcast.image), channel_id=1, source_target_pairs={{0,224},{32,0},{64,32},{96,64},{128,96},{160,128},{192,160},{224,1... | collective-permute-start | bytes 884744 | tf_op jit(solution)/shard_map/ppermute | solution.py:265
  9.0 9.7 %collective-permute-start.2 = (bf16[128,1152]{1,0:T(8,128)(2,1)}, bf16[128,1152]{1,0:T(8,128)(2,1)S(1)}, u32[]{:S(2)}, u32[]{:S(2)}) collective-permute-start(bf16[128,1152]{1,0:T(8,128)(2,1)} %bitcast.1.text), channel_id=1, source_target_pairs={{0,32},{32,64},{64,96},{96,128},{128,160},{160,192},{192,224},{224... | collective-permute-start | bytes 884744 | tf_op jit(solution)/shard_map/ppermute | solution.py:265
  9.0 18.2 %collective-permute-start.5 = (bf16[2,128,1152]{2,1,0:T(8,128)(2,1)S(1)}, bf16[2,128,1152]{2,1,0:T(8,128)(2,1)S(1)}, u32[]{:S(2)}, u32[]{:S(2)}) collective-permute-start(bf16[2,128,1152]{2,1,0:T(8,128)(2,1)S(1)} %pack_feats.1.refs_0_), channel_id=1, source_target_pairs={{0,2},{2,4},{4,6},{6,0},{1,3},{3,5},{5,7},{7,1},{8,10},{10,12},{12... | collective-permute-start | bytes 1769480 | tf_op jit(solution)/shard_map/ppermute | solution.py:285
  10.3 17.0 %collective-permute-start.6 = (bf16[2,128,1152]{2,1,0:T(8,128)(2,1)S(1)}, bf16[2,128,1152]{2,1,0:T(8,128)(2,1)S(1)}, u32[]{:S(2)}, u32[]{:S(2)}) collective-permute-start(bf16[2,128,1152]{2,1,0:T(8,128)(2,1)S(1)} %pack_feats.1.refs_0_), channel_id=1, source_target_pairs={{0,6},{2,0},{4,2},{6,4},{1,7},{3,1},{5,3},{7,5},{8,14},{10,8},{12,... | collective-permute-start | bytes 1769480 | tf_op jit(solution)/shard_map/ppermute | solution.py:285
  11.8 10.8 %collective-permute-start = (bf16[128,1152]{1,0:T(8,128)(2,1)S(1)}, bf16[128,1152]{1,0:T(8,128)(2,1)S(1)}, u32[]{:S(2)}, u32[]{:S(2)}) collective-permute-start(bf16[128,1152]{1,0:T(8,128)(2,1)S(1)} %get-tuple-element.54), channel_id=1, source_target_pairs={{0,16},{16,0},{1,17},{17,1},{2,18},{18,2},{3,19},{19,3},{4,20},{20... | collective-permute-start | bytes 884744 | tf_op jit(solution)/shard_map/ppermute | solution.py:277
  13.1 1.7 %copy-start = (bf16[1152,1152]{1,0:T(8,128)(2,1)S(1)}, bf16[1152,1152]{1,0:T(8,128)(2,1)}, u32[]{:S(2)}) copy-start(bf16[1152,1152]{1,0:T(8,128)(2,1)} %image_head_hbm.1) | copy-start | bytes 7962628
  19.8 7.4 %collective-permute-start.4 = (bf16[128,1152]{1,0:T(8,128)(2,1)S(1)}, bf16[128,1152]{1,0:T(8,128)(2,1)S(1)}, u32[]{:S(2)}, u32[]{:S(2)}) collective-permute-start(bf16[128,1152]{1,0:T(8,128)(2,1)S(1)} %get-tuple-element.64.v1), channel_id=1, source_target_pairs={{0,16},{16,0},{1,17},{17,1},{2,18},{18,2},{3,19},{19,3},{4,20},{20... | collective-permute-start | bytes 884744 | tf_op jit(solution)/shard_map/ppermute | solution.py:277
  27.2 7.6 %collective-permute-start.7 = (bf16[128,1152]{1,0:T(8,128)(2,1)S(1)}, bf16[128,1152]{1,0:T(8,128)(2,1)S(1)}, u32[]{:S(2)}, u32[]{:S(2)}) collective-permute-start(bf16[128,1152]{1,0:T(8,128)(2,1)S(1)} %collective-permute-done.4.u2), channel_id=1, source_target_pairs={{0,32},{16,240},{32,64},{48,16},{64,96},{80,48},{96,128},{112,80},... | collective-permute-start | bytes 884744 | tf_op jit(solution)/shard_map/ppermute | solution.py:273
  27.3 8.7 %collective-permute-start.8 = (bf16[128,1152]{1,0:T(8,128)(2,1)S(1)}, bf16[128,1152]{1,0:T(8,128)(2,1)S(1)}, u32[]{:S(2)}, u32[]{:S(2)}) collective-permute-start(bf16[128,1152]{1,0:T(8,128)(2,1)S(1)} %get-tuple-element.70.u1), channel_id=1, source_target_pairs={{0,16},{16,0},{1,17},{17,1},{2,18},{18,2},{3,19},{19,3},{4,20},{20... | collective-permute-start | bytes 884744 | tf_op jit(solution)/shard_map/ppermute | solution.py:277
  30.2 10.4 %collective-permute-start.12 = (bf16[128,1152]{1,0:T(8,128)(2,1)S(1)}, bf16[128,1152]{1,0:T(8,128)(2,1)S(1)}, u32[]{:S(2)}, u32[]{:S(2)}) collective-permute-start(bf16[128,1152]{1,0:T(8,128)(2,1)S(1)} %slice_bitcast_fusion.1), channel_id=1, source_target_pairs={{0,2},{2,4},{4,6},{6,0},{1,3},{3,5},{5,7},{7,1},{8,10},{10,12},{12... | collective-permute-start | bytes 884744 | tf_op jit(solution)/shard_map/ppermute | solution.py:285
  30.5 10.0 %collective-permute-start.13 = (bf16[128,1152]{1,0:T(8,128)(2,1)S(1)}, bf16[128,1152]{1,0:T(8,128)(2,1)S(1)}, u32[]{:S(2)}, u32[]{:S(2)}) collective-permute-start(bf16[128,1152]{1,0:T(8,128)(2,1)S(1)} %slice_bitcast_fusion), channel_id=1, source_target_pairs={{0,6},{2,0},{4,2},{6,4},{1,7},{3,1},{5,3},{7,5},{8,14},{10,8},{12,... | collective-permute-start | bytes 884744 | tf_op jit(solution)/shard_map/ppermute | solution.py:285
  37.9 5.7 %collective-permute-start.10 = (bf16[2,384,128]{2,1,0:T(8,128)(2,1)S(1)}, bf16[2,384,128]{2,1,0:T(8,128)(2,1)S(1)}, u32[]{:S(2)}, u32[]{:S(2)}) collective-permute-start(bf16[2,384,128]{2,1,0:T(8,128)(2,1)S(1)} %get-tuple-element.78), channel_id=1, source_target_pairs={{0,6},{2,0},{4,2},{6,4},{1,7},{3,1},{5,3},{7,5},{8,14},{10,8},{12,... | collective-permute-start | bytes 589832 | tf_op jit(solution)/shard_map/ppermute | solution.py:285
  39.4 6.1 %collective-permute-start.11 = (bf16[2,384,128]{2,1,0:T(8,128)(2,1)S(1)}, bf16[2,384,128]{2,1,0:T(8,128)(2,1)S(1)}, u32[]{:S(2)}, u32[]{:S(2)}) collective-permute-start(bf16[2,384,128]{2,1,0:T(8,128)(2,1)S(1)} %get-tuple-element.79), channel_id=1, source_target_pairs={{0,4},{2,6},{4,0},{6,2},{1,5},{3,7},{5,1},{7,3},{8,12},{10,14},{12... | collective-permute-start | bytes 589832 | tf_op jit(solution)/shard_map/ppermute | solution.py:285
  39.9 8.5 %collective-permute-start.9 = (bf16[2,384,128]{2,1,0:T(8,128)(2,1)S(1)}, bf16[2,384,128]{2,1,0:T(8,128)(2,1)S(1)}, u32[]{:S(2)}, u32[]{:S(2)}) collective-permute-start(bf16[2,384,128]{2,1,0:T(8,128)(2,1)S(1)} %get-tuple-element.77), channel_id=1, source_target_pairs={{0,2},{2,4},{4,6},{6,0},{1,3},{3,5},{5,7},{7,1},{8,10},{10,12},{12... | collective-permute-start | bytes 589832 | tf_op jit(solution)/shard_map/ppermute | solution.py:285
  48.4 5.5 %collective-permute-start.14 = (bf16[4,384,128]{2,1,0:T(8,128)(2,1)S(1)}, bf16[4,384,128]{2,1,0:T(8,128)(2,1)S(1)}, u32[]{:S(2)}, u32[]{:S(2)}) collective-permute-start(bf16[4,384,128]{2,1,0:T(8,128)(2,1)S(1)} %others.1), channel_id=1, source_target_pairs={{0,1},{1,0},{2,3},{3,2},{4,5},{5,4},{6,7},{7,6},{8,9},{9,8},{10,11... | collective-permute-start | bytes 1179656 | tf_op jit(solution)/shard_map/ppermute | solution.py:281
  54.9 7.3 %collective-permute-start.15 = (bf16[8,81,128]{2,1,0:T(8,128)(2,1)S(1)}, bf16[8,81,128]{2,1,0:T(8,128)(2,1)S(1)}, u32[]{:S(2)}, u32[]{:S(2)}) collective-permute-start(bf16[8,81,128]{2,1,0:T(8,128)(2,1)S(1)} %get-tuple-element.102), channel_id=1, source_target_pairs={{0,8},{16,24},{8,0},{24,16},{1,9},{17,25},{9,1},{25,17},{2,10},{18... | collective-permute-start | bytes 497672 | tf_op jit(solution)/shard_map/ppermute | solution.py:291
  57.9 8.7 %collective-permute-start.16 = (bf16[8,81,128]{2,1,0:T(8,128)(2,1)S(1)}, bf16[8,81,128]{2,1,0:T(8,128)(2,1)S(1)}, u32[]{:S(2)}, u32[]{:S(2)}) collective-permute-start(bf16[8,81,128]{2,1,0:T(8,128)(2,1)S(1)} %get-tuple-element.103), channel_id=1, source_target_pairs={{0,16},{16,8},{8,24},{24,0},{1,17},{17,9},{9,25},{25,1},{2,18},{18... | collective-permute-start | bytes 497672 | tf_op jit(solution)/shard_map/ppermute | solution.py:291
  57.9 8.7 %collective-permute-start.17 = (bf16[8,81,128]{2,1,0:T(8,128)(2,1)S(1)}, bf16[8,81,128]{2,1,0:T(8,128)(2,1)S(1)}, u32[]{:S(2)}, u32[]{:S(2)}) collective-permute-start(bf16[8,81,128]{2,1,0:T(8,128)(2,1)S(1)} %get-tuple-element.104), channel_id=1, source_target_pairs={{0,24},{16,0},{8,16},{24,8},{1,25},{17,1},{9,17},{25,9},{2,26},{18... | collective-permute-start | bytes 497672 | tf_op jit(solution)/shard_map/ppermute | solution.py:291
  78.0 4.2 %collective-permute-start.18 = (bf16[81,128]{1,0:T(8,128)(2,1)S(1)}, bf16[81,128]{1,0:T(8,128)(2,1)S(1)}, u32[]{:S(2)}, u32[]{:S(2)}) collective-permute-start(bf16[81,128]{1,0:T(8,128)(2,1)S(1)} %add_z.1), channel_id=1, source_target_pairs={{0,8},{8,0},{1,9},{9,1},{2,10},{10,2},{3,11},{11,3},{4,12},{12,4},... | collective-permute-start | bytes 62216 | tf_op jit(solution)/shard_map/ppermute | solution.py:295
  82.2 4.5 %collective-permute-start.20 = (bf16[2,81,128]{2,1,0:T(8,128)(2,1)S(1)}, bf16[2,81,128]{2,1,0:T(8,128)(2,1)S(1)}, u32[]{:S(2)}, u32[]{:S(2)}) collective-permute-start(bf16[2,81,128]{2,1,0:T(8,128)(2,1)S(1)} %get-tuple-element.106), channel_id=1, source_target_pairs={{0,4},{2,6},{4,0},{6,2},{1,5},{3,7},{5,1},{7,3},{8,12},{10,14},{12... | collective-permute-start | bytes 124424 | tf_op jit(solution)/shard_map/ppermute | solution.py:285
  82.9 3.8 %collective-permute-start.21 = (bf16[2,81,128]{2,1,0:T(8,128)(2,1)S(1)}, bf16[2,81,128]{2,1,0:T(8,128)(2,1)S(1)}, u32[]{:S(2)}, u32[]{:S(2)}) collective-permute-start(bf16[2,81,128]{2,1,0:T(8,128)(2,1)S(1)} %get-tuple-element.106), channel_id=1, source_target_pairs={{0,6},{2,0},{4,2},{6,4},{1,7},{3,1},{5,3},{7,5},{8,14},{10,8},{12,... | collective-permute-start | bytes 124424 | tf_op jit(solution)/shard_map/ppermute | solution.py:285
  83.8 4.1 %collective-permute-start.19 = (bf16[2,81,128]{2,1,0:T(8,128)(2,1)S(1)}, bf16[2,81,128]{2,1,0:T(8,128)(2,1)S(1)}, u32[]{:S(2)}, u32[]{:S(2)}) collective-permute-start(bf16[2,81,128]{2,1,0:T(8,128)(2,1)S(1)} %get-tuple-element.106), channel_id=1, source_target_pairs={{0,2},{2,4},{4,6},{6,0},{1,3},{3,5},{5,7},{7,1},{8,10},{10,12},{12... | collective-permute-start | bytes 124424 | tf_op jit(solution)/shard_map/ppermute | solution.py:285
  87.9 6.7 %collective-permute-start.22 = (bf16[4,2,81,128]{3,2,1,0:T(8,128)(2,1)S(1)}, bf16[4,2,81,128]{3,2,1,0:T(8,128)(2,1)S(1)}, u32[]{:S(2)}, u32[]{:S(2)}) collective-permute-start(bf16[4,2,81,128]{3,2,1,0:T(8,128)(2,1)S(1)} %pad_maximum_fusion.mine), channel_id=1, source_target_pairs={{0,1},{1,0},{2,3},{3,2},{4,5},{5,4},{6,7},{7,6},{8,9},{9,8},{10,11... | collective-permute-start | bytes 497672 | tf_op jit(solution)/shard_map/ppermute | solution.py:281

commit v5 on v4

--- a/solution.py
+++ b/solution.py
@@ -90,9 +90,13 @@
         copy.wait()
 
 
-def project_kernel(both, image_head, text_head, emb_u, emb_v, unit_u, unit_v, norm_u, norm_v):
+def project_kernel(
+    scalars, both, image_head, text_head, emb_u, emb_v, unit_u, unit_v, norm_u, norm_v, pair_scalars
+):
     col = lax.axis_index("ylo")
     core = lax.axis_index("core")
+    pair_scalars[:4] = jnp.exp(jnp.full((4, LANES), scalars[0], F32))
+    pair_scalars[4:] = jnp.full((4, LANES), scalars[1], F32)
     image_unit, image_norm = project(pick(core, both[0], both[1]), image_head)
     text_unit, text_norm = project(pick(core, both[1], both[0]), text_head)
     u = pick(col, text_unit, image_unit)
@@ -105,12 +109,16 @@
     norm_v[...] = pick(col, image_norm, text_norm)
 
 
-def project_came_kernel(image, text, image_head, text_head, emb_u, emb_v):
-    col = lax.axis_index("ylo")
-    images = project(image[...], image_head)[0].astype(BF16)
-    texts = project(text[...], text_head)[0].astype(BF16)
-    emb_u[...] = pick(col, texts, images)
-    emb_v[...] = pick(col, images, texts)
+def project_came_kernel(kind, image, text, image_head, text_head, emb):
+    images = lax.axis_index("ylo") == kind
+
+    @pl.when(images)
+    def _():
+        emb[...] = project(image[...], image_head)[0].astype(BF16)
+
+    @pl.when(jnp.logical_not(images))
+    def _():
+        emb[...] = project(text[...], text_head)[0].astype(BF16)
 
 
 def turn_kernel(*refs):
@@ -123,8 +131,8 @@
 
 
 def pair_weights(own, other, scalars, same):
-    scale = jnp.exp(scalars[0])
-    logits = scale * nt(own, other) + scalars[1]
+    scale = scalars[:1]
+    logits = scale * nt(own, other) + scalars[4:5]
     probs = jax.nn.sigmoid(logits)
     if same:
         row = lax.broadcasted_iota(jnp.int32, probs.shape, 0)
@@ -314,20 +322,22 @@
         in_specs=[HBM_SPEC] * 2, scratch=[pltpu.SemaphoreType.DMA((2,))], mib=46,
     )
     image_1, text_1, packed = lax.optimization_barrier((image_1, text_1, packed))
-    u1, v1 = call(
-        project_came_kernel, "project_came", [block, block],
-        (image_1, text_1, image_head, text_head),
-    )
+    came = (image_1, text_1, image_head, text_head)
+    v1 = call(functools.partial(project_came_kernel, 0), "project_v", block, came)
     u2 = y_swap(v1)
-    raw_v0, both, u1 = lax.optimization_barrier((raw_v0, both, u1))
-    u, v, unit_u, unit_v, norm_u, norm_v = call(
-        project_kernel, "project", [block, block, block32, block32, column, column],
-        (both, image_head, text_head),
+    raw_v0, both, image_1, text_1, v1 = lax.optimization_barrier(
+        (raw_v0, both, image_1, text_1, v1)
+    )
+    came = (image_1, text_1, image_head, text_head)
+    u1 = call(functools.partial(project_came_kernel, 1), "project_u", block, came)
+    u, v, unit_u, unit_v, norm_u, norm_v, scalars = call(
+        project_kernel, "project",
+        [block, block, block32, block32, column, column, shape((8, LANES), F32)],
+        (scalars, both, image_head, text_head), in_specs=[SMEM_SPEC] + [VMEM_SPEC] * 3,
     )
     grad_u, grad_v = call(
         early_kernel, "early", [block32, block32],
         (scalars, u, v, u1, v1, raw_v0, image_head, text_head),
-        in_specs=[SMEM_SPEC] + [VMEM_SPEC] * 7,
         scratch=[pltpu.VMEM((ROWS, D), BF16)],
     )
     u2, u1, grad_u, grad_v, feats_1, feats_3 = lax.optimization_barrier(
@@ -337,14 +347,12 @@
     v3 = y_swap(u1)
     feats_2 = (x_turn(feats_1[0], 1), x_turn(feats_3[1], 3))
     grad_v = call(
-        middle_kernel, "middle", block32, (scalars, v, u2, grad_v),
-        in_specs=[SMEM_SPEC] + [VMEM_SPEC] * 3,
+        middle_kernel, "middle", block32, (scalars, v, u2, grad_v)
     )
     sent = shape((2, SENT, ROWS))
     image_dpre, text_dpre, *parts = call(
         late_kernel, "late", [block, block, sent, sent, sent, sent],
         (scalars, u, v, u3, v3, grad_u, grad_v, unit_u, unit_v, norm_u, norm_v),
-        in_specs=[SMEM_SPEC] + [VMEM_SPEC] * 10,
         scratch=[pltpu.VMEM((D, ROWS), BF16)] * 2,
     )
     image_dpre, text_dpre, feats_2 = lax.optimization_barrier((image_dpre, text_dpre, feats_2))

time: 96.2 us -> 95.5 us (level)
  waiting for transfers between devices: 22.7 us -> 26.1 us
  starting transfers between devices: 40 us -> 37.2 us
    ppermute x3, starting transfers between devices: 13.1 us -> 11 us  [core_swap(): return lax.ppermute(array, 'core', [(0, 1), (1, 0)])]
    ppermute x10, waiting for transfers between devices: 8.26 us -> 10.3 us  [x_turn(): return lax.ppermute(array, 'x', [(i, (i + by) % NX) for i in range(NX)])]
    pallas_call x16 -> x17, Pallas kernels: 17.9 us -> 17.1 us  [call(): pl.pallas_call(kernel, out_shape=out_shape, in_specs=in_specs or [pl.Bloc...]
  transfers between devices with their start and end apart: 23 -> 23, of which waited for: 13 -> 13; matrix products, arithmetic and copies ran while one was open for 0% -> 0% of each run, Pallas kernels for 15% -> 14%
where the time goes in v5:
time: 95.5 us; the launch traced here: 95.3 us
  starting transfers between devices  37.2 us (39%)
  waiting for transfers between devices  26.1 us (27%)
  Pallas kernels  17.1 us (18%)
  blocking collectives  11 us (12%)
  between operations  2.1 us (2%)
  local copies, waits for them, and re-layouts  1.8 us (2%)
    pallas_call x17, Pallas kernels, call(): pl.pallas_call(kernel, out_shape=out_shape, in_specs=in_specs or [pl.Bloc...  17.1 us
    all_to_all x1, blocking collectives, body(): pieces = lax.all_to_all(pieces, 'z', 0, 0, tiled=True)  11 us
    ppermute x3, starting transfers between devices, core_swap(): return lax.ppermute(array, 'core', [(0, 1), (1, 0)])  11 us
    ppermute x10, starting transfers between devices, x_turn(): return lax.ppermute(array, 'x', [(i, (i + by) % NX) for i in range(NX)])  10.6 us
    ppermute x10, waiting for transfers between devices, x_turn(): return lax.ppermute(array, 'x', [(i, (i + by) % NX) for i in range(NX)])  10.3 us
    ppermute x3, waiting for transfers between devices, y_turn(): return lax.ppermute(array, ('ylo', 'yhi'), pairs)  6.78 us
    ppermute x3, starting transfers between devices, y_swap(): return lax.ppermute(array, 'ylo', [(0, 1), (1, 0)])  5.75 us
    ppermute x3, starting transfers between devices, y_turn(): return lax.ppermute(array, ('ylo', 'yhi'), pairs)  5.14 us
  transfers between devices with their start and end apart: 23, of which 13 were waited for; matrix products, arithmetic and copies ran while one was open for 0% of the time, Pallas kernels for 14%

profile of v5, /device:TPU:1, one launch (start us, length us, event | category | flops | bytes accessed | tf_op | source)
XLA Modules:
  0.0 95.3 jit_solution(6833922903560615151)
XLA Ops:
  0.6 1.1 %choose.1 = (bf16[2,128,1152]{2,1,0:T(8,128)(2,1)S(1)}, bf16[128,1152]{1,0:T(8,128)(2,1)S(1)}) custom-call(bf16[128,1152]{1,0:T(8,128)(2,1)} %bitcast.image, bf16[128,1152]{1,0:T(8,128)(2,1)} %bitcast.1.text), custom_call_target="tpu_custom_call" | custom-call | flops 1 | bytes 1 | tf_op jit(solution)/shard_map/choose/pallas_call | solution.py:32
  1.8 3.3 %collective-permute-start.3 = (bf16[2,128,1152]{2,1,0:T(8,128)(2,1)S(1)}, bf16[2,128,1152]{2,1,0:T(8,128)(2,1)S(1)}, u32[]{:S(2)}, u32[]{:S(2)}) collective-permute-start(bf16[2,128,1152]{2,1,0:T(8,128)(2,1)S(1)} %get-tuple-element.61.both), channel_id=1, source_target_pairs={{0,1},{1,0},{2,3},{3,2},{4,5},{5,4},{6,7},{7,6},{8,9},{9,8},{10,11... | collective-permute-start | bytes 1769480 | tf_op jit(solution)/shard_map/ppermute | solution.py:289
  5.1 3.9 %collective-permute-start.1 = (bf16[128,1152]{1,0:T(8,128)(2,1)}, bf16[128,1152]{1,0:T(8,128)(2,1)S(1)}, u32[]{:S(2)}, u32[]{:S(2)}) collective-permute-start(bf16[128,1152]{1,0:T(8,128)(2,1)} %bitcast.image), channel_id=1, source_target_pairs={{0,224},{32,0},{64,32},{96,64},{128,96},{160,128},{192,160},{224,1... | collective-permute-start | bytes 884744 | tf_op jit(solution)/shard_map/ppermute | solution.py:273
  9.0 1.3 %collective-permute-start.5 = (bf16[2,128,1152]{2,1,0:T(8,128)(2,1)S(1)}, bf16[2,128,1152]{2,1,0:T(8,128)(2,1)S(1)}, u32[]{:S(2)}, u32[]{:S(2)}) collective-permute-start(bf16[2,128,1152]{2,1,0:T(8,128)(2,1)S(1)} %pack_feats.1.refs_0_), channel_id=1, source_target_pairs={{0,2},{2,4},{4,6},{6,0},{1,3},{3,5},{5,7},{7,1},{8,10},{10,12},{12... | collective-permute-start | bytes 1769480 | tf_op jit(solution)/shard_map/ppermute | solution.py:293
  10.3 1.5 %collective-permute-start.6 = (bf16[2,128,1152]{2,1,0:T(8,128)(2,1)S(1)}, bf16[2,128,1152]{2,1,0:T(8,128)(2,1)S(1)}, u32[]{:S(2)}, u32[]{:S(2)}) collective-permute-start(bf16[2,128,1152]{2,1,0:T(8,128)(2,1)S(1)} %pack_feats.1.refs_0_), channel_id=1, source_target_pairs={{0,6},{2,0},{4,2},{6,4},{1,7},{3,1},{5,3},{7,5},{8,14},{10,8},{12,... | collective-permute-start | bytes 1769480 | tf_op jit(solution)/shard_map/ppermute | solution.py:293
  11.8 1.3 %collective-permute-start = (bf16[128,1152]{1,0:T(8,128)(2,1)S(1)}, bf16[128,1152]{1,0:T(8,128)(2,1)S(1)}, u32[]{:S(2)}, u32[]{:S(2)}) collective-permute-start(bf16[128,1152]{1,0:T(8,128)(2,1)S(1)} %get-tuple-element.55), channel_id=1, source_target_pairs={{0,16},{16,0},{1,17},{17,1},{2,18},{18,2},{3,19},{19,3},{4,20},{20... | collective-permute-start | bytes 884744 | tf_op jit(solution)/shard_map/ppermute | solution.py:285
  13.1 1.7 %copy-done = bf16[1152,1152]{1,0:T(8,128)(2,1)S(1)} copy-done((bf16[1152,1152]{1,0:T(8,128)(2,1)S(1)}, bf16[1152,1152]{1,0:T(8,128)(2,1)}, u32[]{:S(2)}) %copy-start) | copy-done | bytes 2654232
  14.8 2.0 %load.1 = (bf16[1152,1152]{1,0:T(8,128)(2,1)S(1)}, bf16[1152,1152]{1,0:T(8,128)(2,1)S(1)}) custom-call(bf16[1152,1152]{1,0:T(8,128)(2,1)S(1)} %copy-done, bf16[1152,1152]{1,0:T(8,128)(2,1)} %text_head_hbm.1), custom_call_target="tpu_custom_call" | custom-call | flops 1 | bytes 1 | tf_op jit(solution)/shard_map/load/pallas_call | solution.py:32
  16.8 1.8 %collective-permute-done.2.text = bf16[128,1152]{1,0:T(8,128)(2,1)S(1)} collective-permute-done((bf16[128,1152]{1,0:T(8,128)(2,1)}, bf16[128,1152]{1,0:T(8,128)(2,1)S(1)}, u32[]{:S(2)}, u32[]{:S(2)}) %collective-permute-start.2) | collective-permute-done | bytes 294944 | tf_op jit(solution)/shard_map/ppermute | solution.py:273
  19.4 1.4 %collective-permute-start.4 = (bf16[128,1152]{1,0:T(8,128)(2,1)S(1)}, bf16[128,1152]{1,0:T(8,128)(2,1)S(1)}, u32[]{:S(2)}, u32[]{:S(2)}) collective-permute-start(bf16[128,1152]{1,0:T(8,128)(2,1)S(1)} %project_v.1.v1), channel_id=1, source_target_pairs={{0,16},{16,0},{1,17},{17,1},{2,18},{18,2},{3,19},{19,3},{4,20},{20... | collective-permute-start | bytes 884744 | tf_op jit(solution)/shard_map/ppermute | solution.py:285
  22.8 1.8 %project.1 = (bf16[128,1152]{1,0:T(8,128)(2,1)S(1)}, bf16[128,1152]{1,0:T(8,128)(2,1)S(1)}, f32[128,1152]{1,0:T(8,128)S(1)}, f32[128,1152]{1,0:T(8,128)S(1)}, f3...) custom-call(f32[2]{0:T(128)S(1)} %pad_maximum_fusion.2.scalars, ...), custom_call_target="tpu_custom_call" | custom-call | flops 1 | bytes 1 | tf_op jit(solution)/shard_map/project/pallas_call | solution.py:32
  24.6 2.3 %early.1 = (f32[128,1152]{1,0:T(8,128)S(1)}, f32[128,1152]{1,0:T(8,128)S(1)}) custom-call(f32[8,128]{1,0:T(8,128)S(1)} %get-tuple-element.62.scalars, bf16[128,1152]{1,0:T(8,128)(2,1)S(1)} %get-tuple-element.63.u, bf16[128,1152]{1,0:T(8,128)(2,1)S(1)} %get-tuple-element.64.v, bf16[128,1152]{1,0:T(8,128)(2,1)S(1)} %project_u.1.u1, ...), custom_call_target="tpu_custom_call" | custom-call | flops 1 | bytes 1 | tf_op jit(solution)/shard_map/early/pallas_call | solution.py:32
  27.1 3.1 %collective-permute-start.8 = (bf16[128,1152]{1,0:T(8,128)(2,1)S(1)}, bf16[128,1152]{1,0:T(8,128)(2,1)S(1)}, u32[]{:S(2)}, u32[]{:S(2)}) collective-permute-start(bf16[128,1152]{1,0:T(8,128)(2,1)S(1)} %project_u.1.u1), channel_id=1, source_target_pairs={{0,16},{16,0},{1,17},{17,1},{2,18},{18,2},{3,19},{19,3},{4,20},{20... | collective-permute-start | bytes 884744 | tf_op jit(solution)/shard_map/ppermute | solution.py:285
  30.5 2.7 %collective-permute-start.13 = (bf16[128,1152]{1,0:T(8,128)(2,1)S(1)}, bf16[128,1152]{1,0:T(8,128)(2,1)S(1)}, u32[]{:S(2)}, u32[]{:S(2)}) collective-permute-start(bf16[128,1152]{1,0:T(8,128)(2,1)S(1)} %slice_bitcast_fusion), channel_id=1, source_target_pairs={{0,6},{2,0},{4,2},{6,4},{1,7},{3,1},{5,3},{7,5},{8,14},{10,8},{12,... | collective-permute-start | bytes 884744 | tf_op jit(solution)/shard_map/ppermute | solution.py:293
  33.8 1.2 %collective-permute-done.7.u3 = bf16[128,1152]{1,0:T(8,128)(2,1)S(1)} collective-permute-done((bf16[128,1152]{1,0:T(8,128)(2,1)S(1)}, bf16[128,1152]{1,0:T(8,128)(2,1)S(1)}, u32[]{:S(2)}, u32[]{:S(2)}) %collective-permute-start.7) | collective-permute-done | bytes 294944 | tf_op jit(solution)/shard_map/ppermute | solution.py:281
  35.9 1.5 %late.1 = (bf16[128,1152]{1,0:T(8,128)(2,1)S(1)}, bf16[128,1152]{1,0:T(8,128)(2,1)S(1)}, bf16[2,384,128]{2,1,0:T(8,128)(2,1)S(1)}, bf16[2,384,128]{2,1,0:T(8,128...) custom-call(f32[8,128]{1,0:T(8,128)S(1)} %get-tuple-element.62.scalars, ...), custom_call_target="tpu_custom_call" | custom-call | flops 1 | bytes 1 | tf_op jit(solution)/shard_map/late/pallas_call | solution.py:32
  37.3 1.7 %collective-permute-start.10 = (bf16[2,384,128]{2,1,0:T(8,128)(2,1)S(1)}, bf16[2,384,128]{2,1,0:T(8,128)(2,1)S(1)}, u32[]{:S(2)}, u32[]{:S(2)}) collective-permute-start(bf16[2,384,128]{2,1,0:T(8,128)(2,1)S(1)} %get-tuple-element.80), channel_id=1, source_target_pairs={{0,6},{2,0},{4,2},{6,4},{1,7},{3,1},{5,3},{7,5},{8,14},{10,8},{12,... | collective-permute-start | bytes 589832 | tf_op jit(solution)/shard_map/ppermute | solution.py:293
  40.1 2.4 %feats_grad.1 = (bf16[128,1152]{1,0:T(8,128)(2,1)}, bf16[128,1152]{1,0:T(8,128)(2,1)}) custom-call(bf16[128,1152]{1,0:T(8,128)(2,1)S(1)} %get-tuple-element.86.image_dpre, bf16[128,1152]{1,0:T(8,128)(2,1)S(1)} %get-tuple-element.87.text_dpre, bf16[1152,1152]{1,0:T(8,128)(2,1)S(1)} %get-tuple-element.59.image_head, ...), custom_call_target="tpu_custom_call" | custom-call | flops 1 | bytes 1 | tf_op jit(solution)/shard_map/feats_grad/pallas_call | solution.py:32
  43.2 1.0 %collective-permute-done.10.refs_2_ = bf16[2,384,128]{2,1,0:T(8,128)(2,1)S(1)} collective-permute-done((bf16[2,384,128]{2,1,0:T(8,128)(2,1)S(1)}, bf16[2,384,128]{2,1,0:T(8,128)(2,1)S(1)}, u32[]{:S(2)}, u32[]{:S(2)}) %collective-permute-start.10) | collective-permute-done | bytes 196640 | tf_op jit(solution)/shard_map/ppermute | solution.py:293
  45.1 4.8 %collective-permute-done.9.refs_1_ = bf16[2,384,128]{2,1,0:T(8,128)(2,1)S(1)} collective-permute-done((bf16[2,384,128]{2,1,0:T(8,128)(2,1)S(1)}, bf16[2,384,128]{2,1,0:T(8,128)(2,1)S(1)}, u32[]{:S(2)}, u32[]{:S(2)}) %collective-permute-start.9) | collective-permute-done | bytes 196640 | tf_op jit(solution)/shard_map/ppermute | solution.py:293
  50.0 2.2 %collective-permute-start.14 = (bf16[4,384,128]{2,1,0:T(8,128)(2,1)S(1)}, bf16[4,384,128]{2,1,0:T(8,128)(2,1)S(1)}, u32[]{:S(2)}, u32[]{:S(2)}) collective-permute-start(bf16[4,384,128]{2,1,0:T(8,128)(2,1)S(1)} %others.1), channel_id=1, source_target_pairs={{0,1},{1,0},{2,3},{3,2},{4,5},{5,4},{6,7},{7,6},{8,9},{9,8},{10,11... | collective-permute-start | bytes 1179656 | tf_op jit(solution)/shard_map/ppermute | solution.py:289
  54.4 2.5 %collective-permute-start.15 = (bf16[8,81,128]{2,1,0:T(8,128)(2,1)S(1)}, bf16[8,81,128]{2,1,0:T(8,128)(2,1)S(1)}, u32[]{:S(2)}, u32[]{:S(2)}) collective-permute-start(bf16[8,81,128]{2,1,0:T(8,128)(2,1)S(1)} %get-tuple-element.104), channel_id=1, source_target_pairs={{0,8},{16,24},{8,0},{24,16},{1,9},{17,25},{9,1},{25,17},{2,10},{18... | collective-permute-start | bytes 497672 | tf_op jit(solution)/shard_map/ppermute | solution.py:299
  56.9 2.7 %collective-permute-start.17 = (bf16[8,81,128]{2,1,0:T(8,128)(2,1)S(1)}, bf16[8,81,128]{2,1,0:T(8,128)(2,1)S(1)}, u32[]{:S(2)}, u32[]{:S(2)}) collective-permute-start(bf16[8,81,128]{2,1,0:T(8,128)(2,1)S(1)} %get-tuple-element.106), channel_id=1, source_target_pairs={{0,24},{16,0},{8,16},{24,8},{1,25},{17,1},{9,17},{25,9},{2,26},{18... | collective-permute-start | bytes 497672 | tf_op jit(solution)/shard_map/ppermute | solution.py:299
  59.6 2.2 %collective-permute-done.15.refs_1_ = bf16[8,81,128]{2,1,0:T(8,128)(2,1)S(1)} collective-permute-done((bf16[8,81,128]{2,1,0:T(8,128)(2,1)S(1)}, bf16[8,81,128]{2,1,0:T(8,128)(2,1)S(1)}, u32[]{:S(2)}, u32[]{:S(2)}) %collective-permute-start.15) | collective-permute-done | bytes 165920 | tf_op jit(solution)/shard_map/ppermute | solution.py:299
  61.8 4.6 %collective-permute-done.16.refs_2_ = bf16[8,81,128]{2,1,0:T(8,128)(2,1)S(1)} collective-permute-done((bf16[8,81,128]{2,1,0:T(8,128)(2,1)S(1)}, bf16[8,81,128]{2,1,0:T(8,128)(2,1)S(1)}, u32[]{:S(2)}, u32[]{:S(2)}) %collective-permute-start.16) | collective-permute-done | bytes 165920 | tf_op jit(solution)/shard_map/ppermute | solution.py:299
  66.5 11.0 %all_to_all.5.pieces = bf16[8,81,128]{2,1,0:T(8,128)(2,1)S(1)} all-to-all(bf16[8,81,128]{2,1,0:T(8,128)(2,1)S(1)} %add_y.1), channel_id=1, replica_groups=mesh['z'=8,'ylo'=2,'yhi'=2,'x'=4,'core'=2] {'z'}, dimensions={0} | all-to-all | bytes 331776 | tf_op jit(solution)/shard_map/all_to_all | solution.py:387
  78.3 3.5 %collective-permute-done.18 = bf16[81,128]{1,0:T(8,128)(2,1)S(1)} collective-permute-done((bf16[81,128]{1,0:T(8,128)(2,1)S(1)}, bf16[81,128]{1,0:T(8,128)(2,1)S(1)}, u32[]{:S(2)}, u32[]{:S(2)}) %collective-permute-start.18) | collective-permute-done | bytes 20768 | tf_op jit(solution)/shard_map/ppermute | solution.py:303
  83.8 2.4 %collective-permute-done.20 = bf16[2,81,128]{2,1,0:T(8,128)(2,1)S(1)} collective-permute-done((bf16[2,81,128]{2,1,0:T(8,128)(2,1)S(1)}, bf16[2,81,128]{2,1,0:T(8,128)(2,1)S(1)}, u32[]{:S(2)}, u32[]{:S(2)}) %collective-permute-start.20) | collective-permute-done | bytes 41504 | tf_op jit(solution)/shard_map/ppermute | solution.py:293
  86.2 1.2 %collective-permute-done.19 = bf16[2,81,128]{2,1,0:T(8,128)(2,1)S(1)} collective-permute-done((bf16[2,81,128]{2,1,0:T(8,128)(2,1)S(1)}, bf16[2,81,128]{2,1,0:T(8,128)(2,1)S(1)}, u32[]{:S(2)}, u32[]{:S(2)}) %collective-permute-start.19) | collective-permute-done | bytes 41504 | tf_op jit(solution)/shard_map/ppermute | solution.py:293
  87.4 5.5 %collective-permute-start.22 = (bf16[4,2,81,128]{3,2,1,0:T(8,128)(2,1)S(1)}, bf16[4,2,81,128]{3,2,1,0:T(8,128)(2,1)S(1)}, u32[]{:S(2)}, u32[]{:S(2)}) collective-permute-start(bf16[4,2,81,128]{3,2,1,0:T(8,128)(2,1)S(1)} %pad_maximum_fusion.mine), channel_id=1, source_target_pairs={{0,1},{1,0},{2,3},{3,2},{4,5},{5,4},{6,7},{7,6},{8,9},{9,8},{10,11... | collective-permute-start | bytes 497672 | tf_op jit(solution)/shard_map/ppermute | solution.py:289
  92.9 1.0 %collective-permute-done.22.other = bf16[4,2,81,128]{3,2,1,0:T(8,128)(2,1)S(1)} collective-permute-done((bf16[4,2,81,128]{3,2,1,0:T(8,128)(2,1)S(1)}, bf16[4,2,81,128]{3,2,1,0:T(8,128)(2,1)S(1)}, u32[]{:S(2)}, u32[]{:S(2)}) %collective-permute-start.22) | collective-permute-done | bytes 165920 | tf_op jit(solution)/shard_map/ppermute | solution.py:289
  94.0 1.4 %place.1 = f32[72,2,1152]{2,1,0:T(2,128)} custom-call(bf16[4,2,81,128]{3,2,1,0:T(8,128)(2,1)S(1)} %pad_maximum_fusion.mine, bf16[4,2,81,128]{3,2,1,0:T(8,128)(2,1)S(1)} %collective-permute-done.22.other), custom_call_target="tpu_custom_call" | custom-call | flops 1 | bytes 1 | tf_op jit(solution)/shard_map/place/pallas_call | solution.py:32
  (39 shorter events, 11.4 us)
Async XLA Ops:
  1.8 7.2 %collective-permute-start.3 = (bf16[2,128,1152]{2,1,0:T(8,128)(2,1)S(1)}, bf16[2,128,1152]{2,1,0:T(8,128)(2,1)S(1)}, u32[]{:S(2)}, u32[]{:S(2)}) collective-permute-start(bf16[2,128,1152]{2,1,0:T(8,128)(2,1)S(1)} %get-tuple-element.61.both), channel_id=1, source_target_pairs={{0,1},{1,0},{2,3},{3,2},{4,5},{5,4},{6,7},{7,6},{8,9},{9,8},{10,11... | collective-permute-start | bytes 1769480 | tf_op jit(solution)/shard_map/ppermute | solution.py:289
  5.1 11.7 %collective-permute-start.1 = (bf16[128,1152]{1,0:T(8,128)(2,1)}, bf16[128,1152]{1,0:T(8,128)(2,1)S(1)}, u32[]{:S(2)}, u32[]{:S(2)}) collective-permute-start(bf16[128,1152]{1,0:T(8,128)(2,1)} %bitcast.image), channel_id=1, source_target_pairs={{0,224},{32,0},{64,32},{96,64},{128,96},{160,128},{192,160},{224,1... | collective-permute-start | bytes 884744 | tf_op jit(solution)/shard_map/ppermute | solution.py:273
  9.0 9.7 %collective-permute-start.2 = (bf16[128,1152]{1,0:T(8,128)(2,1)}, bf16[128,1152]{1,0:T(8,128)(2,1)S(1)}, u32[]{:S(2)}, u32[]{:S(2)}) collective-permute-start(bf16[128,1152]{1,0:T(8,128)(2,1)} %bitcast.1.text), channel_id=1, source_target_pairs={{0,32},{32,64},{64,96},{96,128},{128,160},{160,192},{192,224},{224... | collective-permute-start | bytes 884744 | tf_op jit(solution)/shard_map/ppermute | solution.py:273
  9.0 18.0 %collective-permute-start.5 = (bf16[2,128,1152]{2,1,0:T(8,128)(2,1)S(1)}, bf16[2,128,1152]{2,1,0:T(8,128)(2,1)S(1)}, u32[]{:S(2)}, u32[]{:S(2)}) collective-permute-start(bf16[2,128,1152]{2,1,0:T(8,128)(2,1)S(1)} %pack_feats.1.refs_0_), channel_id=1, source_target_pairs={{0,2},{2,4},{4,6},{6,0},{1,3},{3,5},{5,7},{7,1},{8,10},{10,12},{12... | collective-permute-start | bytes 1769480 | tf_op jit(solution)/shard_map/ppermute | solution.py:293
  10.3 16.7 %collective-permute-start.6 = (bf16[2,128,1152]{2,1,0:T(8,128)(2,1)S(1)}, bf16[2,128,1152]{2,1,0:T(8,128)(2,1)S(1)}, u32[]{:S(2)}, u32[]{:S(2)}) collective-permute-start(bf16[2,128,1152]{2,1,0:T(8,128)(2,1)S(1)} %pack_feats.1.refs_0_), channel_id=1, source_target_pairs={{0,6},{2,0},{4,2},{6,4},{1,7},{3,1},{5,3},{7,5},{8,14},{10,8},{12,... | collective-permute-start | bytes 1769480 | tf_op jit(solution)/shard_map/ppermute | solution.py:293
  11.8 10.3 %collective-permute-start = (bf16[128,1152]{1,0:T(8,128)(2,1)S(1)}, bf16[128,1152]{1,0:T(8,128)(2,1)S(1)}, u32[]{:S(2)}, u32[]{:S(2)}) collective-permute-start(bf16[128,1152]{1,0:T(8,128)(2,1)S(1)} %get-tuple-element.55), channel_id=1, source_target_pairs={{0,16},{16,0},{1,17},{17,1},{2,18},{18,2},{3,19},{19,3},{4,20},{20... | collective-permute-start | bytes 884744 | tf_op jit(solution)/shard_map/ppermute | solution.py:285
  13.1 1.7 %copy-start = (bf16[1152,1152]{1,0:T(8,128)(2,1)S(1)}, bf16[1152,1152]{1,0:T(8,128)(2,1)}, u32[]{:S(2)}) copy-start(bf16[1152,1152]{1,0:T(8,128)(2,1)} %image_head_hbm.1) | copy-start | bytes 7962628
  19.4 7.6 %collective-permute-start.4 = (bf16[128,1152]{1,0:T(8,128)(2,1)S(1)}, bf16[128,1152]{1,0:T(8,128)(2,1)S(1)}, u32[]{:S(2)}, u32[]{:S(2)}) collective-permute-start(bf16[128,1152]{1,0:T(8,128)(2,1)S(1)} %project_v.1.v1), channel_id=1, source_target_pairs={{0,16},{16,0},{1,17},{17,1},{2,18},{18,2},{3,19},{19,3},{4,20},{20... | collective-permute-start | bytes 884744 | tf_op jit(solution)/shard_map/ppermute | solution.py:285
  27.0 8.0 %collective-permute-start.7 = (bf16[128,1152]{1,0:T(8,128)(2,1)S(1)}, bf16[128,1152]{1,0:T(8,128)(2,1)S(1)}, u32[]{:S(2)}, u32[]{:S(2)}) collective-permute-start(bf16[128,1152]{1,0:T(8,128)(2,1)S(1)} %collective-permute-done.4.u2), channel_id=1, source_target_pairs={{0,32},{16,240},{32,64},{48,16},{64,96},{80,48},{96,128},{112,80},... | collective-permute-start | bytes 884744 | tf_op jit(solution)/shard_map/ppermute | solution.py:281
  27.1 8.8 %collective-permute-start.8 = (bf16[128,1152]{1,0:T(8,128)(2,1)S(1)}, bf16[128,1152]{1,0:T(8,128)(2,1)S(1)}, u32[]{:S(2)}, u32[]{:S(2)}) collective-permute-start(bf16[128,1152]{1,0:T(8,128)(2,1)S(1)} %project_u.1.u1), channel_id=1, source_target_pairs={{0,16},{16,0},{1,17},{17,1},{2,18},{18,2},{3,19},{19,3},{4,20},{20... | collective-permute-start | bytes 884744 | tf_op jit(solution)/shard_map/ppermute | solution.py:285
  30.2 10.0 %collective-permute-start.12 = (bf16[128,1152]{1,0:T(8,128)(2,1)S(1)}, bf16[128,1152]{1,0:T(8,128)(2,1)S(1)}, u32[]{:S(2)}, u32[]{:S(2)}) collective-permute-start(bf16[128,1152]{1,0:T(8,128)(2,1)S(1)} %slice_bitcast_fusion.1), channel_id=1, source_target_pairs={{0,2},{2,4},{4,6},{6,0},{1,3},{3,5},{5,7},{7,1},{8,10},{10,12},{12... | collective-permute-start | bytes 884744 | tf_op jit(solution)/shard_map/ppermute | solution.py:293
  30.5 9.7 %collective-permute-start.13 = (bf16[128,1152]{1,0:T(8,128)(2,1)S(1)}, bf16[128,1152]{1,0:T(8,128)(2,1)S(1)}, u32[]{:S(2)}, u32[]{:S(2)}) collective-permute-start(bf16[128,1152]{1,0:T(8,128)(2,1)S(1)} %slice_bitcast_fusion), channel_id=1, source_target_pairs={{0,6},{2,0},{4,2},{6,4},{1,7},{3,1},{5,3},{7,5},{8,14},{10,8},{12,... | collective-permute-start | bytes 884744 | tf_op jit(solution)/shard_map/ppermute | solution.py:293
  37.3 6.9 %collective-permute-start.10 = (bf16[2,384,128]{2,1,0:T(8,128)(2,1)S(1)}, bf16[2,384,128]{2,1,0:T(8,128)(2,1)S(1)}, u32[]{:S(2)}, u32[]{:S(2)}) collective-permute-start(bf16[2,384,128]{2,1,0:T(8,128)(2,1)S(1)} %get-tuple-element.80), channel_id=1, source_target_pairs={{0,6},{2,0},{4,2},{6,4},{1,7},{3,1},{5,3},{7,5},{8,14},{10,8},{12,... | collective-permute-start | bytes 589832 | tf_op jit(solution)/shard_map/ppermute | solution.py:293
  39.0 6.1 %collective-permute-start.11 = (bf16[2,384,128]{2,1,0:T(8,128)(2,1)S(1)}, bf16[2,384,128]{2,1,0:T(8,128)(2,1)S(1)}, u32[]{:S(2)}, u32[]{:S(2)}) collective-permute-start(bf16[2,384,128]{2,1,0:T(8,128)(2,1)S(1)} %get-tuple-element.81), channel_id=1, source_target_pairs={{0,4},{2,6},{4,0},{6,2},{1,5},{3,7},{5,1},{7,3},{8,12},{10,14},{12... | collective-permute-start | bytes 589832 | tf_op jit(solution)/shard_map/ppermute | solution.py:293
  39.5 10.4 %collective-permute-start.9 = (bf16[2,384,128]{2,1,0:T(8,128)(2,1)S(1)}, bf16[2,384,128]{2,1,0:T(8,128)(2,1)S(1)}, u32[]{:S(2)}, u32[]{:S(2)}) collective-permute-start(bf16[2,384,128]{2,1,0:T(8,128)(2,1)S(1)} %get-tuple-element.79), channel_id=1, source_target_pairs={{0,2},{2,4},{4,6},{6,0},{1,3},{3,5},{5,7},{7,1},{8,10},{10,12},{12... | collective-permute-start | bytes 589832 | tf_op jit(solution)/shard_map/ppermute | solution.py:293
  50.0 3.5 %collective-permute-start.14 = (bf16[4,384,128]{2,1,0:T(8,128)(2,1)S(1)}, bf16[4,384,128]{2,1,0:T(8,128)(2,1)S(1)}, u32[]{:S(2)}, u32[]{:S(2)}) collective-permute-start(bf16[4,384,128]{2,1,0:T(8,128)(2,1)S(1)} %others.1), channel_id=1, source_target_pairs={{0,1},{1,0},{2,3},{3,2},{4,5},{5,4},{6,7},{7,6},{8,9},{9,8},{10,11... | collective-permute-start | bytes 1179656 | tf_op jit(solution)/shard_map/ppermute | solution.py:289
  54.4 7.3 %collective-permute-start.15 = (bf16[8,81,128]{2,1,0:T(8,128)(2,1)S(1)}, bf16[8,81,128]{2,1,0:T(8,128)(2,1)S(1)}, u32[]{:S(2)}, u32[]{:S(2)}) collective-permute-start(bf16[8,81,128]{2,1,0:T(8,128)(2,1)S(1)} %get-tuple-element.104), channel_id=1, source_target_pairs={{0,8},{16,24},{8,0},{24,16},{1,9},{17,25},{9,1},{25,17},{2,10},{18... | collective-permute-start | bytes 497672 | tf_op jit(solution)/shard_map/ppermute | solution.py:299
  56.9 9.5 %collective-permute-start.16 = (bf16[8,81,128]{2,1,0:T(8,128)(2,1)S(1)}, bf16[8,81,128]{2,1,0:T(8,128)(2,1)S(1)}, u32[]{:S(2)}, u32[]{:S(2)}) collective-permute-start(bf16[8,81,128]{2,1,0:T(8,128)(2,1)S(1)} %get-tuple-element.105), channel_id=1, source_target_pairs={{0,16},{16,8},{8,24},{24,0},{1,17},{17,9},{9,25},{25,1},{2,18},{18... | collective-permute-start | bytes 497672 | tf_op jit(solution)/shard_map/ppermute | solution.py:299
  56.9 9.5 %collective-permute-start.17 = (bf16[8,81,128]{2,1,0:T(8,128)(2,1)S(1)}, bf16[8,81,128]{2,1,0:T(8,128)(2,1)S(1)}, u32[]{:S(2)}, u32[]{:S(2)}) collective-permute-start(bf16[8,81,128]{2,1,0:T(8,128)(2,1)S(1)} %get-tuple-element.106), channel_id=1, source_target_pairs={{0,24},{16,0},{8,16},{24,8},{1,25},{17,1},{9,17},{25,9},{2,26},{18... | collective-permute-start | bytes 497672 | tf_op jit(solution)/shard_map/ppermute | solution.py:299
  77.5 4.2 %collective-permute-start.18 = (bf16[81,128]{1,0:T(8,128)(2,1)S(1)}, bf16[81,128]{1,0:T(8,128)(2,1)S(1)}, u32[]{:S(2)}, u32[]{:S(2)}) collective-permute-start(bf16[81,128]{1,0:T(8,128)(2,1)S(1)} %add_z.1), channel_id=1, source_target_pairs={{0,8},{8,0},{1,9},{9,1},{2,10},{10,2},{3,11},{11,3},{4,12},{12,4},... | collective-permute-start | bytes 62216 | tf_op jit(solution)/shard_map/ppermute | solution.py:303
  81.7 4.5 %collective-permute-start.20 = (bf16[2,81,128]{2,1,0:T(8,128)(2,1)S(1)}, bf16[2,81,128]{2,1,0:T(8,128)(2,1)S(1)}, u32[]{:S(2)}, u32[]{:S(2)}) collective-permute-start(bf16[2,81,128]{2,1,0:T(8,128)(2,1)S(1)} %get-tuple-element.108), channel_id=1, source_target_pairs={{0,4},{2,6},{4,0},{6,2},{1,5},{3,7},{5,1},{7,3},{8,12},{10,14},{12... | collective-permute-start | bytes 124424 | tf_op jit(solution)/shard_map/ppermute | solution.py:293
  82.3 3.9 %collective-permute-start.21 = (bf16[2,81,128]{2,1,0:T(8,128)(2,1)S(1)}, bf16[2,81,128]{2,1,0:T(8,128)(2,1)S(1)}, u32[]{:S(2)}, u32[]{:S(2)}) collective-permute-start(bf16[2,81,128]{2,1,0:T(8,128)(2,1)S(1)} %get-tuple-element.108), channel_id=1, source_target_pairs={{0,6},{2,0},{4,2},{6,4},{1,7},{3,1},{5,3},{7,5},{8,14},{10,8},{12,... | collective-permute-start | bytes 124424 | tf_op jit(solution)/shard_map/ppermute | solution.py:293
  83.3 4.1 %collective-permute-start.19 = (bf16[2,81,128]{2,1,0:T(8,128)(2,1)S(1)}, bf16[2,81,128]{2,1,0:T(8,128)(2,1)S(1)}, u32[]{:S(2)}, u32[]{:S(2)}) collective-permute-start(bf16[2,81,128]{2,1,0:T(8,128)(2,1)S(1)} %get-tuple-element.108), channel_id=1, source_target_pairs={{0,2},{2,4},{4,6},{6,0},{1,3},{3,5},{5,7},{7,1},{8,10},{10,12},{12... | collective-permute-start | bytes 124424 | tf_op jit(solution)/shard_map/ppermute | solution.py:293
  87.4 6.5 %collective-permute-start.22 = (bf16[4,2,81,128]{3,2,1,0:T(8,128)(2,1)S(1)}, bf16[4,2,81,128]{3,2,1,0:T(8,128)(2,1)S(1)}, u32[]{:S(2)}, u32[]{:S(2)}) collective-permute-start(bf16[4,2,81,128]{3,2,1,0:T(8,128)(2,1)S(1)} %pad_maximum_fusion.mine), channel_id=1, source_target_pairs={{0,1},{1,0},{2,3},{3,2},{4,5},{5,4},{6,7},{7,6},{8,9},{9,8},{10,11... | collective-permute-start | bytes 497672 | tf_op jit(solution)/shard_map/ppermute | solution.py:289

commit v6 on v5

--- a/solution.py
+++ b/solution.py
@@ -127,7 +127,7 @@
     blocks += [part[...] for part in parts[-2:]]
     for place, rows in enumerate(blocks):
         step, side = divmod(place, NCORE)
-        turned[side][:, step * ROWS:(step + 1) * ROWS] = rows.astype(F32).T.astype(BF16)
+        turned[side][:, step * ROWS:(step + 1) * ROWS] = rows.T
 
 
 def pair_weights(own, other, scalars, same):
@@ -187,8 +187,9 @@
     text = pick(col, dpre_u, dpre_v)
     image_dpre[...] = image.astype(BF16)
     text_dpre[...] = text.astype(BF16)
-    mine_t[...] = pick(core, image, text).T.astype(BF16)
-    other_t[...] = pick(core, text, image).T.astype(BF16)
+    image, text = image.astype(BF16), text.astype(BF16)
+    mine_t[...] = pick(core, image, text).T
+    other_t[...] = pick(core, text, image).T
     for step, sent in enumerate((sent0, sent1, sent2, sent3)):
         to = lax.rem(at + step, NX)
         rows = pl.ds(pl.multiple_of(to * MAIN, MAIN), MAIN)
@@ -260,11 +261,12 @@
         came_x = lax.rem(at + NX - step, NX)
         for flip in range(NYHI):
             index = NYHI * came_x + lax.rem(half_at + flip, NYHI)
-            own = mine[step, flip].astype(F32)
-            across = other[step, flip].astype(F32)
+            own = mine[step, flip]
+            across = other[step, flip]
             lanes = pl.ds(pl.multiple_of(index * LANES, LANES), LANES)
             rows = pl.ds(index * TAIL_ROWS, TAIL_ROWS)
             for head, part in enumerate((pick(core, own, across), pick(core, across, own))):
+                part = part.astype(F32)
                 out[:, head, lanes] = part[:PER_BLK]
                 out[rows, head, TAIL_AT:] = part[PER_BLK:]
 
@@ -363,7 +365,8 @@
     feats_own, feats_across = call(
         turn_kernel, "turn", [shape((D, NX * ROWS))] * 2, (packed, feats_1, feats_3, *feats_2)
     )
-    came = [x_turn(parts[1], 1), x_turn(parts[3], 3), x_turn(parts[2], 2)]
+    far = x_turn(parts[2], 2)
+    came = [x_turn(parts[1], 1), x_turn(parts[3], 3), far]
     came, image_out, text_out, feats_own, feats_across = lax.optimization_barrier(
         (came, image_out, text_out, feats_own, feats_across)
     )
@@ -387,7 +390,8 @@
     pieces = lax.all_to_all(pieces, "z", 0, 0, tiled=True)
     mine = call(add_z_kernel, "add_z", shape((PIECE, LANES)), (pieces,))
     two = jnp.stack([mine, half_swap(mine)])
-    eight = jnp.stack([two] + [x_turn(two, by) for by in range(1, NX)])
+    far = x_turn(two, 2)
+    eight = jnp.stack([two, x_turn(two, 1), far, x_turn(two, 3)])
     places = (eight, core_swap(eight))
     head_grads = call(place_kernel, "place", shape((PER_BLK, 2, D), F32), places)
     return (image_out[None], text_out[None], head_grads)

time: 95.5 us -> 95.5 us (level)
  no operation moved by 1% of the time
where the time goes in v6:
time: 95.5 us; the launch traced here: 95.3 us
  starting transfers between devices  37.2 us (39%)
  waiting for transfers between devices  26.1 us (27%)
  Pallas kernels  17 us (18%)
  blocking collectives  11 us (12%)
  between operations  2.09 us (2%)
  local copies, waits for them, and re-layouts  1.8 us (2%)
    pallas_call x17, Pallas kernels, call(): pl.pallas_call(kernel, out_shape=out_shape, in_specs=in_specs or [pl.Bloc...  17 us
    ppermute x3, starting transfers between devices, core_swap(): return lax.ppermute(array, 'core', [(0, 1), (1, 0)])  11 us
    all_to_all x1, blocking collectives, body(): pieces = lax.all_to_all(pieces, 'z', 0, 0, tiled=True)  11 us
    ppermute x10, starting transfers between devices, x_turn(): return lax.ppermute(array, 'x', [(i, (i + by) % NX) for i in range(NX)])  10.6 us
    ppermute x10, waiting for transfers between devices, x_turn(): return lax.ppermute(array, 'x', [(i, (i + by) % NX) for i in range(NX)])  10.4 us
    ppermute x3, waiting for transfers between devices, y_turn(): return lax.ppermute(array, ('ylo', 'yhi'), pairs)  6.79 us
    ppermute x3, starting transfers between devices, y_swap(): return lax.ppermute(array, 'ylo', [(0, 1), (1, 0)])  5.75 us
    ppermute x3, starting transfers between devices, y_turn(): return lax.ppermute(array, ('ylo', 'yhi'), pairs)  5.14 us
  transfers between devices with their start and end apart: 23, of which 13 were waited for; matrix products, arithmetic and copies ran while one was open for 0% of the time, Pallas kernels for 14%

profile of v6, /device:TPU:1, one launch (start us, length us, event | category | flops | bytes accessed | tf_op | source)
XLA Modules:
  0.0 95.3 jit_solution(16002039090996689765)
XLA Ops:
  0.6 1.1 %choose.1 = (bf16[2,128,1152]{2,1,0:T(8,128)(2,1)S(1)}, bf16[128,1152]{1,0:T(8,128)(2,1)S(1)}) custom-call(bf16[128,1152]{1,0:T(8,128)(2,1)} %bitcast.image, bf16[128,1152]{1,0:T(8,128)(2,1)} %bitcast.1.text), custom_call_target="tpu_custom_call" | custom-call | flops 1 | bytes 1 | tf_op jit(solution)/shard_map/choose/pallas_call | solution.py:32
  1.8 3.3 %collective-permute-start.3 = (bf16[2,128,1152]{2,1,0:T(8,128)(2,1)S(1)}, bf16[2,128,1152]{2,1,0:T(8,128)(2,1)S(1)}, u32[]{:S(2)}, u32[]{:S(2)}) collective-permute-start(bf16[2,128,1152]{2,1,0:T(8,128)(2,1)S(1)} %get-tuple-element.61.both), channel_id=1, source_target_pairs={{0,1},{1,0},{2,3},{3,2},{4,5},{5,4},{6,7},{7,6},{8,9},{9,8},{10,11... | collective-permute-start | bytes 1769480 | tf_op jit(solution)/shard_map/ppermute | solution.py:291
  5.1 3.9 %collective-permute-start.1 = (bf16[128,1152]{1,0:T(8,128)(2,1)}, bf16[128,1152]{1,0:T(8,128)(2,1)S(1)}, u32[]{:S(2)}, u32[]{:S(2)}) collective-permute-start(bf16[128,1152]{1,0:T(8,128)(2,1)} %bitcast.image), channel_id=1, source_target_pairs={{0,224},{32,0},{64,32},{96,64},{128,96},{160,128},{192,160},{224,1... | collective-permute-start | bytes 884744 | tf_op jit(solution)/shard_map/ppermute | solution.py:275
  9.0 1.3 %collective-permute-start.5 = (bf16[2,128,1152]{2,1,0:T(8,128)(2,1)S(1)}, bf16[2,128,1152]{2,1,0:T(8,128)(2,1)S(1)}, u32[]{:S(2)}, u32[]{:S(2)}) collective-permute-start(bf16[2,128,1152]{2,1,0:T(8,128)(2,1)S(1)} %pack_feats.1.refs_0_), channel_id=1, source_target_pairs={{0,2},{2,4},{4,6},{6,0},{1,3},{3,5},{5,7},{7,1},{8,10},{10,12},{12... | collective-permute-start | bytes 1769480 | tf_op jit(solution)/shard_map/ppermute | solution.py:295
  10.3 1.5 %collective-permute-start.6 = (bf16[2,128,1152]{2,1,0:T(8,128)(2,1)S(1)}, bf16[2,128,1152]{2,1,0:T(8,128)(2,1)S(1)}, u32[]{:S(2)}, u32[]{:S(2)}) collective-permute-start(bf16[2,128,1152]{2,1,0:T(8,128)(2,1)S(1)} %pack_feats.1.refs_0_), channel_id=1, source_target_pairs={{0,6},{2,0},{4,2},{6,4},{1,7},{3,1},{5,3},{7,5},{8,14},{10,8},{12,... | collective-permute-start | bytes 1769480 | tf_op jit(solution)/shard_map/ppermute | solution.py:295
  11.8 1.3 %collective-permute-start = (bf16[128,1152]{1,0:T(8,128)(2,1)S(1)}, bf16[128,1152]{1,0:T(8,128)(2,1)S(1)}, u32[]{:S(2)}, u32[]{:S(2)}) collective-permute-start(bf16[128,1152]{1,0:T(8,128)(2,1)S(1)} %get-tuple-element.55), channel_id=1, source_target_pairs={{0,16},{16,0},{1,17},{17,1},{2,18},{18,2},{3,19},{19,3},{4,20},{20... | collective-permute-start | bytes 884744 | tf_op jit(solution)/shard_map/ppermute | solution.py:287
  13.1 1.7 %copy-done = bf16[1152,1152]{1,0:T(8,128)(2,1)S(1)} copy-done((bf16[1152,1152]{1,0:T(8,128)(2,1)S(1)}, bf16[1152,1152]{1,0:T(8,128)(2,1)}, u32[]{:S(2)}) %copy-start) | copy-done | bytes 2654232
  14.8 2.0 %load.1 = (bf16[1152,1152]{1,0:T(8,128)(2,1)S(1)}, bf16[1152,1152]{1,0:T(8,128)(2,1)S(1)}) custom-call(bf16[1152,1152]{1,0:T(8,128)(2,1)S(1)} %copy-done, bf16[1152,1152]{1,0:T(8,128)(2,1)} %text_head_hbm.1), custom_call_target="tpu_custom_call" | custom-call | flops 1 | bytes 1 | tf_op jit(solution)/shard_map/load/pallas_call | solution.py:32
  16.8 1.8 %collective-permute-done.2.text = bf16[128,1152]{1,0:T(8,128)(2,1)S(1)} collective-permute-done((bf16[128,1152]{1,0:T(8,128)(2,1)}, bf16[128,1152]{1,0:T(8,128)(2,1)S(1)}, u32[]{:S(2)}, u32[]{:S(2)}) %collective-permute-start.2) | collective-permute-done | bytes 294944 | tf_op jit(solution)/shard_map/ppermute | solution.py:275
  19.4 1.4 %collective-permute-start.4 = (bf16[128,1152]{1,0:T(8,128)(2,1)S(1)}, bf16[128,1152]{1,0:T(8,128)(2,1)S(1)}, u32[]{:S(2)}, u32[]{:S(2)}) collective-permute-start(bf16[128,1152]{1,0:T(8,128)(2,1)S(1)} %project_v.1.v1), channel_id=1, source_target_pairs={{0,16},{16,0},{1,17},{17,1},{2,18},{18,2},{3,19},{19,3},{4,20},{20... | collective-permute-start | bytes 884744 | tf_op jit(solution)/shard_map/ppermute | solution.py:287
  22.8 1.8 %project.1 = (bf16[128,1152]{1,0:T(8,128)(2,1)S(1)}, bf16[128,1152]{1,0:T(8,128)(2,1)S(1)}, f32[128,1152]{1,0:T(8,128)S(1)}, f32[128,1152]{1,0:T(8,128)S(1)}, f3...) custom-call(f32[2]{0:T(128)S(1)} %pad_maximum_fusion.2.scalars, ...), custom_call_target="tpu_custom_call" | custom-call | flops 1 | bytes 1 | tf_op jit(solution)/shard_map/project/pallas_call | solution.py:32
  24.6 2.3 %early.1 = (f32[128,1152]{1,0:T(8,128)S(1)}, f32[128,1152]{1,0:T(8,128)S(1)}) custom-call(f32[8,128]{1,0:T(8,128)S(1)} %get-tuple-element.62.scalars, bf16[128,1152]{1,0:T(8,128)(2,1)S(1)} %get-tuple-element.63.u, bf16[128,1152]{1,0:T(8,128)(2,1)S(1)} %get-tuple-element.64.v, bf16[128,1152]{1,0:T(8,128)(2,1)S(1)} %project_u.1.u1, ...), custom_call_target="tpu_custom_call" | custom-call | flops 1 | bytes 1 | tf_op jit(solution)/shard_map/early/pallas_call | solution.py:32
  27.1 3.1 %collective-permute-start.8 = (bf16[128,1152]{1,0:T(8,128)(2,1)S(1)}, bf16[128,1152]{1,0:T(8,128)(2,1)S(1)}, u32[]{:S(2)}, u32[]{:S(2)}) collective-permute-start(bf16[128,1152]{1,0:T(8,128)(2,1)S(1)} %project_u.1.u1), channel_id=1, source_target_pairs={{0,16},{16,0},{1,17},{17,1},{2,18},{18,2},{3,19},{19,3},{4,20},{20... | collective-permute-start | bytes 884744 | tf_op jit(solution)/shard_map/ppermute | solution.py:287
  30.5 2.7 %collective-permute-start.13 = (bf16[128,1152]{1,0:T(8,128)(2,1)S(1)}, bf16[128,1152]{1,0:T(8,128)(2,1)S(1)}, u32[]{:S(2)}, u32[]{:S(2)}) collective-permute-start(bf16[128,1152]{1,0:T(8,128)(2,1)S(1)} %slice_bitcast_fusion), channel_id=1, source_target_pairs={{0,6},{2,0},{4,2},{6,4},{1,7},{3,1},{5,3},{7,5},{8,14},{10,8},{12,... | collective-permute-start | bytes 884744 | tf_op jit(solution)/shard_map/ppermute | solution.py:295
  33.8 1.2 %collective-permute-done.7.u3 = bf16[128,1152]{1,0:T(8,128)(2,1)S(1)} collective-permute-done((bf16[128,1152]{1,0:T(8,128)(2,1)S(1)}, bf16[128,1152]{1,0:T(8,128)(2,1)S(1)}, u32[]{:S(2)}, u32[]{:S(2)}) %collective-permute-start.7) | collective-permute-done | bytes 294944 | tf_op jit(solution)/shard_map/ppermute | solution.py:283
  35.9 1.4 %late.1 = (bf16[128,1152]{1,0:T(8,128)(2,1)S(1)}, bf16[128,1152]{1,0:T(8,128)(2,1)S(1)}, bf16[2,384,128]{2,1,0:T(8,128)(2,1)S(1)}, bf16[2,384,128]{2,1,0:T(8,128...) custom-call(f32[8,128]{1,0:T(8,128)S(1)} %get-tuple-element.62.scalars, ...), custom_call_target="tpu_custom_call" | custom-call | flops 1 | bytes 1 | tf_op jit(solution)/shard_map/late/pallas_call | solution.py:32
  37.3 1.7 %collective-permute-start.10 = (bf16[2,384,128]{2,1,0:T(8,128)(2,1)S(1)}, bf16[2,384,128]{2,1,0:T(8,128)(2,1)S(1)}, u32[]{:S(2)}, u32[]{:S(2)}) collective-permute-start(bf16[2,384,128]{2,1,0:T(8,128)(2,1)S(1)} %get-tuple-element.80), channel_id=1, source_target_pairs={{0,6},{2,0},{4,2},{6,4},{1,7},{3,1},{5,3},{7,5},{8,14},{10,8},{12,... | collective-permute-start | bytes 589832 | tf_op jit(solution)/shard_map/ppermute | solution.py:295
  40.1 2.4 %feats_grad.1 = (bf16[128,1152]{1,0:T(8,128)(2,1)}, bf16[128,1152]{1,0:T(8,128)(2,1)}) custom-call(bf16[128,1152]{1,0:T(8,128)(2,1)S(1)} %get-tuple-element.86.image_dpre, bf16[128,1152]{1,0:T(8,128)(2,1)S(1)} %get-tuple-element.87.text_dpre, bf16[1152,1152]{1,0:T(8,128)(2,1)S(1)} %get-tuple-element.59.image_head, ...), custom_call_target="tpu_custom_call" | custom-call | flops 1 | bytes 1 | tf_op jit(solution)/shard_map/feats_grad/pallas_call | solution.py:32
  43.2 1.2 %collective-permute-done.10.refs_2_ = bf16[2,384,128]{2,1,0:T(8,128)(2,1)S(1)} collective-permute-done((bf16[2,384,128]{2,1,0:T(8,128)(2,1)S(1)}, bf16[2,384,128]{2,1,0:T(8,128)(2,1)S(1)}, u32[]{:S(2)}, u32[]{:S(2)}) %collective-permute-start.10) | collective-permute-done | bytes 196640 | tf_op jit(solution)/shard_map/ppermute | solution.py:295
  45.1 4.8 %collective-permute-done.9.refs_1_ = bf16[2,384,128]{2,1,0:T(8,128)(2,1)S(1)} collective-permute-done((bf16[2,384,128]{2,1,0:T(8,128)(2,1)S(1)}, bf16[2,384,128]{2,1,0:T(8,128)(2,1)S(1)}, u32[]{:S(2)}, u32[]{:S(2)}) %collective-permute-start.9) | collective-permute-done | bytes 196640 | tf_op jit(solution)/shard_map/ppermute | solution.py:295
  49.9 2.2 %collective-permute-start.14 = (bf16[4,384,128]{2,1,0:T(8,128)(2,1)S(1)}, bf16[4,384,128]{2,1,0:T(8,128)(2,1)S(1)}, u32[]{:S(2)}, u32[]{:S(2)}) collective-permute-start(bf16[4,384,128]{2,1,0:T(8,128)(2,1)S(1)} %others.1), channel_id=1, source_target_pairs={{0,1},{1,0},{2,3},{3,2},{4,5},{5,4},{6,7},{7,6},{8,9},{9,8},{10,11... | collective-permute-start | bytes 1179656 | tf_op jit(solution)/shard_map/ppermute | solution.py:291
  54.4 2.5 %collective-permute-start.15 = (bf16[8,81,128]{2,1,0:T(8,128)(2,1)S(1)}, bf16[8,81,128]{2,1,0:T(8,128)(2,1)S(1)}, u32[]{:S(2)}, u32[]{:S(2)}) collective-permute-start(bf16[8,81,128]{2,1,0:T(8,128)(2,1)S(1)} %get-tuple-element.104), channel_id=1, source_target_pairs={{0,8},{16,24},{8,0},{24,16},{1,9},{17,25},{9,1},{25,17},{2,10},{18... | collective-permute-start | bytes 497672 | tf_op jit(solution)/shard_map/ppermute | solution.py:301
  56.9 2.7 %collective-permute-start.17 = (bf16[8,81,128]{2,1,0:T(8,128)(2,1)S(1)}, bf16[8,81,128]{2,1,0:T(8,128)(2,1)S(1)}, u32[]{:S(2)}, u32[]{:S(2)}) collective-permute-start(bf16[8,81,128]{2,1,0:T(8,128)(2,1)S(1)} %get-tuple-element.106), channel_id=1, source_target_pairs={{0,24},{16,0},{8,16},{24,8},{1,25},{17,1},{9,17},{25,9},{2,26},{18... | collective-permute-start | bytes 497672 | tf_op jit(solution)/shard_map/ppermute | solution.py:301
  59.5 2.2 %collective-permute-done.15.refs_1_ = bf16[8,81,128]{2,1,0:T(8,128)(2,1)S(1)} collective-permute-done((bf16[8,81,128]{2,1,0:T(8,128)(2,1)S(1)}, bf16[8,81,128]{2,1,0:T(8,128)(2,1)S(1)}, u32[]{:S(2)}, u32[]{:S(2)}) %collective-permute-start.15) | collective-permute-done | bytes 165920 | tf_op jit(solution)/shard_map/ppermute | solution.py:301
  61.7 4.6 %collective-permute-done.16.refs_2_ = bf16[8,81,128]{2,1,0:T(8,128)(2,1)S(1)} collective-permute-done((bf16[8,81,128]{2,1,0:T(8,128)(2,1)S(1)}, bf16[8,81,128]{2,1,0:T(8,128)(2,1)S(1)}, u32[]{:S(2)}, u32[]{:S(2)}) %collective-permute-start.16) | collective-permute-done | bytes 165920 | tf_op jit(solution)/shard_map/ppermute | solution.py:301
  66.4 11.0 %all_to_all.5.pieces = bf16[8,81,128]{2,1,0:T(8,128)(2,1)S(1)} all-to-all(bf16[8,81,128]{2,1,0:T(8,128)(2,1)S(1)} %add_y.1), channel_id=1, replica_groups=mesh['z'=8,'ylo'=2,'yhi'=2,'x'=4,'core'=2] {'z'}, dimensions={0} | all-to-all | bytes 331776 | tf_op jit(solution)/shard_map/all_to_all | solution.py:390
  78.2 3.5 %collective-permute-done.18 = bf16[81,128]{1,0:T(8,128)(2,1)S(1)} collective-permute-done((bf16[81,128]{1,0:T(8,128)(2,1)S(1)}, bf16[81,128]{1,0:T(8,128)(2,1)S(1)}, u32[]{:S(2)}, u32[]{:S(2)}) %collective-permute-start.18) | collective-permute-done | bytes 20768 | tf_op jit(solution)/shard_map/ppermute | solution.py:305
  83.8 2.4 %collective-permute-done.20 = bf16[2,81,128]{2,1,0:T(8,128)(2,1)S(1)} collective-permute-done((bf16[2,81,128]{2,1,0:T(8,128)(2,1)S(1)}, bf16[2,81,128]{2,1,0:T(8,128)(2,1)S(1)}, u32[]{:S(2)}, u32[]{:S(2)}) %collective-permute-start.20) | collective-permute-done | bytes 41504 | tf_op jit(solution)/shard_map/ppermute | solution.py:295
  86.2 1.2 %collective-permute-done.19 = bf16[2,81,128]{2,1,0:T(8,128)(2,1)S(1)} collective-permute-done((bf16[2,81,128]{2,1,0:T(8,128)(2,1)S(1)}, bf16[2,81,128]{2,1,0:T(8,128)(2,1)S(1)}, u32[]{:S(2)}, u32[]{:S(2)}) %collective-permute-start.19) | collective-permute-done | bytes 41504 | tf_op jit(solution)/shard_map/ppermute | solution.py:295
  87.4 5.5 %collective-permute-start.22 = (bf16[4,2,81,128]{3,2,1,0:T(8,128)(2,1)S(1)}, bf16[4,2,81,128]{3,2,1,0:T(8,128)(2,1)S(1)}, u32[]{:S(2)}, u32[]{:S(2)}) collective-permute-start(bf16[4,2,81,128]{3,2,1,0:T(8,128)(2,1)S(1)} %pad_maximum_fusion.mine), channel_id=1, source_target_pairs={{0,1},{1,0},{2,3},{3,2},{4,5},{5,4},{6,7},{7,6},{8,9},{9,8},{10,11... | collective-permute-start | bytes 497672 | tf_op jit(solution)/shard_map/ppermute | solution.py:291
  92.9 1.0 %collective-permute-done.22.other = bf16[4,2,81,128]{3,2,1,0:T(8,128)(2,1)S(1)} collective-permute-done((bf16[4,2,81,128]{3,2,1,0:T(8,128)(2,1)S(1)}, bf16[4,2,81,128]{3,2,1,0:T(8,128)(2,1)S(1)}, u32[]{:S(2)}, u32[]{:S(2)}) %collective-permute-start.22) | collective-permute-done | bytes 165920 | tf_op jit(solution)/shard_map/ppermute | solution.py:291
  93.9 1.3 %place.1 = f32[72,2,1152]{2,1,0:T(2,128)} custom-call(bf16[4,2,81,128]{3,2,1,0:T(8,128)(2,1)S(1)} %pad_maximum_fusion.mine, bf16[4,2,81,128]{3,2,1,0:T(8,128)(2,1)S(1)} %collective-permute-done.22.other), custom_call_target="tpu_custom_call" | custom-call | flops 1 | bytes 1 | tf_op jit(solution)/shard_map/place/pallas_call | solution.py:32
  (39 shorter events, 11.2 us)
Async XLA Ops:
  1.8 7.2 %collective-permute-start.3 = (bf16[2,128,1152]{2,1,0:T(8,128)(2,1)S(1)}, bf16[2,128,1152]{2,1,0:T(8,128)(2,1)S(1)}, u32[]{:S(2)}, u32[]{:S(2)}) collective-permute-start(bf16[2,128,1152]{2,1,0:T(8,128)(2,1)S(1)} %get-tuple-element.61.both), channel_id=1, source_target_pairs={{0,1},{1,0},{2,3},{3,2},{4,5},{5,4},{6,7},{7,6},{8,9},{9,8},{10,11... | collective-permute-start | bytes 1769480 | tf_op jit(solution)/shard_map/ppermute | solution.py:291
  5.1 11.7 %collective-permute-start.1 = (bf16[128,1152]{1,0:T(8,128)(2,1)}, bf16[128,1152]{1,0:T(8,128)(2,1)S(1)}, u32[]{:S(2)}, u32[]{:S(2)}) collective-permute-start(bf16[128,1152]{1,0:T(8,128)(2,1)} %bitcast.image), channel_id=1, source_target_pairs={{0,224},{32,0},{64,32},{96,64},{128,96},{160,128},{192,160},{224,1... | collective-permute-start | bytes 884744 | tf_op jit(solution)/shard_map/ppermute | solution.py:275
  9.0 9.7 %collective-permute-start.2 = (bf16[128,1152]{1,0:T(8,128)(2,1)}, bf16[128,1152]{1,0:T(8,128)(2,1)S(1)}, u32[]{:S(2)}, u32[]{:S(2)}) collective-permute-start(bf16[128,1152]{1,0:T(8,128)(2,1)} %bitcast.1.text), channel_id=1, source_target_pairs={{0,32},{32,64},{64,96},{96,128},{128,160},{160,192},{192,224},{224... | collective-permute-start | bytes 884744 | tf_op jit(solution)/shard_map/ppermute | solution.py:275
  9.0 18.0 %collective-permute-start.5 = (bf16[2,128,1152]{2,1,0:T(8,128)(2,1)S(1)}, bf16[2,128,1152]{2,1,0:T(8,128)(2,1)S(1)}, u32[]{:S(2)}, u32[]{:S(2)}) collective-permute-start(bf16[2,128,1152]{2,1,0:T(8,128)(2,1)S(1)} %pack_feats.1.refs_0_), channel_id=1, source_target_pairs={{0,2},{2,4},{4,6},{6,0},{1,3},{3,5},{5,7},{7,1},{8,10},{10,12},{12... | collective-permute-start | bytes 1769480 | tf_op jit(solution)/shard_map/ppermute | solution.py:295
  10.3 16.7 %collective-permute-start.6 = (bf16[2,128,1152]{2,1,0:T(8,128)(2,1)S(1)}, bf16[2,128,1152]{2,1,0:T(8,128)(2,1)S(1)}, u32[]{:S(2)}, u32[]{:S(2)}) collective-permute-start(bf16[2,128,1152]{2,1,0:T(8,128)(2,1)S(1)} %pack_feats.1.refs_0_), channel_id=1, source_target_pairs={{0,6},{2,0},{4,2},{6,4},{1,7},{3,1},{5,3},{7,5},{8,14},{10,8},{12,... | collective-permute-start | bytes 1769480 | tf_op jit(solution)/shard_map/ppermute | solution.py:295
  11.8 10.3 %collective-permute-start = (bf16[128,1152]{1,0:T(8,128)(2,1)S(1)}, bf16[128,1152]{1,0:T(8,128)(2,1)S(1)}, u32[]{:S(2)}, u32[]{:S(2)}) collective-permute-start(bf16[128,1152]{1,0:T(8,128)(2,1)S(1)} %get-tuple-element.55), channel_id=1, source_target_pairs={{0,16},{16,0},{1,17},{17,1},{2,18},{18,2},{3,19},{19,3},{4,20},{20... | collective-permute-start | bytes 884744 | tf_op jit(solution)/shard_map/ppermute | solution.py:287
  13.1 1.7 %copy-start = (bf16[1152,1152]{1,0:T(8,128)(2,1)S(1)}, bf16[1152,1152]{1,0:T(8,128)(2,1)}, u32[]{:S(2)}) copy-start(bf16[1152,1152]{1,0:T(8,128)(2,1)} %image_head_hbm.1) | copy-start | bytes 7962628
  19.4 7.6 %collective-permute-start.4 = (bf16[128,1152]{1,0:T(8,128)(2,1)S(1)}, bf16[128,1152]{1,0:T(8,128)(2,1)S(1)}, u32[]{:S(2)}, u32[]{:S(2)}) collective-permute-start(bf16[128,1152]{1,0:T(8,128)(2,1)S(1)} %project_v.1.v1), channel_id=1, source_target_pairs={{0,16},{16,0},{1,17},{17,1},{2,18},{18,2},{3,19},{19,3},{4,20},{20... | collective-permute-start | bytes 884744 | tf_op jit(solution)/shard_map/ppermute | solution.py:287
  27.0 8.0 %collective-permute-start.7 = (bf16[128,1152]{1,0:T(8,128)(2,1)S(1)}, bf16[128,1152]{1,0:T(8,128)(2,1)S(1)}, u32[]{:S(2)}, u32[]{:S(2)}) collective-permute-start(bf16[128,1152]{1,0:T(8,128)(2,1)S(1)} %collective-permute-done.4.u2), channel_id=1, source_target_pairs={{0,32},{16,240},{32,64},{48,16},{64,96},{80,48},{96,128},{112,80},... | collective-permute-start | bytes 884744 | tf_op jit(solution)/shard_map/ppermute | solution.py:283
  27.1 8.8 %collective-permute-start.8 = (bf16[128,1152]{1,0:T(8,128)(2,1)S(1)}, bf16[128,1152]{1,0:T(8,128)(2,1)S(1)}, u32[]{:S(2)}, u32[]{:S(2)}) collective-permute-start(bf16[128,1152]{1,0:T(8,128)(2,1)S(1)} %project_u.1.u1), channel_id=1, source_target_pairs={{0,16},{16,0},{1,17},{17,1},{2,18},{18,2},{3,19},{19,3},{4,20},{20... | collective-permute-start | bytes 884744 | tf_op jit(solution)/shard_map/ppermute | solution.py:287
  30.2 9.9 %collective-permute-start.12 = (bf16[128,1152]{1,0:T(8,128)(2,1)S(1)}, bf16[128,1152]{1,0:T(8,128)(2,1)S(1)}, u32[]{:S(2)}, u32[]{:S(2)}) collective-permute-start(bf16[128,1152]{1,0:T(8,128)(2,1)S(1)} %slice_bitcast_fusion.1), channel_id=1, source_target_pairs={{0,2},{2,4},{4,6},{6,0},{1,3},{3,5},{5,7},{7,1},{8,10},{10,12},{12... | collective-permute-start | bytes 884744 | tf_op jit(solution)/shard_map/ppermute | solution.py:295
  30.5 9.6 %collective-permute-start.13 = (bf16[128,1152]{1,0:T(8,128)(2,1)S(1)}, bf16[128,1152]{1,0:T(8,128)(2,1)S(1)}, u32[]{:S(2)}, u32[]{:S(2)}) collective-permute-start(bf16[128,1152]{1,0:T(8,128)(2,1)S(1)} %slice_bitcast_fusion), channel_id=1, source_target_pairs={{0,6},{2,0},{4,2},{6,4},{1,7},{3,1},{5,3},{7,5},{8,14},{10,8},{12,... | collective-permute-start | bytes 884744 | tf_op jit(solution)/shard_map/ppermute | solution.py:295
  37.3 7.0 %collective-permute-start.10 = (bf16[2,384,128]{2,1,0:T(8,128)(2,1)S(1)}, bf16[2,384,128]{2,1,0:T(8,128)(2,1)S(1)}, u32[]{:S(2)}, u32[]{:S(2)}) collective-permute-start(bf16[2,384,128]{2,1,0:T(8,128)(2,1)S(1)} %get-tuple-element.80), channel_id=1, source_target_pairs={{0,6},{2,0},{4,2},{6,4},{1,7},{3,1},{5,3},{7,5},{8,14},{10,8},{12,... | collective-permute-start | bytes 589832 | tf_op jit(solution)/shard_map/ppermute | solution.py:295
  39.0 6.1 %collective-permute-start.11 = (bf16[2,384,128]{2,1,0:T(8,128)(2,1)S(1)}, bf16[2,384,128]{2,1,0:T(8,128)(2,1)S(1)}, u32[]{:S(2)}, u32[]{:S(2)}) collective-permute-start(bf16[2,384,128]{2,1,0:T(8,128)(2,1)S(1)} %get-tuple-element.81), channel_id=1, source_target_pairs={{0,4},{2,6},{4,0},{6,2},{1,5},{3,7},{5,1},{7,3},{8,12},{10,14},{12... | collective-permute-start | bytes 589832 | tf_op jit(solution)/shard_map/ppermute | solution.py:295
  39.5 10.4 %collective-permute-start.9 = (bf16[2,384,128]{2,1,0:T(8,128)(2,1)S(1)}, bf16[2,384,128]{2,1,0:T(8,128)(2,1)S(1)}, u32[]{:S(2)}, u32[]{:S(2)}) collective-permute-start(bf16[2,384,128]{2,1,0:T(8,128)(2,1)S(1)} %get-tuple-element.79), channel_id=1, source_target_pairs={{0,2},{2,4},{4,6},{6,0},{1,3},{3,5},{5,7},{7,1},{8,10},{10,12},{12... | collective-permute-start | bytes 589832 | tf_op jit(solution)/shard_map/ppermute | solution.py:295
  49.9 3.5 %collective-permute-start.14 = (bf16[4,384,128]{2,1,0:T(8,128)(2,1)S(1)}, bf16[4,384,128]{2,1,0:T(8,128)(2,1)S(1)}, u32[]{:S(2)}, u32[]{:S(2)}) collective-permute-start(bf16[4,384,128]{2,1,0:T(8,128)(2,1)S(1)} %others.1), channel_id=1, source_target_pairs={{0,1},{1,0},{2,3},{3,2},{4,5},{5,4},{6,7},{7,6},{8,9},{9,8},{10,11... | collective-permute-start | bytes 1179656 | tf_op jit(solution)/shard_map/ppermute | solution.py:291
  54.4 7.4 %collective-permute-start.15 = (bf16[8,81,128]{2,1,0:T(8,128)(2,1)S(1)}, bf16[8,81,128]{2,1,0:T(8,128)(2,1)S(1)}, u32[]{:S(2)}, u32[]{:S(2)}) collective-permute-start(bf16[8,81,128]{2,1,0:T(8,128)(2,1)S(1)} %get-tuple-element.104), channel_id=1, source_target_pairs={{0,8},{16,24},{8,0},{24,16},{1,9},{17,25},{9,1},{25,17},{2,10},{18... | collective-permute-start | bytes 497672 | tf_op jit(solution)/shard_map/ppermute | solution.py:301
  56.9 9.5 %collective-permute-start.16 = (bf16[8,81,128]{2,1,0:T(8,128)(2,1)S(1)}, bf16[8,81,128]{2,1,0:T(8,128)(2,1)S(1)}, u32[]{:S(2)}, u32[]{:S(2)}) collective-permute-start(bf16[8,81,128]{2,1,0:T(8,128)(2,1)S(1)} %get-tuple-element.105), channel_id=1, source_target_pairs={{0,16},{16,8},{8,24},{24,0},{1,17},{17,9},{9,25},{25,1},{2,18},{18... | collective-permute-start | bytes 497672 | tf_op jit(solution)/shard_map/ppermute | solution.py:301
  56.9 9.5 %collective-permute-start.17 = (bf16[8,81,128]{2,1,0:T(8,128)(2,1)S(1)}, bf16[8,81,128]{2,1,0:T(8,128)(2,1)S(1)}, u32[]{:S(2)}, u32[]{:S(2)}) collective-permute-start(bf16[8,81,128]{2,1,0:T(8,128)(2,1)S(1)} %get-tuple-element.106), channel_id=1, source_target_pairs={{0,24},{16,0},{8,16},{24,8},{1,25},{17,1},{9,17},{25,9},{2,26},{18... | collective-permute-start | bytes 497672 | tf_op jit(solution)/shard_map/ppermute | solution.py:301
  77.4 4.2 %collective-permute-start.18 = (bf16[81,128]{1,0:T(8,128)(2,1)S(1)}, bf16[81,128]{1,0:T(8,128)(2,1)S(1)}, u32[]{:S(2)}, u32[]{:S(2)}) collective-permute-start(bf16[81,128]{1,0:T(8,128)(2,1)S(1)} %add_z.1), channel_id=1, source_target_pairs={{0,8},{8,0},{1,9},{9,1},{2,10},{10,2},{3,11},{11,3},{4,12},{12,4},... | collective-permute-start | bytes 62216 | tf_op jit(solution)/shard_map/ppermute | solution.py:305
  81.7 4.5 %collective-permute-start.20 = (bf16[2,81,128]{2,1,0:T(8,128)(2,1)S(1)}, bf16[2,81,128]{2,1,0:T(8,128)(2,1)S(1)}, u32[]{:S(2)}, u32[]{:S(2)}) collective-permute-start(bf16[2,81,128]{2,1,0:T(8,128)(2,1)S(1)} %get-tuple-element.108), channel_id=1, source_target_pairs={{0,4},{2,6},{4,0},{6,2},{1,5},{3,7},{5,1},{7,3},{8,12},{10,14},{12... | collective-permute-start | bytes 124424 | tf_op jit(solution)/shard_map/ppermute | solution.py:295
  82.3 3.9 %collective-permute-start.21 = (bf16[2,81,128]{2,1,0:T(8,128)(2,1)S(1)}, bf16[2,81,128]{2,1,0:T(8,128)(2,1)S(1)}, u32[]{:S(2)}, u32[]{:S(2)}) collective-permute-start(bf16[2,81,128]{2,1,0:T(8,128)(2,1)S(1)} %get-tuple-element.108), channel_id=1, source_target_pairs={{0,6},{2,0},{4,2},{6,4},{1,7},{3,1},{5,3},{7,5},{8,14},{10,8},{12,... | collective-permute-start | bytes 124424 | tf_op jit(solution)/shard_map/ppermute | solution.py:295
  83.3 4.1 %collective-permute-start.19 = (bf16[2,81,128]{2,1,0:T(8,128)(2,1)S(1)}, bf16[2,81,128]{2,1,0:T(8,128)(2,1)S(1)}, u32[]{:S(2)}, u32[]{:S(2)}) collective-permute-start(bf16[2,81,128]{2,1,0:T(8,128)(2,1)S(1)} %get-tuple-element.108), channel_id=1, source_target_pairs={{0,2},{2,4},{4,6},{6,0},{1,3},{3,5},{5,7},{7,1},{8,10},{10,12},{12... | collective-permute-start | bytes 124424 | tf_op jit(solution)/shard_map/ppermute | solution.py:295
  87.4 6.5 %collective-permute-start.22 = (bf16[4,2,81,128]{3,2,1,0:T(8,128)(2,1)S(1)}, bf16[4,2,81,128]{3,2,1,0:T(8,128)(2,1)S(1)}, u32[]{:S(2)}, u32[]{:S(2)}) collective-permute-start(bf16[4,2,81,128]{3,2,1,0:T(8,128)(2,1)S(1)} %pad_maximum_fusion.mine), channel_id=1, source_target_pairs={{0,1},{1,0},{2,3},{3,2},{4,5},{5,4},{6,7},{7,6},{8,9},{9,8},{10,11... | collective-permute-start | bytes 497672 | tf_op jit(solution)/shard_map/ppermute | solution.py:291

commit v7 on v6

--- a/solution.py
+++ b/solution.py
@@ -45,7 +45,6 @@
 
 
 VMEM_SPEC = pl.BlockSpec(memory_space=pltpu.VMEM)
-HBM_SPEC = pl.BlockSpec(memory_space=pltpu.HBM)
 SMEM_SPEC = pl.BlockSpec(memory_space=pltpu.SMEM)
 
 
@@ -77,17 +76,6 @@
 def pack_feats_kernel(both, across, packed):
     packed[0] = both[0]
     packed[1] = across[1]
-
-
-def load_kernel(image_head_hbm, text_head_hbm, image_head, text_head, sems):
-    copies = [
-        pltpu.make_async_copy(image_head_hbm, image_head, sems.at[0]),
-        pltpu.make_async_copy(text_head_hbm, text_head, sems.at[1]),
-    ]
-    for copy in copies:
-        copy.start()
-    for copy in copies:
-        copy.wait()
 
 
 def project_kernel(
@@ -319,10 +307,6 @@
     raw_v0 = y_swap(raw_u)
     packed = call(pack_feats_kernel, "pack_feats", shape((2, ROWS, D)), (both, core_swap(both)))
     feats_1, feats_3 = x_turn(packed, 1), x_turn(packed, 3)
-    image_head, text_head = call(
-        load_kernel, "load", [shape((D, D)), shape((D, D))], (image_head, text_head),
-        in_specs=[HBM_SPEC] * 2, scratch=[pltpu.SemaphoreType.DMA((2,))], mib=46,
-    )
     image_1, text_1, packed = lax.optimization_barrier((image_1, text_1, packed))
     came = (image_1, text_1, image_head, text_head)
     v1 = call(functools.partial(project_came_kernel, 0), "project_v", block, came)

time: 95.5 us -> 101 us (1.058)
  waiting for transfers between devices: 26.1 us -> 31.9 us
  local copies, waits for them, and re-layouts: 1.8 us -> 5.52 us
  Pallas kernels: 17 us -> 14.9 us
  starting transfers between devices: 37.2 us -> 35.3 us
    ppermute x2, waiting for transfers between devices: 1.81 us -> 5.55 us  [z_shift(): return lax.ppermute(array, 'z', [(z, (z + by) % NZ) for z in range(NZ)])]
    unnamed x2 -> x10, local copies, waits for them, and re-layouts: 1.75 us -> 5.47 us
    ppermute x1, waiting for transfers between devices: 1.21 us -> 4 us  [u_shift(): return lax.ppermute(array, BLK, pairs)]
    ppermute x3, starting transfers between devices: 5.75 us -> 3.31 us  [y_swap(): return lax.ppermute(array, 'ylo', [(0, 1), (1, 0)])]
    pallas_call x17 -> x16, Pallas kernels: 17 us -> 14.9 us  [call(): pl.pallas_call(kernel, out_shape=out_shape, in_specs=in_specs or [pl.Bloc...]
  transfers between devices with their start and end apart: 23 -> 23, of which waited for: 13 -> 13; matrix products, arithmetic and copies ran while one was open for 0% -> 0% of each run, Pallas kernels for 14% -> 11%
where the time goes in v7:
time: 101 us
  starting transfers between devices  35.3 us (35%)
  waiting for transfers between devices  31.9 us (32%)
  Pallas kernels  14.9 us (15%)
  blocking collectives  11.3 us (11%)
  local copies, waits for them, and re-layouts  5.52 us (5%)
  between operations  2.08 us (2%)
    pallas_call x16, Pallas kernels, call(): pl.pallas_call(kernel, out_shape=out_shape, in_specs=in_specs or [pl.Bloc...  14.9 us
    ppermute x10, starting transfers between devices, x_turn(): return lax.ppermute(array, 'x', [(i, (i + by) % NX) for i in range(NX)])  11.5 us
    all_to_all x1, blocking collectives, body(): pieces = lax.all_to_all(pieces, 'z', 0, 0, tiled=True)  11.3 us
    ppermute x3, starting transfers between devices, core_swap(): return lax.ppermute(array, 'core', [(0, 1), (1, 0)])  10.6 us
    ppermute x10, waiting for transfers between devices, x_turn(): return lax.ppermute(array, 'x', [(i, (i + by) % NX) for i in range(NX)])  10.6 us
    ppermute x3, waiting for transfers between devices, y_turn(): return lax.ppermute(array, ('ylo', 'yhi'), pairs)  6.5 us
    ppermute x2, waiting for transfers between devices, z_shift(): return lax.ppermute(array, 'z', [(z, (z + by) % NZ) for z in range(NZ)])  5.55 us
    unnamed x10, local copies, waits for them, and re-layouts  5.47 us
  transfers between devices with their start and end apart: 23, of which 13 were waited for; matrix products, arithmetic and copies ran while one was open for 0% of the time, Pallas kernels for 11%

profile of v7, /device:TPU:1, one launch (start us, length us, event | category | flops | bytes accessed | tf_op | source)
XLA Modules:
  0.0 101.1 jit_solution(10624034398086465644)
XLA Ops:
  1.6 1.0 %choose.1 = (bf16[2,128,1152]{2,1,0:T(8,128)(2,1)S(1)}, bf16[128,1152]{1,0:T(8,128)(2,1)S(1)}) custom-call(bf16[128,1152]{1,0:T(8,128)(2,1)S(1)} %bitcast.16, bf16[128,1152]{1,0:T(8,128)(2,1)} %bitcast.1.text), custom_call_target="tpu_custom_call" | custom-call | flops 1 | bytes 1 | tf_op jit(solution)/shard_map/choose/pallas_call | solution.py:32
  2.6 3.3 %collective-permute-start.3 = (bf16[2,128,1152]{2,1,0:T(8,128)(2,1)S(1)}, bf16[2,128,1152]{2,1,0:T(8,128)(2,1)S(1)}, u32[]{:S(2)}, u32[]{:S(2)}) collective-permute-start(bf16[2,128,1152]{2,1,0:T(8,128)(2,1)S(1)} %get-tuple-element.57.both), channel_id=1, source_target_pairs={{0,1},{1,0},{2,3},{3,2},{4,5},{5,4},{6,7},{7,6},{8,9},{9,8},{10,11... | collective-permute-start | bytes 1769480 | tf_op jit(solution)/shard_map/ppermute | solution.py:279
  6.0 3.9 %collective-permute-start.1 = (bf16[128,1152]{1,0:T(8,128)(2,1)}, bf16[128,1152]{1,0:T(8,128)(2,1)S(1)}, u32[]{:S(2)}, u32[]{:S(2)}) collective-permute-start(bf16[128,1152]{1,0:T(8,128)(2,1)} %bitcast.15), channel_id=1, source_target_pairs={{0,224},{32,0},{64,32},{96,64},{128,96},{160,128},{192,160},{224,1... | collective-permute-start | bytes 884744 | tf_op jit(solution)/shard_map/ppermute | solution.py:263
  9.9 1.3 %collective-permute-start.5 = (bf16[2,128,1152]{2,1,0:T(8,128)(2,1)S(1)}, bf16[2,128,1152]{2,1,0:T(8,128)(2,1)S(1)}, u32[]{:S(2)}, u32[]{:S(2)}) collective-permute-start(bf16[2,128,1152]{2,1,0:T(8,128)(2,1)S(1)} %pack_feats.1.refs_0_), channel_id=1, source_target_pairs={{0,2},{2,4},{4,6},{6,0},{1,3},{3,5},{5,7},{7,1},{8,10},{10,12},{12... | collective-permute-start | bytes 1769480 | tf_op jit(solution)/shard_map/ppermute | solution.py:283
  11.2 1.5 %collective-permute-start.6 = (bf16[2,128,1152]{2,1,0:T(8,128)(2,1)S(1)}, bf16[2,128,1152]{2,1,0:T(8,128)(2,1)S(1)}, u32[]{:S(2)}, u32[]{:S(2)}) collective-permute-start(bf16[2,128,1152]{2,1,0:T(8,128)(2,1)S(1)} %pack_feats.1.refs_0_), channel_id=1, source_target_pairs={{0,6},{2,0},{4,2},{6,4},{1,7},{3,1},{5,3},{7,5},{8,14},{10,8},{12,... | collective-permute-start | bytes 1769480 | tf_op jit(solution)/shard_map/ppermute | solution.py:283
  12.6 1.3 %collective-permute-start = (bf16[128,1152]{1,0:T(8,128)(2,1)S(1)}, bf16[128,1152]{1,0:T(8,128)(2,1)S(1)}, u32[]{:S(2)}, u32[]{:S(2)}) collective-permute-start(bf16[128,1152]{1,0:T(8,128)(2,1)S(1)} %get-tuple-element.53), channel_id=1, source_target_pairs={{0,16},{16,0},{1,17},{17,1},{2,18},{18,2},{3,19},{19,3},{4,20},{20... | collective-permute-start | bytes 884744 | tf_op jit(solution)/shard_map/ppermute | solution.py:275
  13.9 2.6 %collective-permute-done.1.image = bf16[128,1152]{1,0:T(8,128)(2,1)S(1)} collective-permute-done((bf16[128,1152]{1,0:T(8,128)(2,1)}, bf16[128,1152]{1,0:T(8,128)(2,1)S(1)}, u32[]{:S(2)}, u32[]{:S(2)}) %collective-permute-start.1) | collective-permute-done | bytes 294944 | tf_op jit(solution)/shard_map/ppermute | solution.py:263
  16.5 3.0 %collective-permute-done.2.text = bf16[128,1152]{1,0:T(8,128)(2,1)S(1)} collective-permute-done((bf16[128,1152]{1,0:T(8,128)(2,1)}, bf16[128,1152]{1,0:T(8,128)(2,1)S(1)}, u32[]{:S(2)}, u32[]{:S(2)}) %collective-permute-start.2) | collective-permute-done | bytes 294944 | tf_op jit(solution)/shard_map/ppermute | solution.py:263
  19.5 1.7 %copy-done = bf16[1152,1152]{1,0:T(8,128)(2,1)S(1)} copy-done((bf16[1152,1152]{1,0:T(8,128)(2,1)S(1)}, bf16[1152,1152]{1,0:T(8,128)(2,1)}, u32[]{:S(2)}) %copy-start) | copy-done | bytes 2654232
  21.2 1.7 %copy-done.2 = bf16[1152,1152]{1,0:T(8,128)(2,1)S(1)} copy-done((bf16[1152,1152]{1,0:T(8,128)(2,1)S(1)}, bf16[1152,1152]{1,0:T(8,128)(2,1)}, u32[]{:S(2)}) %copy-start.2) | copy-done | bytes 2654232
  23.7 1.4 %collective-permute-start.4 = (bf16[128,1152]{1,0:T(8,128)(2,1)S(1)}, bf16[128,1152]{1,0:T(8,128)(2,1)S(1)}, u32[]{:S(2)}, u32[]{:S(2)}) collective-permute-start(bf16[128,1152]{1,0:T(8,128)(2,1)S(1)} %project_v.1.v1), channel_id=1, source_target_pairs={{0,16},{16,0},{1,17},{17,1},{2,18},{18,2},{3,19},{19,3},{4,20},{20... | collective-permute-start | bytes 884744 | tf_op jit(solution)/shard_map/ppermute | solution.py:275
  28.2 1.8 %project.1 = (bf16[128,1152]{1,0:T(8,128)(2,1)S(1)}, bf16[128,1152]{1,0:T(8,128)(2,1)S(1)}, f32[128,1152]{1,0:T(8,128)S(1)}, f32[128,1152]{1,0:T(8,128)S(1)}, f3...) custom-call(f32[2]{0:T(128)S(1)} %pad_maximum_fusion.2.scalars, ...), custom_call_target="tpu_custom_call" | custom-call | flops 1 | bytes 1 | tf_op jit(solution)/shard_map/project/pallas_call | solution.py:32
  30.0 2.3 %early.1 = (f32[128,1152]{1,0:T(8,128)S(1)}, f32[128,1152]{1,0:T(8,128)S(1)}) custom-call(f32[8,128]{1,0:T(8,128)S(1)} %get-tuple-element.58.scalars, bf16[128,1152]{1,0:T(8,128)(2,1)S(1)} %get-tuple-element.59.u, bf16[128,1152]{1,0:T(8,128)(2,1)S(1)} %get-tuple-element.60.v, bf16[128,1152]{1,0:T(8,128)(2,1)S(1)} %project_u.1.u1, ...), custom_call_target="tpu_custom_call" | custom-call | flops 1 | bytes 1 | tf_op jit(solution)/shard_map/early/pallas_call | solution.py:32
  33.1 1.5 %collective-permute-start.12 = (bf16[128,1152]{1,0:T(8,128)(2,1)S(1)}, bf16[128,1152]{1,0:T(8,128)(2,1)S(1)}, u32[]{:S(2)}, u32[]{:S(2)}) collective-permute-start(bf16[128,1152]{1,0:T(8,128)(2,1)S(1)} %slice_bitcast_fusion.1), channel_id=1, source_target_pairs={{0,2},{2,4},{4,6},{6,0},{1,3},{3,5},{5,7},{7,1},{8,10},{10,12},{12... | collective-permute-start | bytes 884744 | tf_op jit(solution)/shard_map/ppermute | solution.py:283
  34.6 1.5 %collective-permute-start.13 = (bf16[128,1152]{1,0:T(8,128)(2,1)S(1)}, bf16[128,1152]{1,0:T(8,128)(2,1)S(1)}, u32[]{:S(2)}, u32[]{:S(2)}) collective-permute-start(bf16[128,1152]{1,0:T(8,128)(2,1)S(1)} %slice_bitcast_fusion), channel_id=1, source_target_pairs={{0,6},{2,0},{4,2},{6,4},{1,7},{3,1},{5,3},{7,5},{8,14},{10,8},{12,... | collective-permute-start | bytes 884744 | tf_op jit(solution)/shard_map/ppermute | solution.py:283
  36.7 4.0 %collective-permute-done.7.u3 = bf16[128,1152]{1,0:T(8,128)(2,1)S(1)} collective-permute-done((bf16[128,1152]{1,0:T(8,128)(2,1)S(1)}, bf16[128,1152]{1,0:T(8,128)(2,1)S(1)}, u32[]{:S(2)}, u32[]{:S(2)}) %collective-permute-start.7) | collective-permute-done | bytes 294944 | tf_op jit(solution)/shard_map/ppermute | solution.py:271
  40.7 1.4 %late.1 = (bf16[128,1152]{1,0:T(8,128)(2,1)S(1)}, bf16[128,1152]{1,0:T(8,128)(2,1)S(1)}, bf16[2,384,128]{2,1,0:T(8,128)(2,1)S(1)}, bf16[2,384,128]{2,1,0:T(8,128...) custom-call(f32[8,128]{1,0:T(8,128)S(1)} %get-tuple-element.58.scalars, ...), custom_call_target="tpu_custom_call" | custom-call | flops 1 | bytes 1 | tf_op jit(solution)/shard_map/late/pallas_call | solution.py:32
  42.1 2.6 %collective-permute-start.10 = (bf16[2,384,128]{2,1,0:T(8,128)(2,1)S(1)}, bf16[2,384,128]{2,1,0:T(8,128)(2,1)S(1)}, u32[]{:S(2)}, u32[]{:S(2)}) collective-permute-start(bf16[2,384,128]{2,1,0:T(8,128)(2,1)S(1)} %get-tuple-element.76), channel_id=1, source_target_pairs={{0,6},{2,0},{4,2},{6,4},{1,7},{3,1},{5,3},{7,5},{8,14},{10,8},{12,... | collective-permute-start | bytes 589832 | tf_op jit(solution)/shard_map/ppermute | solution.py:283
  45.8 2.4 %feats_grad.1 = (bf16[128,1152]{1,0:T(8,128)(2,1)}, bf16[128,1152]{1,0:T(8,128)(2,1)}) custom-call(bf16[128,1152]{1,0:T(8,128)(2,1)S(1)} %get-tuple-element.82.image_dpre, bf16[128,1152]{1,0:T(8,128)(2,1)S(1)} %get-tuple-element.83.text_dpre, bf16[1152,1152]{1,0:T(8,128)(2,1)S(1)} %copy-done.1, bf16[1152,1152]{1,0:T(8,128)(2,1)S(1)} %copy-done.3), custom_call_target="tpu_custom_call" | custom-call | flops 1 | bytes 1 | tf_op jit(solution)/shard_map/feats_grad/pallas_call | solution.py:32
  50.8 5.1 %collective-permute-done.9.refs_1_ = bf16[2,384,128]{2,1,0:T(8,128)(2,1)S(1)} collective-permute-done((bf16[2,384,128]{2,1,0:T(8,128)(2,1)S(1)}, bf16[2,384,128]{2,1,0:T(8,128)(2,1)S(1)}, u32[]{:S(2)}, u32[]{:S(2)}) %collective-permute-start.9) | collective-permute-done | bytes 196640 | tf_op jit(solution)/shard_map/ppermute | solution.py:283
  56.0 1.9 %collective-permute-start.14 = (bf16[4,384,128]{2,1,0:T(8,128)(2,1)S(1)}, bf16[4,384,128]{2,1,0:T(8,128)(2,1)S(1)}, u32[]{:S(2)}, u32[]{:S(2)}) collective-permute-start(bf16[4,384,128]{2,1,0:T(8,128)(2,1)S(1)} %others.1), channel_id=1, source_target_pairs={{0,1},{1,0},{2,3},{3,2},{4,5},{5,4},{6,7},{7,6},{8,9},{9,8},{10,11... | collective-permute-start | bytes 1179656 | tf_op jit(solution)/shard_map/ppermute | solution.py:279
  60.1 2.7 %collective-permute-start.15 = (bf16[8,81,128]{2,1,0:T(8,128)(2,1)S(1)}, bf16[8,81,128]{2,1,0:T(8,128)(2,1)S(1)}, u32[]{:S(2)}, u32[]{:S(2)}) collective-permute-start(bf16[8,81,128]{2,1,0:T(8,128)(2,1)S(1)} %get-tuple-element.100), channel_id=1, source_target_pairs={{0,8},{16,24},{8,0},{24,16},{1,9},{17,25},{9,1},{25,17},{2,10},{18... | collective-permute-start | bytes 497672 | tf_op jit(solution)/shard_map/ppermute | solution.py:289
  62.8 2.7 %collective-permute-start.17 = (bf16[8,81,128]{2,1,0:T(8,128)(2,1)S(1)}, bf16[8,81,128]{2,1,0:T(8,128)(2,1)S(1)}, u32[]{:S(2)}, u32[]{:S(2)}) collective-permute-start(bf16[8,81,128]{2,1,0:T(8,128)(2,1)S(1)} %get-tuple-element.102), channel_id=1, source_target_pairs={{0,24},{16,0},{8,16},{24,8},{1,25},{17,1},{9,17},{25,9},{2,26},{18... | collective-permute-start | bytes 497672 | tf_op jit(solution)/shard_map/ppermute | solution.py:289
  65.5 2.0 %collective-permute-done.15.refs_1_ = bf16[8,81,128]{2,1,0:T(8,128)(2,1)S(1)} collective-permute-done((bf16[8,81,128]{2,1,0:T(8,128)(2,1)S(1)}, bf16[8,81,128]{2,1,0:T(8,128)(2,1)S(1)}, u32[]{:S(2)}, u32[]{:S(2)}) %collective-permute-start.15) | collective-permute-done | bytes 165920 | tf_op jit(solution)/shard_map/ppermute | solution.py:289
  67.5 4.5 %collective-permute-done.16.refs_2_ = bf16[8,81,128]{2,1,0:T(8,128)(2,1)S(1)} collective-permute-done((bf16[8,81,128]{2,1,0:T(8,128)(2,1)S(1)}, bf16[8,81,128]{2,1,0:T(8,128)(2,1)S(1)}, u32[]{:S(2)}, u32[]{:S(2)}) %collective-permute-start.16) | collective-permute-done | bytes 165920 | tf_op jit(solution)/shard_map/ppermute | solution.py:289
  72.1 11.3 %all_to_all.5.pieces = bf16[8,81,128]{2,1,0:T(8,128)(2,1)S(1)} all-to-all(bf16[8,81,128]{2,1,0:T(8,128)(2,1)S(1)} %add_y.1), channel_id=1, replica_groups=mesh['z'=8,'ylo'=2,'yhi'=2,'x'=4,'core'=2] {'z'}, dimensions={0} | all-to-all | bytes 331776 | tf_op jit(solution)/shard_map/all_to_all | solution.py:374
  84.0 3.6 %collective-permute-done.18 = bf16[81,128]{1,0:T(8,128)(2,1)S(1)} collective-permute-done((bf16[81,128]{1,0:T(8,128)(2,1)S(1)}, bf16[81,128]{1,0:T(8,128)(2,1)S(1)}, u32[]{:S(2)}, u32[]{:S(2)}) %collective-permute-start.18) | collective-permute-done | bytes 20768 | tf_op jit(solution)/shard_map/ppermute | solution.py:293
  89.7 2.4 %collective-permute-done.20 = bf16[2,81,128]{2,1,0:T(8,128)(2,1)S(1)} collective-permute-done((bf16[2,81,128]{2,1,0:T(8,128)(2,1)S(1)}, bf16[2,81,128]{2,1,0:T(8,128)(2,1)S(1)}, u32[]{:S(2)}, u32[]{:S(2)}) %collective-permute-start.20) | collective-permute-done | bytes 41504 | tf_op jit(solution)/shard_map/ppermute | solution.py:283
  92.1 1.1 %collective-permute-done.19 = bf16[2,81,128]{2,1,0:T(8,128)(2,1)S(1)} collective-permute-done((bf16[2,81,128]{2,1,0:T(8,128)(2,1)S(1)}, bf16[2,81,128]{2,1,0:T(8,128)(2,1)S(1)}, u32[]{:S(2)}, u32[]{:S(2)}) %collective-permute-start.19) | collective-permute-done | bytes 41504 | tf_op jit(solution)/shard_map/ppermute | solution.py:283
  93.3 5.5 %collective-permute-start.22 = (bf16[4,2,81,128]{3,2,1,0:T(8,128)(2,1)S(1)}, bf16[4,2,81,128]{3,2,1,0:T(8,128)(2,1)S(1)}, u32[]{:S(2)}, u32[]{:S(2)}) collective-permute-start(bf16[4,2,81,128]{3,2,1,0:T(8,128)(2,1)S(1)} %pad_maximum_fusion.mine), channel_id=1, source_target_pairs={{0,1},{1,0},{2,3},{3,2},{4,5},{5,4},{6,7},{7,6},{8,9},{9,8},{10,11... | collective-permute-start | bytes 497672 | tf_op jit(solution)/shard_map/ppermute | solution.py:279
  98.8 1.0 %collective-permute-done.22.other = bf16[4,2,81,128]{3,2,1,0:T(8,128)(2,1)S(1)} collective-permute-done((bf16[4,2,81,128]{3,2,1,0:T(8,128)(2,1)S(1)}, bf16[4,2,81,128]{3,2,1,0:T(8,128)(2,1)S(1)}, u32[]{:S(2)}, u32[]{:S(2)}) %collective-permute-start.22) | collective-permute-done | bytes 165920 | tf_op jit(solution)/shard_map/ppermute | solution.py:279
  99.8 1.3 %place.1 = f32[72,2,1152]{2,1,0:T(2,128)} custom-call(bf16[4,2,81,128]{3,2,1,0:T(8,128)(2,1)S(1)} %pad_maximum_fusion.mine, bf16[4,2,81,128]{3,2,1,0:T(8,128)(2,1)S(1)} %collective-permute-done.22.other), custom_call_target="tpu_custom_call" | custom-call | flops 1 | bytes 1 | tf_op jit(solution)/shard_map/place/pallas_call | solution.py:32
  (46 shorter events, 13.7 us)
Async XLA Ops:
  0.6 1.0 copy-start.4
  2.6 7.2 %collective-permute-start.3 = (bf16[2,128,1152]{2,1,0:T(8,128)(2,1)S(1)}, bf16[2,128,1152]{2,1,0:T(8,128)(2,1)S(1)}, u32[]{:S(2)}, u32[]{:S(2)}) collective-permute-start(bf16[2,128,1152]{2,1,0:T(8,128)(2,1)S(1)} %get-tuple-element.57.both), channel_id=1, source_target_pairs={{0,1},{1,0},{2,3},{3,2},{4,5},{5,4},{6,7},{7,6},{8,9},{9,8},{10,11... | collective-permute-start | bytes 1769480 | tf_op jit(solution)/shard_map/ppermute | solution.py:279
  6.0 10.5 %collective-permute-start.1 = (bf16[128,1152]{1,0:T(8,128)(2,1)}, bf16[128,1152]{1,0:T(8,128)(2,1)S(1)}, u32[]{:S(2)}, u32[]{:S(2)}) collective-permute-start(bf16[128,1152]{1,0:T(8,128)(2,1)} %bitcast.15), channel_id=1, source_target_pairs={{0,224},{32,0},{64,32},{96,64},{128,96},{160,128},{192,160},{224,1... | collective-permute-start | bytes 884744 | tf_op jit(solution)/shard_map/ppermute | solution.py:263
  9.8 9.7 %collective-permute-start.2 = (bf16[128,1152]{1,0:T(8,128)(2,1)}, bf16[128,1152]{1,0:T(8,128)(2,1)S(1)}, u32[]{:S(2)}, u32[]{:S(2)}) collective-permute-start(bf16[128,1152]{1,0:T(8,128)(2,1)} %bitcast.1.text), channel_id=1, source_target_pairs={{0,32},{32,64},{64,96},{96,128},{128,160},{160,192},{192,224},{224... | collective-permute-start | bytes 884744 | tf_op jit(solution)/shard_map/ppermute | solution.py:263
  9.9 22.5 %collective-permute-start.5 = (bf16[2,128,1152]{2,1,0:T(8,128)(2,1)S(1)}, bf16[2,128,1152]{2,1,0:T(8,128)(2,1)S(1)}, u32[]{:S(2)}, u32[]{:S(2)}) collective-permute-start(bf16[2,128,1152]{2,1,0:T(8,128)(2,1)S(1)} %pack_feats.1.refs_0_), channel_id=1, source_target_pairs={{0,2},{2,4},{4,6},{6,0},{1,3},{3,5},{5,7},{7,1},{8,10},{10,12},{12... | collective-permute-start | bytes 1769480 | tf_op jit(solution)/shard_map/ppermute | solution.py:283
  11.2 21.2 %collective-permute-start.6 = (bf16[2,128,1152]{2,1,0:T(8,128)(2,1)S(1)}, bf16[2,128,1152]{2,1,0:T(8,128)(2,1)S(1)}, u32[]{:S(2)}, u32[]{:S(2)}) collective-permute-start(bf16[2,128,1152]{2,1,0:T(8,128)(2,1)S(1)} %pack_feats.1.refs_0_), channel_id=1, source_target_pairs={{0,6},{2,0},{4,2},{6,4},{1,7},{3,1},{5,3},{7,5},{8,14},{10,8},{12,... | collective-permute-start | bytes 1769480 | tf_op jit(solution)/shard_map/ppermute | solution.py:283
  12.6 13.8 %collective-permute-start = (bf16[128,1152]{1,0:T(8,128)(2,1)S(1)}, bf16[128,1152]{1,0:T(8,128)(2,1)S(1)}, u32[]{:S(2)}, u32[]{:S(2)}) collective-permute-start(bf16[128,1152]{1,0:T(8,128)(2,1)S(1)} %get-tuple-element.53), channel_id=1, source_target_pairs={{0,16},{16,0},{1,17},{17,1},{2,18},{18,2},{3,19},{19,3},{4,20},{20... | collective-permute-start | bytes 884744 | tf_op jit(solution)/shard_map/ppermute | solution.py:275
  19.5 1.8 %copy-start = (bf16[1152,1152]{1,0:T(8,128)(2,1)S(1)}, bf16[1152,1152]{1,0:T(8,128)(2,1)}, u32[]{:S(2)}) copy-start(bf16[1152,1152]{1,0:T(8,128)(2,1)} %image_head.9) | copy-start | bytes 7962628
  21.2 1.7 %copy-start.2 = (bf16[1152,1152]{1,0:T(8,128)(2,1)S(1)}, bf16[1152,1152]{1,0:T(8,128)(2,1)}, u32[]{:S(2)}) copy-start(bf16[1152,1152]{1,0:T(8,128)(2,1)} %text_head.9) | copy-start | bytes 7962628
  23.7 8.6 %collective-permute-start.4 = (bf16[128,1152]{1,0:T(8,128)(2,1)S(1)}, bf16[128,1152]{1,0:T(8,128)(2,1)S(1)}, u32[]{:S(2)}, u32[]{:S(2)}) collective-permute-start(bf16[128,1152]{1,0:T(8,128)(2,1)S(1)} %project_v.1.v1), channel_id=1, source_target_pairs={{0,16},{16,0},{1,17},{17,1},{2,18},{18,2},{3,19},{19,3},{4,20},{20... | collective-permute-start | bytes 884744 | tf_op jit(solution)/shard_map/ppermute | solution.py:275
  26.5 1.8 %copy-start.1 = (bf16[1152,1152]{1,0:T(8,128)(2,1)S(1)}, bf16[1152,1152]{1,0:T(8,128)(2,1)}, u32[]{:S(2)}) copy-start(bf16[1152,1152]{1,0:T(8,128)(2,1)} %image_head.9) | copy-start | bytes 7962628
  32.4 8.3 %collective-permute-start.7 = (bf16[128,1152]{1,0:T(8,128)(2,1)S(1)}, bf16[128,1152]{1,0:T(8,128)(2,1)S(1)}, u32[]{:S(2)}, u32[]{:S(2)}) collective-permute-start(bf16[128,1152]{1,0:T(8,128)(2,1)S(1)} %collective-permute-done.4.u2), channel_id=1, source_target_pairs={{0,32},{16,240},{32,64},{48,16},{64,96},{80,48},{96,128},{112,80},... | collective-permute-start | bytes 884744 | tf_op jit(solution)/shard_map/ppermute | solution.py:271
  32.5 8.2 %collective-permute-start.8 = (bf16[128,1152]{1,0:T(8,128)(2,1)S(1)}, bf16[128,1152]{1,0:T(8,128)(2,1)S(1)}, u32[]{:S(2)}, u32[]{:S(2)}) collective-permute-start(bf16[128,1152]{1,0:T(8,128)(2,1)S(1)} %project_u.1.u1), channel_id=1, source_target_pairs={{0,16},{16,0},{1,17},{17,1},{2,18},{18,2},{3,19},{19,3},{4,20},{20... | collective-permute-start | bytes 884744 | tf_op jit(solution)/shard_map/ppermute | solution.py:275
  33.1 12.7 %collective-permute-start.12 = (bf16[128,1152]{1,0:T(8,128)(2,1)S(1)}, bf16[128,1152]{1,0:T(8,128)(2,1)S(1)}, u32[]{:S(2)}, u32[]{:S(2)}) collective-permute-start(bf16[128,1152]{1,0:T(8,128)(2,1)S(1)} %slice_bitcast_fusion.1), channel_id=1, source_target_pairs={{0,2},{2,4},{4,6},{6,0},{1,3},{3,5},{5,7},{7,1},{8,10},{10,12},{12... | collective-permute-start | bytes 884744 | tf_op jit(solution)/shard_map/ppermute | solution.py:283
  34.6 11.2 %collective-permute-start.13 = (bf16[128,1152]{1,0:T(8,128)(2,1)S(1)}, bf16[128,1152]{1,0:T(8,128)(2,1)S(1)}, u32[]{:S(2)}, u32[]{:S(2)}) collective-permute-start(bf16[128,1152]{1,0:T(8,128)(2,1)S(1)} %slice_bitcast_fusion), channel_id=1, source_target_pairs={{0,6},{2,0},{4,2},{6,4},{1,7},{3,1},{5,3},{7,5},{8,14},{10,8},{12,... | collective-permute-start | bytes 884744 | tf_op jit(solution)/shard_map/ppermute | solution.py:283
  40.7 5.1 %copy-start.3 = (bf16[1152,1152]{1,0:T(8,128)(2,1)S(1)}, bf16[1152,1152]{1,0:T(8,128)(2,1)}, u32[]{:S(2)}) copy-start(bf16[1152,1152]{1,0:T(8,128)(2,1)} %text_head.9) | copy-start | bytes 7962628
  42.1 7.7 %collective-permute-start.10 = (bf16[2,384,128]{2,1,0:T(8,128)(2,1)S(1)}, bf16[2,384,128]{2,1,0:T(8,128)(2,1)S(1)}, u32[]{:S(2)}, u32[]{:S(2)}) collective-permute-start(bf16[2,384,128]{2,1,0:T(8,128)(2,1)S(1)} %get-tuple-element.76), channel_id=1, source_target_pairs={{0,6},{2,0},{4,2},{6,4},{1,7},{3,1},{5,3},{7,5},{8,14},{10,8},{12,... | collective-permute-start | bytes 589832 | tf_op jit(solution)/shard_map/ppermute | solution.py:283
  44.7 6.1 %collective-permute-start.11 = (bf16[2,384,128]{2,1,0:T(8,128)(2,1)S(1)}, bf16[2,384,128]{2,1,0:T(8,128)(2,1)S(1)}, u32[]{:S(2)}, u32[]{:S(2)}) collective-permute-start(bf16[2,384,128]{2,1,0:T(8,128)(2,1)S(1)} %get-tuple-element.77), channel_id=1, source_target_pairs={{0,4},{2,6},{4,0},{6,2},{1,5},{3,7},{5,1},{7,3},{8,12},{10,14},{12... | collective-permute-start | bytes 589832 | tf_op jit(solution)/shard_map/ppermute | solution.py:283
  45.2 10.8 %collective-permute-start.9 = (bf16[2,384,128]{2,1,0:T(8,128)(2,1)S(1)}, bf16[2,384,128]{2,1,0:T(8,128)(2,1)S(1)}, u32[]{:S(2)}, u32[]{:S(2)}) collective-permute-start(bf16[2,384,128]{2,1,0:T(8,128)(2,1)S(1)} %get-tuple-element.75), channel_id=1, source_target_pairs={{0,2},{2,4},{4,6},{6,0},{1,3},{3,5},{5,7},{7,1},{8,10},{10,12},{12... | collective-permute-start | bytes 589832 | tf_op jit(solution)/shard_map/ppermute | solution.py:283
  56.0 3.2 %collective-permute-start.14 = (bf16[4,384,128]{2,1,0:T(8,128)(2,1)S(1)}, bf16[4,384,128]{2,1,0:T(8,128)(2,1)S(1)}, u32[]{:S(2)}, u32[]{:S(2)}) collective-permute-start(bf16[4,384,128]{2,1,0:T(8,128)(2,1)S(1)} %others.1), channel_id=1, source_target_pairs={{0,1},{1,0},{2,3},{3,2},{4,5},{5,4},{6,7},{7,6},{8,9},{9,8},{10,11... | collective-permute-start | bytes 1179656 | tf_op jit(solution)/shard_map/ppermute | solution.py:279
  60.1 7.3 %collective-permute-start.15 = (bf16[8,81,128]{2,1,0:T(8,128)(2,1)S(1)}, bf16[8,81,128]{2,1,0:T(8,128)(2,1)S(1)}, u32[]{:S(2)}, u32[]{:S(2)}) collective-permute-start(bf16[8,81,128]{2,1,0:T(8,128)(2,1)S(1)} %get-tuple-element.100), channel_id=1, source_target_pairs={{0,8},{16,24},{8,0},{24,16},{1,9},{17,25},{9,1},{25,17},{2,10},{18... | collective-permute-start | bytes 497672 | tf_op jit(solution)/shard_map/ppermute | solution.py:289
  62.8 9.2 %collective-permute-start.16 = (bf16[8,81,128]{2,1,0:T(8,128)(2,1)S(1)}, bf16[8,81,128]{2,1,0:T(8,128)(2,1)S(1)}, u32[]{:S(2)}, u32[]{:S(2)}) collective-permute-start(bf16[8,81,128]{2,1,0:T(8,128)(2,1)S(1)} %get-tuple-element.101), channel_id=1, source_target_pairs={{0,16},{16,8},{8,24},{24,0},{1,17},{17,9},{9,25},{25,1},{2,18},{18... | collective-permute-start | bytes 497672 | tf_op jit(solution)/shard_map/ppermute | solution.py:289
  62.8 9.2 %collective-permute-start.17 = (bf16[8,81,128]{2,1,0:T(8,128)(2,1)S(1)}, bf16[8,81,128]{2,1,0:T(8,128)(2,1)S(1)}, u32[]{:S(2)}, u32[]{:S(2)}) collective-permute-start(bf16[8,81,128]{2,1,0:T(8,128)(2,1)S(1)} %get-tuple-element.102), channel_id=1, source_target_pairs={{0,24},{16,0},{8,16},{24,8},{1,25},{17,1},{9,17},{25,9},{2,26},{18... | collective-permute-start | bytes 497672 | tf_op jit(solution)/shard_map/ppermute | solution.py:289
  83.4 4.2 %collective-permute-start.18 = (bf16[81,128]{1,0:T(8,128)(2,1)S(1)}, bf16[81,128]{1,0:T(8,128)(2,1)S(1)}, u32[]{:S(2)}, u32[]{:S(2)}) collective-permute-start(bf16[81,128]{1,0:T(8,128)(2,1)S(1)} %add_z.1), channel_id=1, source_target_pairs={{0,8},{8,0},{1,9},{9,1},{2,10},{10,2},{3,11},{11,3},{4,12},{12,4},... | collective-permute-start | bytes 62216 | tf_op jit(solution)/shard_map/ppermute | solution.py:293
  87.7 4.5 %collective-permute-start.20 = (bf16[2,81,128]{2,1,0:T(8,128)(2,1)S(1)}, bf16[2,81,128]{2,1,0:T(8,128)(2,1)S(1)}, u32[]{:S(2)}, u32[]{:S(2)}) collective-permute-start(bf16[2,81,128]{2,1,0:T(8,128)(2,1)S(1)} %get-tuple-element.104), channel_id=1, source_target_pairs={{0,4},{2,6},{4,0},{6,2},{1,5},{3,7},{5,1},{7,3},{8,12},{10,14},{12... | collective-permute-start | bytes 124424 | tf_op jit(solution)/shard_map/ppermute | solution.py:283
  88.3 3.9 %collective-permute-start.21 = (bf16[2,81,128]{2,1,0:T(8,128)(2,1)S(1)}, bf16[2,81,128]{2,1,0:T(8,128)(2,1)S(1)}, u32[]{:S(2)}, u32[]{:S(2)}) collective-permute-start(bf16[2,81,128]{2,1,0:T(8,128)(2,1)S(1)} %get-tuple-element.104), channel_id=1, source_target_pairs={{0,6},{2,0},{4,2},{6,4},{1,7},{3,1},{5,3},{7,5},{8,14},{10,8},{12,... | collective-permute-start | bytes 124424 | tf_op jit(solution)/shard_map/ppermute | solution.py:283
  89.2 4.1 %collective-permute-start.19 = (bf16[2,81,128]{2,1,0:T(8,128)(2,1)S(1)}, bf16[2,81,128]{2,1,0:T(8,128)(2,1)S(1)}, u32[]{:S(2)}, u32[]{:S(2)}) collective-permute-start(bf16[2,81,128]{2,1,0:T(8,128)(2,1)S(1)} %get-tuple-element.104), channel_id=1, source_target_pairs={{0,2},{2,4},{4,6},{6,0},{1,3},{3,5},{5,7},{7,1},{8,10},{10,12},{12... | collective-permute-start | bytes 124424 | tf_op jit(solution)/shard_map/ppermute | solution.py:283
  93.3 6.5 %collective-permute-start.22 = (bf16[4,2,81,128]{3,2,1,0:T(8,128)(2,1)S(1)}, bf16[4,2,81,128]{3,2,1,0:T(8,128)(2,1)S(1)}, u32[]{:S(2)}, u32[]{:S(2)}) collective-permute-start(bf16[4,2,81,128]{3,2,1,0:T(8,128)(2,1)S(1)} %pad_maximum_fusion.mine), channel_id=1, source_target_pairs={{0,1},{1,0},{2,3},{3,2},{4,5},{5,4},{6,7},{7,6},{8,9},{9,8},{10,11... | collective-permute-start | bytes 497672 | tf_op jit(solution)/shard_map/ppermute | solution.py:279
